TPU v7x, 32 devices: a whole 2x2x4 slice. The times are simulated.
32 devices in a mesh: groups: 2 (over y), box: 8 (over z, x), trial: 2 (over core).
Axes of the slice: x: 2, y: 2, z: 4, core: 2. Of those that a mesh axis runs over, the one named last changes fastest.
Arguments:
- medium: float32 [4, 3, 8, 128, 128], P('trial', None, None, 'box'), may hold values from 0.5 to 2, as said below
- store: float32 [32, 3, 256], P(('groups', 'box', 'trial')), parts along dimension 0, may hold values from -6 to 6
- surf_off: int32 [256], replicated, may hold values from 0 to 16383, as said below
- owners: int32 [6], replicated, may hold values from 0 to 15, as said below
- brick_map: int32 [8], replicated, may hold values from 0 to 7, each once
Outputs:
- velocity: float32 [8, 3, 8, 128, 128], P(('groups', 'trial'), None, 'box'), parts along dimension 0
- stress: float32 [8, 6, 8, 128, 128], P(('groups', 'trial'), None, 'box'), parts along dimension 0
There are 2 independent parts, one for each index of `groups`. A program takes and returns all parts, laid end to end along the dimension named above; an argument that names none is the same for every part. Nothing has to cross between parts.
Inputs may be any that keep to these rules, and one draw needn't show every extreme that they name: `surf_off`: entries k * 32 to (k+1) * 32 - 1 name distinct cells y * 128 + z of x-plane k. `owners`: distinct slots. `brick_map`: a permutation. `medium`: lam within 1 to 2, mu and buoyancy within 0.5 to 1.
All inputs are finite; a program needn't handle non-finite values.
Results may differ from a plain program's by a relative error of at most 0.00002.
Values sent between devices are 32-bit elements; how exact they have to be, the bound alone decides.
No kernel may reach another device: no remote copies, remote signals or barrier semaphores. Data moves between devices by JAX's collectives and lax.ppermute only.
A program may use at most 64 MiB of HBM per device.

v0:
```python
import functools

import jax
import jax.numpy as jnp
from jax import lax
from jax.experimental import pallas as pl
from jax.experimental.pallas import tpu as pltpu
from jax.sharding import PartitionSpec as P

STEPS = 6
TIME_STEP = 0.25
VX, VY, VZ, XX, YY, ZZ, XY, XZ, YZ = range(9)
ROWS = 8
LINES = 24


def ring_place(box, count):
    return jnp.where(box % 2 == 0, box // 2, count - 1 - box // 2)


def ring_box(place, count):
    return jnp.where(place < count // 2, 2 * place, 2 * (count - 1 - place) + 1)


def ring_offsets(count):
    steps = [0]
    for distance in range(1, count // 2):
        steps += [-distance, distance]
    return steps + [count // 2]


def split_values(value, per):
    group = lax.broadcasted_iota(jnp.int32, value.shape, 1) // per
    high = value.astype(jnp.bfloat16).astype(jnp.float32)
    rest = value - high
    middle = rest.astype(jnp.bfloat16).astype(jnp.float32)
    low = rest - middle
    return jnp.where(
        group == 0, high, jnp.where(group == 1, middle, jnp.where(group == 2, low, 0.0))
    )


class Plane:
    def __init__(self, fields, cells_y, cells_z):
        self.fields, self.chunks = fields, cells_y // ROWS
        row = lax.broadcasted_iota(jnp.int32, (ROWS, cells_z), 0)
        lane = lax.broadcasted_iota(jnp.int32, (ROWS, cells_z), 1)
        self.first_row, self.last_row = row == 0, row == ROWS - 1
        self.first_lane, self.last_lane = lane == 0, lane == cells_z - 1
        self.cells_z = cells_z
        self.loaded, self.rolled = {}, {}

    def at(self, field, plane, chunk, key):
        if (field, key, chunk) not in self.loaded:
            self.loaded[field, key, chunk] = self.fields[
                field, plane, chunk * ROWS : chunk * ROWS + ROWS, :
            ]
        return self.loaded[field, key, chunk]

    def roll_rows(self, field, plane, chunk, by):
        if not 0 <= chunk < self.chunks:
            return 0.0
        if (field, chunk) not in self.rolled:
            self.rolled[field, chunk] = pltpu.roll(self.at(field, plane, chunk, 0), by, 0)
        return self.rolled[field, chunk]

    def back_y(self, field, plane, chunk):
        here = self.roll_rows(field, plane, chunk, 1)
        before = self.roll_rows(field, plane, chunk - 1, 1)
        return self.at(field, plane, chunk, 0) - jnp.where(self.first_row, before, here)

    def fore_y(self, field, plane, chunk):
        here = self.roll_rows(field, plane, chunk, ROWS - 1)
        after = self.roll_rows(field, plane, chunk + 1, ROWS - 1)
        return jnp.where(self.last_row, after, here) - self.at(field, plane, chunk, 0)

    def back_z(self, value):
        return value - jnp.where(self.first_lane, 0.0, pltpu.roll(value, 1, 1))

    def fore_z(self, value):
        return jnp.where(self.last_lane, 0.0, pltpu.roll(value, self.cells_z - 1, 1)) - value


def propagate(plan, *refs):
    trial, count, planes, cells_y, cells_z, per, first = plan
    refs = list(refs)
    place_ref, map_ref, owners_ref = refs[:3]
    piece_refs = refs[3 : 3 + count]
    rest = refs[3 + count :]
    if count > 1 and first:
        hot_y, hot_z = rest[:2]
        rest = rest[2:]
    else:
        hot_y, hot_z, given_ref = rest[:3]
        rest = rest[3:]
    if not first:
        rest = rest[2:]
    vel_ref, str_ref = rest[:2]
    rest = rest[2:]
    if first:
        values = rest[0]
        rest = rest[1:]
    else:
        values = given_ref
    fields, medium, added, stored, lines, sems = rest
    block_y = cells_y // count
    chunks = cells_y // ROWS

    if count > 1:
        centre = place_ref[0]
        start = ring_place(centre, count)
        boxes = [ring_box(lax.rem(start + step + count, count), count) for step in ring_offsets(count)]
        blocks = [map_ref[box] for box in boxes]
    else:
        centre = planes // 2
        blocks = [0]
    for block, piece in zip(blocks, piece_refs):
        top = pl.multiple_of(block * block_y, 8)
        for component in range(3):
            for plane in range(planes):
                source = (component * planes + plane) * block_y
                medium[component, plane, pl.ds(top, block_y), :] = (
                    TIME_STEP * piece[source : source + block_y, :]
                )

    outside = jnp.zeros((cells_y, cells_z), jnp.float32)
    for field in (XY, XZ, VX):
        fields[field, 0] = outside
    for field in (XX, VY, VZ):
        fields[field, planes + 1] = outside

    if first and count > 1:
        halves = planes * per // cells_z
        for box, piece in zip(boxes, piece_refs):
            source = 3 * planes * block_y
            stored[box] = piece[source : source + 6 * halves + (-6 * halves) % ROWS, :]
        for step in range(STEPS):
            owner = owners_ref[step]
            for comp in range(3):
                for half in range(halves):
                    source = (owner % 2) * 3 * halves + comp * halves + half
                    lines[half, pl.ds(step * 3 + comp, 1), :] = stored[owner // 2, pl.ds(source, 1), :]
        for plane in range(planes):
            half, place = divmod(plane * per, cells_z)
            line = lines[half]
            group = lax.broadcasted_iota(jnp.int32, line.shape, 1) // per
            spread = pltpu.roll(line, (cells_z - place) % cells_z, 1) if place else line
            spread = jnp.where(
                group == 0,
                spread,
                jnp.where(group == 1, pltpu.roll(spread, per, 1), pltpu.roll(spread, 2 * per, 1)),
            )
            values[plane] = split_values(spread, per)
    elif first:
        for plane in range(planes):
            values[plane] = split_values(given_ref[plane], per)

    def injection(step, comp, plane):
        row = values[plane, pl.ds(step * 3 + comp, 1), :]
        return lax.dot_general(
            hot_y[plane],
            (hot_z[plane] * row).astype(jnp.bfloat16),
            (((1,), (1,)), ((), ())),
            preferred_element_type=jnp.float32,
        )

    def limits(step):
        reach = STEPS - 1 - step
        return jnp.maximum(centre - reach, 0), jnp.minimum(centre + reach, planes - 1)

    def medium_at(component, plane, chunk):
        return medium[component, plane, chunk * ROWS : chunk * ROWS + ROWS, :]

    def put(field, plane, chunk, value):
        fields[field, plane + 1, chunk * ROWS : chunk * ROWS + ROWS, :] = value

    def added_at(comp, plane, chunk):
        return added[comp, plane, chunk * ROWS : chunk * ROWS + ROWS, :]

    def start_velocity(plane, carry):
        for comp in range(3):
            fields[comp, plane + 1] = injection(0, comp, plane)
        return carry

    def velocity_x(plane, carry):
        here = Plane(fields, cells_y, cells_z)
        index = plane + 1
        for chunk in range(chunks):
            pull = (
                (here.at(XX, index + 1, chunk, 1) - here.at(XX, index, chunk, 0))
                + here.back_y(XY, index, chunk)
                + here.back_z(here.at(XZ, index, chunk, 0))
            )
            new = here.at(VX, index, chunk, 0) + medium_at(2, plane, chunk) * pull
            put(VX, plane, chunk, new + added_at(0, plane, chunk))
        return carry

    def velocity_yz(plane, carry):
        here = Plane(fields, cells_y, cells_z)
        index = plane + 1
        for chunk in range(chunks):
            gain = medium_at(2, plane, chunk)
            pull = (
                (here.at(XY, index, chunk, 0) - here.at(XY, index - 1, chunk, -1))
                + here.fore_y(YY, index, chunk)
                + here.back_z(here.at(YZ, index, chunk, 0))
            )
            new = here.at(VY, index, chunk, 0) + gain * pull
            put(VY, plane, chunk, new + added_at(1, plane, chunk))
            pull = (
                (here.at(XZ, index, chunk, 0) - here.at(XZ, index - 1, chunk, -1))
                + here.back_y(YZ, index, chunk)
                + here.fore_z(here.at(ZZ, index, chunk, 0))
            )
            new = here.at(VZ, index, chunk, 0) + gain * pull
            put(VZ, plane, chunk, new + added_at(2, plane, chunk))
        return carry

    def stress(step, fresh, final, plane, carry):
        here = Plane(fields, cells_y, cells_z)
        index = plane + 1
        if not final:
            for comp in range(3):
                added[comp, plane] = injection(step + 1, comp, plane)
        for chunk in range(chunks):
            vx, vy, vz = (here.at(field, index, chunk, 0) for field in (VX, VY, VZ))
            lam, mu = medium_at(0, plane, chunk), medium_at(1, plane, chunk)
            twice = mu + mu
            grad_x = vx - here.at(VX, index - 1, chunk, -1)
            grad_y = here.back_y(VY, index, chunk)
            grad_z = here.back_z(vz)
            spread = lam * (grad_x + grad_y + grad_z)
            changes = (
                (XX, spread + twice * grad_x),
                (YY, spread + twice * grad_y),
                (ZZ, spread + twice * grad_z),
                (XY, mu * (here.fore_y(VX, index, chunk) + (here.at(VY, index + 1, chunk, 1) - vy))),
                (XZ, mu * (here.fore_z(vx) + (here.at(VZ, index + 1, chunk, 1) - vz))),
                (YZ, mu * (here.fore_z(vy) + here.fore_y(VZ, index, chunk))),
            )
            for field, change in changes:
                put(field, plane, chunk, change if fresh else here.at(field, index, chunk, 0) + change)
        return carry

    def velocities(step):
        low, high = limits(step)
        lax.fori_loop(jnp.maximum(low - 1, 0), high + 1, velocity_x, 0)
        lax.fori_loop(low, jnp.minimum(high + 2, planes), velocity_yz, 0)

    low, high = limits(0)
    lax.fori_loop(jnp.maximum(low - 1, 0), jnp.minimum(high + 2, planes), start_velocity, 0)
    lax.fori_loop(low, high + 1, functools.partial(stress, 0, True, False), 0)

    def one_step(step, carry):
        velocities(step)
        low, high = limits(step)
        lax.fori_loop(low, high + 1, functools.partial(stress, step, False, False), 0)
        return carry

    lax.fori_loop(1, STEPS - 1, one_step, 0)
    velocities(STEPS - 1)
    stress(STEPS - 1, False, True, centre, 0)

    copies = (
        pltpu.make_async_copy(fields.at[0:3, centre + 1], vel_ref.at[trial, :, 0], sems.at[0]),
        pltpu.make_async_copy(fields.at[3:9, centre + 1], str_ref.at[trial, :, 0], sems.at[1]),
    )
    for copy in copies:
        copy.start()
    for copy in copies:
        copy.wait()


def run_trial(trial, trials, shape, scalars, pieces, hots, given, before):
    planes, cells_y, cells_z, per = shape
    count, first = len(pieces), before is None
    smem, vmem, anywhere = (
        pl.BlockSpec(memory_space=space) for space in (pltpu.SMEM, pltpu.VMEM, pl.ANY)
    )
    operands = list(scalars) + list(pieces) + list(hots)
    specs = [smem] * 3 + [vmem] * (len(operands) - 3)
    if given is not None:
        operands.append(given)
        specs.append(vmem)
    out_shape = [
        jax.ShapeDtypeStruct((trials, 3, 1, cells_y, cells_z), jnp.float32),
        jax.ShapeDtypeStruct((trials, 6, 1, cells_y, cells_z), jnp.float32),
    ]
    out_specs = [anywhere, anywhere]
    aliases = {}
    if first:
        out_shape.append(jax.ShapeDtypeStruct((planes, LINES, cells_z), jnp.float32))
        out_specs.append(vmem)
    else:
        aliases = {len(operands): 0, len(operands) + 1: 1}
        operands += list(before)
        specs += [anywhere, anywhere]
    return pl.pallas_call(
        functools.partial(propagate, (trial, count, planes, cells_y, cells_z, per, first)),
        out_shape=out_shape,
        in_specs=specs,
        out_specs=out_specs,
        input_output_aliases=aliases,
        scratch_shapes=[
            pltpu.VMEM((9, planes + 2, cells_y, cells_z), jnp.float32),
            pltpu.VMEM((3, planes, cells_y, cells_z), jnp.float32),
            pltpu.VMEM((3, planes, cells_y, cells_z), jnp.float32),
            pltpu.VMEM((count, 2 * ROWS, cells_z), jnp.float32),
            pltpu.VMEM((2, LINES, cells_z), jnp.float32),
            pltpu.SemaphoreType.DMA((2,)),
        ],
        compiler_params=pltpu.CompilerParams(vmem_limit_bytes=40 * 1024 * 1024),
        cost_estimate=pl.CostEstimate(flops=30_000_000, bytes_accessed=5_000_000, transcendentals=0),
    )(*operands)


def from_behind(value, axis, steps):
    count = lax.axis_size(axis)
    leading, last = (max(0, -steps), min(count, count - steps))
    return lax.ppermute(value, axis, [(source, source + steps) for source in range(leading, last)])


def around(medium, store, count):
    trials = medium.shape[0]
    lanes = medium.shape[-1]
    order = [2 * place for place in range((count + 1) // 2)]
    order += [box for box in range(count - 1, 0, -1) if box % 2 == 1]
    up = [(order[place], order[(place + 1) % count]) for place in range(count)]
    down = [(target, source) for source, target in up]
    mine = store[0].reshape(-1, lanes)
    other = lax.ppermute(mine, "trial", [(0, 1), (1, 0)])
    lower = lax.axis_index("trial") == 0
    rows = [jnp.where(lower, mine, other), jnp.where(lower, other, mine)]
    filler = jnp.zeros(((-2 * mine.shape[0]) % ROWS, lanes), jnp.float32)
    own = [medium[trial].reshape(-1, lanes) for trial in range(trials)]
    own[0] = jnp.concatenate([own[0]] + rows + [filler])
    pieces = [[piece] for piece in own]
    forth, back = list(own), list(own)
    for _ in range(1, count // 2):
        for trial in range(trials):
            forth[trial] = lax.ppermute(forth[trial], "box", up)
            back[trial] = lax.ppermute(back[trial], "box", down)
            pieces[trial] += [forth[trial], back[trial]]
    for trial in range(trials):
        if trial % 2 == 0:
            pieces[trial].append(lax.ppermute(forth[trial], "box", up))
        else:
            pieces[trial].append(lax.ppermute(back[trial], "box", down))
    return pieces


def hot_planes(offsets, cells_y, cells_z):
    rows = jnp.arange(cells_y, dtype=jnp.int32)[None, :, None]
    columns = jnp.arange(cells_z, dtype=jnp.int32)[None, :, None]
    hot_y = (offsets[:, None, :] // cells_z == rows).astype(jnp.bfloat16)
    hot_z = (offsets[:, None, :] % cells_z == columns).astype(jnp.float32)
    return hot_y, hot_z


def per_device(medium, store, surf_off, owners, brick_map):
    boxes = lax.axis_size("box")
    place = lax.axis_index("box")
    trials_here, _, all_planes, brick_y, cells_z = medium.shape
    cells_y = boxes * brick_y
    per = surf_off.shape[0] // all_planes
    offsets = surf_off.reshape(all_planes, per)
    reach = STEPS
    if all_planes <= 2 * reach + 1 and boxes == 8 and lax.axis_size("trial") == 2:
        pieces = around(medium, store, boxes)
        planes = all_planes
        given = None
        scalars = (place[None], brick_map, owners)
    else:
        inverse = jnp.zeros((boxes,), jnp.int32).at[brick_map].set(jnp.arange(boxes, dtype=jnp.int32))
        moved = lax.all_to_all(medium, "box", split_axis=2, concat_axis=3, tiled=True)
        blocks = moved.reshape(trials_here, 3, 1, boxes, brick_y, cells_z)
        mine = jnp.take(blocks, inverse, axis=3).reshape(trials_here, 3, 1, cells_y, cells_z)
        window = jnp.concatenate(
            [from_behind(mine, "box", -shift) for shift in range(-reach, reach + 1)], axis=2
        )
        pieces = [[window[trial].reshape(-1, cells_z)] for trial in range(trials_here)]
        planes = 2 * reach + 1
        slot = place * lax.axis_size("trial") + lax.axis_index("trial")
        rows = lax.psum(jnp.where((owners == slot)[:, None, None], store, 0.0), ("box", "trial"))
        rows = rows.reshape(STEPS * 3, all_planes, per).transpose(1, 0, 2)
        rows = jnp.pad(rows, ((reach, reach), (0, LINES - STEPS * 3), (0, 0)))
        rows = lax.dynamic_slice_in_dim(rows, place, planes, 0)
        given = jnp.tile(rows, (1, 1, cells_z // per))
        offsets = jnp.pad(offsets, ((reach, reach), (0, 0)), constant_values=-1)
        offsets = lax.dynamic_slice_in_dim(offsets, place, planes, 0)
        scalars = (place[None], brick_map, owners)
    hots = hot_planes(jnp.tile(offsets, (1, cells_z // per)), cells_y, cells_z)
    shape = (planes, cells_y, cells_z, per)
    before = None
    for trial in range(trials_here):
        found = run_trial(trial, trials_here, shape, scalars, pieces[trial], hots, given, before)
        before = found[:2]
        if trial == 0:
            given = found[2]
    return tuple(before)


def solution(mesh):
    return jax.shard_map(
        per_device,
        mesh=mesh,
        in_specs=(
            P("trial", None, None, "box", None),
            P(("groups", "box", "trial"), None, None),
            P(),
            P(),
            P(),
        ),
        out_specs=(
            P(("groups", "trial"), None, "box", None, None),
            P(("groups", "trial"), None, "box", None, None),
        ),
        check_vma=False,
    )
```

profile of v0, /device:TPU:10, one launch (start us, length us, event | category | flops | bytes accessed | tf_op | source)
XLA Modules:
  0.0 72.3 jit_solution(5381724505644710568)
XLA Ops:
  0.6 0.7 reduce
  1.3 0.1 collective-permute-start.7
  1.4 1.1 %fusion.4 = (f32[1,3,8,16,128]{4,3,2,1,0:T(8,128)S(1)}, f32[1,3,8,16,128]{4,3,2,1,0:T(8,128)S(1)}) fusion(f32[2,3,8,16,128]{4,3,2,1,0:T(8,128)} %param.5), kind=kLoop, calls=%fused_computation.15 | loop fusion | bytes 786432 | tf_op jit(solution)/shard_map/slice | solution.py:335
  2.5 0.1 pad.3.clone
  2.6 0.0 collective-permute-done.7
  2.6 0.1 maximum_maximum_fusion.refs_3_
  2.7 0.5 collective-permute-start.8
  3.2 0.0 copy-start.2
  3.2 1.6 %collective-permute-start.1 = (f32[384,128]{1,0:T(8,128)S(1)}, f32[384,128]{1,0:T(8,128)S(1)}, u32[]{:S(2)}, u32[]{:S(2)}) collective-permute-start(f32[384,128]{1,0:T(8,128)S(1)} %bitcast.3), channel_id=1, source_target_pairs={{4,0},{8,4},{12,8},{14,12},{10,14},{6,10},{2,6},{0,2},{5,1},{9,5},... | collective-permute-start | bytes 589832 | tf_op jit(solution)/shard_map/ppermute | solution.py:342
  4.8 1.6 %collective-permute-start.9 = (f32[400,128]{1,0:T(8,128)S(1)}, f32[400,128]{1,0:T(8,128)S(1)}, u32[]{:S(2)}, u32[]{:S(2)}) collective-permute-start(f32[400,128]{1,0:T(8,128)S(1)} %maximum_maximum_fusion.refs_3_), channel_id=1, source_target_pairs={{4,0},{8,4},{12,8},{14,12},{10,14},{6,10},{2,6},{0,2},{5,1},{9,5},... | collective-permute-start | bytes 614408 | tf_op jit(solution)/shard_map/ppermute | solution.py:342
  6.4 3.9 %collective-permute-done.8.refs_4_ = f32[400,128]{1,0:T(8,128)S(1)} collective-permute-done((f32[400,128]{1,0:T(8,128)S(1)}, f32[400,128]{1,0:T(8,128)S(1)}, u32[]{:S(2)}, u32[]{:S(2)}) %collective-permute-start.8) | collective-permute-done | bytes 204832 | tf_op jit(solution)/shard_map/ppermute | solution.py:341
  10.2 0.4 collective-permute-start.10
  10.7 0.3 collective-permute-start
  11.0 0.0 collective-permute-done.1.refs_5_
  11.0 1.7 %collective-permute-start.3 = (f32[384,128]{1,0:T(8,128)S(1)}, f32[384,128]{1,0:T(8,128)S(1)}, u32[]{:S(2)}, u32[]{:S(2)}) collective-permute-start(f32[384,128]{1,0:T(8,128)S(1)} %collective-permute-done.1.refs_5_), channel_id=1, source_target_pairs={{4,0},{8,4},{12,8},{14,12},{10,14},{6,10},{2,6},{0,2},{5,1},{9,5},... | collective-permute-start | bytes 589832 | tf_op jit(solution)/shard_map/ppermute | solution.py:342
  12.7 0.0 copy-done.2
  12.7 0.1 tile.9
  12.8 0.1 tile.11
  12.9 8.3 %collective-permute-done.refs_4_ = f32[384,128]{1,0:T(8,128)S(1)} collective-permute-done((f32[384,128]{1,0:T(8,128)S(1)}, f32[384,128]{1,0:T(8,128)S(1)}, u32[]{:S(2)}, u32[]{:S(2)}) %collective-permute-start) | collective-permute-done | bytes 196640 | tf_op jit(solution)/shard_map/ppermute | solution.py:341
  21.1 0.4 collective-permute-start.2
  21.6 0.0 collective-permute-done.9.refs_5_
  21.6 1.6 %collective-permute-start.11 = (f32[400,128]{1,0:T(8,128)S(1)}, f32[400,128]{1,0:T(8,128)S(1)}, u32[]{:S(2)}, u32[]{:S(2)}) collective-permute-start(f32[400,128]{1,0:T(8,128)S(1)} %collective-permute-done.9.refs_5_), channel_id=1, source_target_pairs={{4,0},{8,4},{12,8},{14,12},{10,14},{6,10},{2,6},{0,2},{5,1},{9,5},... | collective-permute-start | bytes 614408 | tf_op jit(solution)/shard_map/ppermute | solution.py:342
  23.2 0.0 collective-permute-done.3.refs_7_
  23.2 1.6 %collective-permute-start.5 = (f32[384,128]{1,0:T(8,128)S(1)}, f32[384,128]{1,0:T(8,128)S(1)}, u32[]{:S(2)}, u32[]{:S(2)}) collective-permute-start(f32[384,128]{1,0:T(8,128)S(1)} %collective-permute-done.3.refs_7_), channel_id=1, source_target_pairs={{4,0},{8,4},{12,8},{14,12},{10,14},{6,10},{2,6},{0,2},{5,1},{9,5},... | collective-permute-start | bytes 589832 | tf_op jit(solution)/shard_map/ppermute | solution.py:342
  24.8 0.0 collective-permute-done.10.refs_6_
  24.8 0.4 collective-permute-start.12
  25.2 3.1 %collective-permute-done.2.refs_6_ = f32[384,128]{1,0:T(8,128)S(1)} collective-permute-done((f32[384,128]{1,0:T(8,128)S(1)}, f32[384,128]{1,0:T(8,128)S(1)}, u32[]{:S(2)}, u32[]{:S(2)}) %collective-permute-start.2) | collective-permute-done | bytes 196640 | tf_op jit(solution)/shard_map/ppermute | solution.py:341
  28.3 0.4 collective-permute-start.4
  28.8 0.8 %collective-permute-done.11.refs_7_ = f32[400,128]{1,0:T(8,128)S(1)} collective-permute-done((f32[400,128]{1,0:T(8,128)S(1)}, f32[400,128]{1,0:T(8,128)S(1)}, u32[]{:S(2)}, u32[]{:S(2)}) %collective-permute-start.11) | collective-permute-done | bytes 204832 | tf_op jit(solution)/shard_map/ppermute | solution.py:342
  29.6 1.6 %collective-permute-start.13 = (f32[400,128]{1,0:T(8,128)S(1)}, f32[400,128]{1,0:T(8,128)S(1)}, u32[]{:S(2)}, u32[]{:S(2)}) collective-permute-start(f32[400,128]{1,0:T(8,128)S(1)} %collective-permute-done.11.refs_7_), channel_id=1, source_target_pairs={{4,0},{8,4},{12,8},{14,12},{10,14},{6,10},{2,6},{0,2},{5,1},{9,5},... | collective-permute-start | bytes 614408 | tf_op jit(solution)/shard_map/ppermute | solution.py:342
  31.2 2.6 %collective-permute-done.5.refs_9_ = f32[384,128]{1,0:T(8,128)S(1)} collective-permute-done((f32[384,128]{1,0:T(8,128)S(1)}, f32[384,128]{1,0:T(8,128)S(1)}, u32[]{:S(2)}, u32[]{:S(2)}) %collective-permute-start.5) | collective-permute-done | bytes 196640 | tf_op jit(solution)/shard_map/ppermute | solution.py:342
  33.8 1.6 %collective-permute-start.6 = (f32[384,128]{1,0:T(8,128)S(1)}, f32[384,128]{1,0:T(8,128)S(1)}, u32[]{:S(2)}, u32[]{:S(2)}) collective-permute-start(f32[384,128]{1,0:T(8,128)S(1)} %collective-permute-done.5.refs_9_), channel_id=1, source_target_pairs={{4,0},{8,4},{12,8},{14,12},{10,14},{6,10},{2,6},{0,2},{5,1},{9,5},... | collective-permute-start | bytes 589832 | tf_op jit(solution)/shard_map/ppermute | solution.py:348
  35.4 0.0 collective-permute-done.12.refs_8_
  35.4 0.5 collective-permute-start.14
  35.9 0.1 fusion
  36.0 1.9 %collective-permute-done.13.refs_9_ = f32[400,128]{1,0:T(8,128)S(1)} collective-permute-done((f32[400,128]{1,0:T(8,128)S(1)}, f32[400,128]{1,0:T(8,128)S(1)}, u32[]{:S(2)}, u32[]{:S(2)}) %collective-permute-start.13) | collective-permute-done | bytes 204832 | tf_op jit(solution)/shard_map/ppermute | solution.py:342
  37.8 3.3 %collective-permute-done.14.refs_10_ = f32[400,128]{1,0:T(8,128)S(1)} collective-permute-done((f32[400,128]{1,0:T(8,128)S(1)}, f32[400,128]{1,0:T(8,128)S(1)}, u32[]{:S(2)}, u32[]{:S(2)}) %collective-permute-start.14) | collective-permute-done | bytes 204832 | tf_op jit(solution)/shard_map/ppermute | solution.py:346
  41.2 0.0 copy-start
  41.2 0.0 copy-start.1
  41.2 0.7 copy-done
  41.8 0.0 copy-done.1
  41.8 15.4 %shard_map.68 = (f32[2,3,1,128,128]{4,3,2,1,0:T(8,128)}, f32[2,6,1,128,128]{4,3,2,1,0:T(8,128)}, f32[8,24,128]{2,1,0:T(8,128)S(1)}) custom-call(s32[1]{0:T(128)} %bitcast.refs_0_, s32[8]{0:T(128)S(1)} %copy-done, s32[6]{0:T(128)S(1)} %copy-done.1, f32[400,128]{1,0:T(8,128)S(1)} %maximum_maximum_fusion.refs_3_, ...), custom_call_target="tpu_custom_call" | custom-call | flops 30000000 | bytes 5000000 | tf_op jit(solution)/shard_map/pallas_call | solution.py:298
  57.2 0.0 collective-permute-done.4.refs_8_
  57.2 0.0 collective-permute-done.6.refs_10_
  57.2 15.1 %shard_map.69 = (f32[2,3,1,128,128]{4,3,2,1,0:T(8,128)}, f32[2,6,1,128,128]{4,3,2,1,0:T(8,128)}) custom-call(s32[1]{0:T(128)} %bitcast.refs_0_, s32[8]{0:T(128)S(1)} %copy-done, s32[6]{0:T(128)S(1)} %copy-done.1, f32[384,128]{1,0:T(8,128)S(1)} %bitcast.5, ...), custom_call_target="tpu_custom_call", output_to_operand_aliasing={{0}: (14, {}), {1}: (15, {})} | custom-call | flops 30000000 | bytes 5000000 | tf_op jit(solution)/shard_map/pallas_call | solution.py:298
  (5 shorter events, 0.0 us)
Async XLA Ops:
  1.3 1.2 %collective-permute-start.7 = (f32[6,128]{1,0:T(8,128)S(1)}, f32[6,128]{1,0:T(8,128)S(1)}, u32[]{:S(2)}, u32[]{:S(2)}) collective-permute-start(f32[6,128]{1,0:T(8,128)S(1)} %reshape_squeeze.11), channel_id=1, source_target_pairs={{0,1},{1,0},{2,3},{3,2},{4,5},{5,4},{6,7},{7,6},{8,9},{9,8},{10,11... | collective-permute-start | bytes 9224 | tf_op jit(solution)/shard_map/ppermute | solution.py:331
  2.7 7.5 %collective-permute-start.8 = (f32[400,128]{1,0:T(8,128)S(1)}, f32[400,128]{1,0:T(8,128)S(1)}, u32[]{:S(2)}, u32[]{:S(2)}) collective-permute-start(f32[400,128]{1,0:T(8,128)S(1)} %maximum_maximum_fusion.refs_3_), channel_id=1, source_target_pairs={{0,4},{4,8},{8,12},{12,14},{14,10},{10,6},{6,2},{2,0},{1,5},{5,9},... | collective-permute-start | bytes 614408 | tf_op jit(solution)/shard_map/ppermute | solution.py:341
  3.2 9.5 %copy-start.2 = (s32[256]{0:T(256)S(1)}, s32[256]{0:T(256)}, u32[]{:S(2)}) copy-start(s32[256]{0:T(256)} %param.7) | copy-start | bytes 3076
  3.2 7.8 %collective-permute-start.1 = (f32[384,128]{1,0:T(8,128)S(1)}, f32[384,128]{1,0:T(8,128)S(1)}, u32[]{:S(2)}, u32[]{:S(2)}) collective-permute-start(f32[384,128]{1,0:T(8,128)S(1)} %bitcast.3), channel_id=1, source_target_pairs={{4,0},{8,4},{12,8},{14,12},{10,14},{6,10},{2,6},{0,2},{5,1},{9,5},... | collective-permute-start | bytes 589832 | tf_op jit(solution)/shard_map/ppermute | solution.py:342
  4.8 16.8 %collective-permute-start.9 = (f32[400,128]{1,0:T(8,128)S(1)}, f32[400,128]{1,0:T(8,128)S(1)}, u32[]{:S(2)}, u32[]{:S(2)}) collective-permute-start(f32[400,128]{1,0:T(8,128)S(1)} %maximum_maximum_fusion.refs_3_), channel_id=1, source_target_pairs={{4,0},{8,4},{12,8},{14,12},{10,14},{6,10},{2,6},{0,2},{5,1},{9,5},... | collective-permute-start | bytes 614408 | tf_op jit(solution)/shard_map/ppermute | solution.py:342
  10.2 14.5 %collective-permute-start.10 = (f32[400,128]{1,0:T(8,128)S(1)}, f32[400,128]{1,0:T(8,128)S(1)}, u32[]{:S(2)}, u32[]{:S(2)}) collective-permute-start(f32[400,128]{1,0:T(8,128)S(1)} %collective-permute-done.8.refs_4_), channel_id=1, source_target_pairs={{0,4},{4,8},{8,12},{12,14},{14,10},{10,6},{6,2},{2,0},{1,5},{5,9},... | collective-permute-start | bytes 614408 | tf_op jit(solution)/shard_map/ppermute | solution.py:341
  10.7 10.5 %collective-permute-start = (f32[384,128]{1,0:T(8,128)S(1)}, f32[384,128]{1,0:T(8,128)S(1)}, u32[]{:S(2)}, u32[]{:S(2)}) collective-permute-start(f32[384,128]{1,0:T(8,128)S(1)} %bitcast.4), channel_id=1, source_target_pairs={{0,4},{4,8},{8,12},{12,14},{14,10},{10,6},{6,2},{2,0},{1,5},{5,9},... | collective-permute-start | bytes 589832 | tf_op jit(solution)/shard_map/ppermute | solution.py:341
  11.0 12.2 %collective-permute-start.3 = (f32[384,128]{1,0:T(8,128)S(1)}, f32[384,128]{1,0:T(8,128)S(1)}, u32[]{:S(2)}, u32[]{:S(2)}) collective-permute-start(f32[384,128]{1,0:T(8,128)S(1)} %collective-permute-done.1.refs_5_), channel_id=1, source_target_pairs={{4,0},{8,4},{12,8},{14,12},{10,14},{6,10},{2,6},{0,2},{5,1},{9,5},... | collective-permute-start | bytes 589832 | tf_op jit(solution)/shard_map/ppermute | solution.py:342
  21.1 7.2 %collective-permute-start.2 = (f32[384,128]{1,0:T(8,128)S(1)}, f32[384,128]{1,0:T(8,128)S(1)}, u32[]{:S(2)}, u32[]{:S(2)}) collective-permute-start(f32[384,128]{1,0:T(8,128)S(1)} %collective-permute-done.refs_4_), channel_id=1, source_target_pairs={{0,4},{4,8},{8,12},{12,14},{14,10},{10,6},{6,2},{2,0},{1,5},{5,9},... | collective-permute-start | bytes 589832 | tf_op jit(solution)/shard_map/ppermute | solution.py:341
  21.6 8.0 %collective-permute-start.11 = (f32[400,128]{1,0:T(8,128)S(1)}, f32[400,128]{1,0:T(8,128)S(1)}, u32[]{:S(2)}, u32[]{:S(2)}) collective-permute-start(f32[400,128]{1,0:T(8,128)S(1)} %collective-permute-done.9.refs_5_), channel_id=1, source_target_pairs={{4,0},{8,4},{12,8},{14,12},{10,14},{6,10},{2,6},{0,2},{5,1},{9,5},... | collective-permute-start | bytes 614408 | tf_op jit(solution)/shard_map/ppermute | solution.py:342
  23.2 10.6 %collective-permute-start.5 = (f32[384,128]{1,0:T(8,128)S(1)}, f32[384,128]{1,0:T(8,128)S(1)}, u32[]{:S(2)}, u32[]{:S(2)}) collective-permute-start(f32[384,128]{1,0:T(8,128)S(1)} %collective-permute-done.3.refs_7_), channel_id=1, source_target_pairs={{4,0},{8,4},{12,8},{14,12},{10,14},{6,10},{2,6},{0,2},{5,1},{9,5},... | collective-permute-start | bytes 589832 | tf_op jit(solution)/shard_map/ppermute | solution.py:342
  24.8 10.6 %collective-permute-start.12 = (f32[400,128]{1,0:T(8,128)S(1)}, f32[400,128]{1,0:T(8,128)S(1)}, u32[]{:S(2)}, u32[]{:S(2)}) collective-permute-start(f32[400,128]{1,0:T(8,128)S(1)} %collective-permute-done.10.refs_6_), channel_id=1, source_target_pairs={{0,4},{4,8},{8,12},{12,14},{14,10},{10,6},{6,2},{2,0},{1,5},{5,9},... | collective-permute-start | bytes 614408 | tf_op jit(solution)/shard_map/ppermute | solution.py:341
  28.3 28.9 %collective-permute-start.4 = (f32[384,128]{1,0:T(8,128)S(1)}, f32[384,128]{1,0:T(8,128)S(1)}, u32[]{:S(2)}, u32[]{:S(2)}) collective-permute-start(f32[384,128]{1,0:T(8,128)S(1)} %collective-permute-done.2.refs_6_), channel_id=1, source_target_pairs={{0,4},{4,8},{8,12},{12,14},{14,10},{10,6},{6,2},{2,0},{1,5},{5,9},... | collective-permute-start | bytes 589832 | tf_op jit(solution)/shard_map/ppermute | solution.py:341
  29.6 8.2 %collective-permute-start.13 = (f32[400,128]{1,0:T(8,128)S(1)}, f32[400,128]{1,0:T(8,128)S(1)}, u32[]{:S(2)}, u32[]{:S(2)}) collective-permute-start(f32[400,128]{1,0:T(8,128)S(1)} %collective-permute-done.11.refs_7_), channel_id=1, source_target_pairs={{4,0},{8,4},{12,8},{14,12},{10,14},{6,10},{2,6},{0,2},{5,1},{9,5},... | collective-permute-start | bytes 614408 | tf_op jit(solution)/shard_map/ppermute | solution.py:342
  33.8 23.4 %collective-permute-start.6 = (f32[384,128]{1,0:T(8,128)S(1)}, f32[384,128]{1,0:T(8,128)S(1)}, u32[]{:S(2)}, u32[]{:S(2)}) collective-permute-start(f32[384,128]{1,0:T(8,128)S(1)} %collective-permute-done.5.refs_9_), channel_id=1, source_target_pairs={{4,0},{8,4},{12,8},{14,12},{10,14},{6,10},{2,6},{0,2},{5,1},{9,5},... | collective-permute-start | bytes 589832 | tf_op jit(solution)/shard_map/ppermute | solution.py:348
  35.4 5.8 %collective-permute-start.14 = (f32[400,128]{1,0:T(8,128)S(1)}, f32[400,128]{1,0:T(8,128)S(1)}, u32[]{:S(2)}, u32[]{:S(2)}) collective-permute-start(f32[400,128]{1,0:T(8,128)S(1)} %collective-permute-done.12.refs_8_), channel_id=1, source_target_pairs={{0,4},{4,8},{8,12},{12,14},{14,10},{10,6},{6,2},{2,0},{1,5},{5,9},... | collective-permute-start | bytes 614408 | tf_op jit(solution)/shard_map/ppermute | solution.py:346
  41.2 0.7 copy-start
  41.2 0.7 copy-start.1
where the time goes:
time: 72.5 us; the launch traced here: 72.3 us
  Pallas kernels  30.4 us (42%)
  waiting for transfers between devices  23.9 us (33%)
  starting transfers between devices  14.3 us (20%)
  local copies, waits for them, and re-layouts  1.98 us (3%)
  other arithmetic  0.93 us (1%)
    pallas_call x2, Pallas kernels, run_trial(): pl.pallas_call(functools.partial(propagate, (trial, count, planes, cells_...  30.4 us
    ppermute x6, waiting for transfers between devices, around(): forth[trial] = lax.ppermute(forth[trial], 'box', up)  15.3 us
    ppermute x6, starting transfers between devices, around(): back[trial] = lax.ppermute(back[trial], 'box', down)  9.62 us
    ppermute x6, waiting for transfers between devices, around(): back[trial] = lax.ppermute(back[trial], 'box', down)  5.34 us
    ppermute x1, waiting for transfers between devices, around(): pieces[trial].append(lax.ppermute(forth[trial], 'box', up))  3.33 us
    ppermute x6, starting transfers between devices, around(): forth[trial] = lax.ppermute(forth[trial], 'box', up)  2.59 us
    ppermute x1, starting transfers between devices, around(): pieces[trial].append(lax.ppermute(back[trial], 'box', down))  1.58 us
  transfers between devices with their start and end apart: 15, of which 7 were waited for; matrix products, arithmetic and copies ran while one was open for 2% of the time, Pallas kernels for 21%

commit v1 on v0

v1 whole, which is shorter than its diff:
```python
import functools

import jax
import jax.numpy as jnp
from jax import lax
from jax.experimental import pallas as pl
from jax.experimental.pallas import tpu as pltpu
from jax.sharding import PartitionSpec as P

STEPS = 6
TIME_STEP = 0.25
VX, VY, VZ, XX, YY, ZZ, XY, XZ, YZ = range(9)
ROWS = 8
LINES = 24


def ring_place(box, count):
    return jnp.where(box % 2 == 0, box // 2, count - 1 - box // 2)


def ring_box(place, count):
    return jnp.where(place < count // 2, 2 * place, 2 * (count - 1 - place) + 1)


def ring_offsets(count):
    steps = [0]
    for distance in range(1, count // 2):
        steps += [-distance, distance]
    return steps + [count // 2]


def split_values(value, per):
    group = lax.broadcasted_iota(jnp.int32, value.shape, 1) // per
    high = value.astype(jnp.bfloat16).astype(jnp.float32)
    rest = value - high
    middle = rest.astype(jnp.bfloat16).astype(jnp.float32)
    low = rest - middle
    return jnp.where(
        group == 0, high, jnp.where(group == 1, middle, jnp.where(group == 2, low, 0.0))
    )


class Plane:
    def __init__(self, fields, index, cells_y, cells_z):
        self.fields, self.index, self.chunks = fields, index, cells_y // ROWS
        row = lax.broadcasted_iota(jnp.int32, (ROWS, cells_z), 0)
        lane = lax.broadcasted_iota(jnp.int32, (ROWS, cells_z), 1)
        self.first_row, self.last_row = row == 0, row == ROWS - 1
        self.first_lane, self.last_lane = lane == 0, lane == cells_z - 1
        self.cells_z = cells_z
        self.loaded, self.rolled = {}, {}

    def at(self, field, chunk, beside=0):
        if (field, chunk, beside) not in self.loaded:
            self.loaded[field, chunk, beside] = self.fields[field][
                self.index + beside, chunk * ROWS : chunk * ROWS + ROWS, :
            ]
        return self.loaded[field, chunk, beside]

    def put(self, field, chunk, value):
        self.fields[field][self.index, chunk * ROWS : chunk * ROWS + ROWS, :] = value

    def roll_rows(self, field, chunk, by):
        if not 0 <= chunk < self.chunks:
            return 0.0
        if (field, chunk) not in self.rolled:
            self.rolled[field, chunk] = pltpu.roll(self.at(field, chunk), by, 0)
        return self.rolled[field, chunk]

    def back_y(self, field, chunk):
        here = self.roll_rows(field, chunk, 1)
        before = self.roll_rows(field, chunk - 1, 1)
        return self.at(field, chunk) - jnp.where(self.first_row, before, here)

    def fore_y(self, field, chunk):
        here = self.roll_rows(field, chunk, ROWS - 1)
        after = self.roll_rows(field, chunk + 1, ROWS - 1)
        return jnp.where(self.last_row, after, here) - self.at(field, chunk)

    def back_x(self, field, chunk):
        return self.at(field, chunk) - self.at(field, chunk, -1)

    def fore_x(self, field, chunk):
        return self.at(field, chunk, 1) - self.at(field, chunk)

    def back_z(self, field, chunk):
        value = self.at(field, chunk)
        return value - jnp.where(self.first_lane, 0.0, pltpu.roll(value, 1, 1))

    def fore_z(self, field, chunk):
        value = self.at(field, chunk)
        return jnp.where(self.last_lane, 0.0, pltpu.roll(value, self.cells_z - 1, 1)) - value


def propagate(plan, *refs):
    parts, row_parts, ring, planes, cells_y, cells_z, per, first = plan
    refs = list(refs)
    place_ref, map_ref, owners_ref = refs[:3]
    operands = 1 + max(part[0] for part in parts)
    piece_refs = refs[3 : 3 + operands]
    rest = refs[3 + operands :]
    hot_y, hot_z = rest[:2]
    rest = rest[2:]
    if ring == 1 or not first:
        given_ref = rest[0]
        rest = rest[1:]
    if not first:
        rest = rest[2:]
    vel_ref, str_ref = rest[:2]
    rest = rest[2:]
    if first:
        values = rest[0]
        rest = rest[1:]
    else:
        values = given_ref
    fields, (medium, added, stored, lines, sems) = rest[:9], rest[9:]
    block_y = cells_y // ring
    chunks = cells_y // ROWS

    if ring > 1:
        centre = place_ref[0]
        start = ring_place(centre, ring)
        boxes = {
            step: ring_box(lax.rem(start + step + ring, ring), ring) for step in ring_offsets(ring)
        }
        blocks = {step: map_ref[box] for step, box in boxes.items()}
    else:
        centre = planes // 2
        blocks = {0: 0}
    for operand, row, first_unit, units, offset in parts:
        top = pl.multiple_of(blocks[offset] * block_y, 8)
        for unit in range(units):
            component, plane = divmod(first_unit + unit, planes)
            source = row + unit * block_y
            medium[component, plane, pl.ds(top, block_y), :] = (
                TIME_STEP * piece_refs[operand][source : source + block_y, :]
            )

    outside = jnp.zeros((cells_y, cells_z), jnp.float32)
    for field in (XY, XZ, VX):
        fields[field][0] = outside
    for field in (XX, VY, VZ):
        fields[field][planes + 1] = outside

    if first and ring > 1:
        halves = planes * per // cells_z
        for operand, row, offset in row_parts:
            stored[boxes[offset]] = piece_refs[operand][row : row + 2 * ROWS, :]
        for step in range(STEPS):
            owner = owners_ref[step]
            for comp in range(3):
                for half in range(halves):
                    source = (owner % 2) * 3 * halves + comp * halves + half
                    lines[half, pl.ds(step * 3 + comp, 1), :] = stored[owner // 2, pl.ds(source, 1), :]
        for plane in range(planes):
            half, begin = divmod(plane * per, cells_z)
            line = lines[half]
            group = lax.broadcasted_iota(jnp.int32, line.shape, 1) // per
            spread = pltpu.roll(line, cells_z - begin, 1) if begin else line
            spread = jnp.where(
                group == 0,
                spread,
                jnp.where(group == 1, pltpu.roll(spread, per, 1), pltpu.roll(spread, 2 * per, 1)),
            )
            values[plane] = split_values(spread, per)
    elif first:
        for plane in range(planes):
            values[plane] = split_values(given_ref[plane], per)

    def inject(step, plane):
        spots = hot_y[plane]
        rows = [values[plane, pl.ds(step * 3 + comp, 1), :] for comp in range(3)]
        weighted = jnp.concatenate([(spots * row).astype(jnp.bfloat16) for row in rows], axis=0)
        found = jnp.dot(weighted, hot_z[plane], preferred_element_type=jnp.float32)
        return [found[comp * cells_y : comp * cells_y + cells_y] for comp in range(3)]

    def limits(step):
        reach = STEPS - 1 - step
        return jnp.maximum(centre - reach, 0), jnp.minimum(centre + reach, planes - 1)

    def medium_at(component, plane, chunk):
        return medium[component, plane, chunk * ROWS : chunk * ROWS + ROWS, :]

    def added_at(comp, plane, chunk):
        return added[comp, plane, chunk * ROWS : chunk * ROWS + ROWS, :]

    def start_velocity(plane, carry):
        for comp, value in enumerate(inject(0, plane)):
            fields[comp][plane + 1] = value
        return carry

    def velocity(components, plane, carry):
        here = Plane(fields, plane + 1, cells_y, cells_z)
        for chunk in range(chunks):
            gain = medium_at(2, plane, chunk)
            pulls = []
            if VX in components:
                pull = here.fore_x(XX, chunk) + here.back_y(XY, chunk) + here.back_z(XZ, chunk)
                pulls.append((VX, pull))
            if VY in components:
                pull = here.back_x(XY, chunk) + here.fore_y(YY, chunk) + here.back_z(YZ, chunk)
                pulls.append((VY, pull))
            if VZ in components:
                pull = here.back_x(XZ, chunk) + here.back_y(YZ, chunk) + here.fore_z(ZZ, chunk)
                pulls.append((VZ, pull))
            for comp, pull in pulls:
                new = here.at(comp, chunk) + gain * pull
                here.put(comp, chunk, new + added_at(comp, plane, chunk))
        return carry

    def stress(step, fresh, final, plane, carry):
        here = Plane(fields, plane + 1, cells_y, cells_z)
        if not final:
            for comp, value in enumerate(inject(step + 1, plane)):
                added[comp, plane] = value
        for chunk in range(chunks):
            lam, mu = medium_at(0, plane, chunk), medium_at(1, plane, chunk)
            twice = mu + mu
            grad_x, grad_y, grad_z = here.back_x(VX, chunk), here.back_y(VY, chunk), here.back_z(VZ, chunk)
            spread = lam * (grad_x + grad_y + grad_z)
            changes = (
                (XX, spread + twice * grad_x),
                (YY, spread + twice * grad_y),
                (ZZ, spread + twice * grad_z),
                (XY, mu * (here.fore_y(VX, chunk) + here.fore_x(VY, chunk))),
                (XZ, mu * (here.fore_z(VX, chunk) + here.fore_x(VZ, chunk))),
                (YZ, mu * (here.fore_z(VY, chunk) + here.fore_y(VZ, chunk))),
            )
            for field, change in changes:
                here.put(field, chunk, change if fresh else here.at(field, chunk) + change)
        return carry

    def velocities(step):
        low, high = limits(step)
        lax.fori_loop(jnp.maximum(low - 1, 0), low, functools.partial(velocity, (VX,)), 0)
        lax.fori_loop(low, high + 1, functools.partial(velocity, (VX, VY, VZ)), 0)
        lax.fori_loop(high + 1, jnp.minimum(high + 2, planes), functools.partial(velocity, (VY, VZ)), 0)

    low, high = limits(0)
    lax.fori_loop(jnp.maximum(low - 1, 0), jnp.minimum(high + 2, planes), start_velocity, 0)
    lax.fori_loop(low, high + 1, functools.partial(stress, 0, True, False), 0)

    def one_step(step, carry):
        velocities(step)
        low, high = limits(step)
        lax.fori_loop(low, high + 1, functools.partial(stress, step, False, False), 0)
        return carry

    lax.fori_loop(1, STEPS - 1, one_step, 0)
    velocities(STEPS - 1)
    stress(STEPS - 1, False, True, centre, 0)

    trial = place_ref[1]
    copies = []
    for field in range(9):
        target = vel_ref.at[trial, field, 0] if field < 3 else str_ref.at[trial, field - 3, 0]
        copies.append(pltpu.make_async_copy(fields[field].at[centre + 1], target, sems.at[field]))
    for copy in copies:
        copy.start()
    for copy in copies:
        copy.wait()


def run_trial(trials, shape, ring, scalars, found, hots, given, before):
    planes, cells_y, cells_z, per = shape
    pieces, parts, row_parts = found
    first = before is None
    smem, vmem, anywhere = (
        pl.BlockSpec(memory_space=space) for space in (pltpu.SMEM, pltpu.VMEM, pl.ANY)
    )
    operands = list(scalars) + list(pieces) + list(hots)
    specs = [smem] * 3 + [vmem] * (len(operands) - 3)
    if given is not None:
        operands.append(given)
        specs.append(vmem)
    out_shape = [
        jax.ShapeDtypeStruct((trials, 3, 1, cells_y, cells_z), jnp.float32),
        jax.ShapeDtypeStruct((trials, 6, 1, cells_y, cells_z), jnp.float32),
    ]
    out_specs = [anywhere, anywhere]
    aliases = {}
    if first:
        out_shape.append(jax.ShapeDtypeStruct((planes, LINES, cells_z), jnp.float32))
        out_specs.append(vmem)
    else:
        aliases = {len(operands): 0, len(operands) + 1: 1}
        operands += list(before)
        specs += [anywhere, anywhere]
    field = pltpu.VMEM((planes + 2, cells_y, cells_z), jnp.float32)
    return pl.pallas_call(
        functools.partial(propagate, (parts, row_parts, ring, planes, cells_y, cells_z, per, first)),
        out_shape=out_shape,
        in_specs=specs,
        out_specs=out_specs,
        input_output_aliases=aliases,
        scratch_shapes=[field] * 9
        + [
            pltpu.VMEM((3, planes, cells_y, cells_z), jnp.float32),
            pltpu.VMEM((3, planes, cells_y, cells_z), jnp.float32),
            pltpu.VMEM((ring, 2 * ROWS, cells_z), jnp.float32),
            pltpu.VMEM((2, LINES, cells_z), jnp.float32),
            pltpu.SemaphoreType.DMA((9,)),
        ],
        compiler_params=pltpu.CompilerParams(vmem_limit_bytes=40 * 1024 * 1024),
        cost_estimate=pl.CostEstimate(flops=30_000_000, bytes_accessed=5_000_000, transcendentals=0),
    )(*operands)


def from_behind(value, axis, steps):
    count = lax.axis_size(axis)
    leading, last = (max(0, -steps), min(count, count - steps))
    return lax.ppermute(value, axis, [(source, source + steps) for source in range(leading, last)])


def around(medium, store, count):
    lanes = medium.shape[-1]
    group = lax.axis_index("groups")
    order = [2 * place for place in range((count + 1) // 2)]
    order += [box for box in range(count - 1, 0, -1) if box % 2 == 1]
    up = [(order[place], order[(place + 1) % count]) for place in range(count)]
    down = [(target, source) for source, target in up]

    def across(value):
        return lax.ppermute(value, "groups", [(0, 1), (1, 0)])

    mine = store[0].reshape(-1, lanes)
    other = lax.ppermute(mine, "trial", [(0, 1), (1, 0)])
    lower = lax.axis_index("trial") == 0
    rows = [jnp.where(lower, mine, other), jnp.where(lower, other, mine)]
    filler = jnp.zeros(((-2 * mine.shape[0]) % ROWS, lanes), jnp.float32)
    bricks = [lax.dynamic_index_in_dim(medium, which, 0, False).reshape(-1, lanes) for which in (group, 1 - group)]
    size = bricks[0].shape[0]
    third, half = size // 3, size // 2
    units = size // medium.shape[3]
    first = jnp.concatenate([bricks[0]] + rows + [filler])
    later = bricks[1][:third]
    pieces, parts, row_parts = [[first], [bricks[1]]], [[(0, 0, 0, units, 0)], [(0, 0, 0, units, 0)]], [(0, size, 0)]

    def keep(which, piece, entries):
        parts[which] += [(len(pieces[which]),) + entry for entry in entries]
        pieces[which].append(piece)

    forth, back, forth_later, back_later, rests = first, first, later, later, []
    for distance in range(1, count // 2):
        forth, back = lax.ppermute(forth, "box", up), lax.ppermute(back, "box", down)
        forth_later = lax.ppermute(forth_later, "box", up)
        back_later = lax.ppermute(back_later, "box", down)
        rest = across(jnp.concatenate([forth[third:size], back[third:size]]))
        rests.append(rest)
        for piece, offset in ((forth, -distance), (back, distance)):
            row_parts.append((len(pieces[0]), size, offset))
            keep(0, piece, [(0, 0, units, offset)])
        for piece, offset in ((forth_later, -distance), (back_later, distance)):
            keep(1, piece, [(0, 0, units // 3, offset)])
        keep(1, rest, [(0, units // 3, units - units // 3, -distance),
                       (size - third, units // 3, units - units // 3, distance)])
    far = count // 2
    forth, back, _ = lax.optimization_barrier((forth, back, rests[0]))
    forth, back = lax.ppermute(forth[:half], "box", up), lax.ppermute(back[half:], "box", down)
    row_parts.append((len(pieces[0]) + 1, size - half, far))
    keep(0, forth, [(0, 0, units // 2, far)])
    keep(0, back, [(0, units // 2, units - units // 2, far)])
    keep(1, lax.ppermute(forth_later, "box", up), [(0, 0, units // 3, far)])
    rest = across(jnp.concatenate([forth[third:], back[: size - half]]))
    pieces[0][-1], _ = lax.optimization_barrier((pieces[0][-1], rests[1]))
    keep(1, rest, [(0, units // 3, units - units // 3, far)])
    return (pieces[0], parts[0], row_parts), (pieces[1], parts[1], [])


def hot_planes(offsets, cells_y, cells_z):
    rows = jnp.arange(cells_y, dtype=jnp.int32)[None, :, None]
    columns = jnp.arange(cells_z, dtype=jnp.int32)[None, None, :]
    hot_y = (offsets[:, None, :] // cells_z == rows).astype(jnp.float32)
    hot_z = (offsets[:, :, None] % cells_z == columns).astype(jnp.bfloat16)
    return hot_y, hot_z


def per_device(medium, store, surf_off, owners, brick_map):
    boxes = lax.axis_size("box")
    place = lax.axis_index("box")
    trials_here, _, all_planes, brick_y, cells_z = medium.shape
    cells_y = boxes * brick_y
    per = surf_off.shape[0] // all_planes
    offsets = surf_off.reshape(all_planes, per)
    reach = STEPS
    pairs = lax.axis_size("trial") == 2 and lax.axis_size("groups") == 2 and trials_here == 2
    if pairs and boxes == 8 and all_planes == 8:
        ring, planes, given = boxes, all_planes, None
        found = around(medium, store, boxes)
        slots = [lax.axis_index("groups"), 1 - lax.axis_index("groups")]
    else:
        inverse = jnp.zeros((boxes,), jnp.int32).at[brick_map].set(jnp.arange(boxes, dtype=jnp.int32))
        moved = lax.all_to_all(medium, "box", split_axis=2, concat_axis=3, tiled=True)
        blocks = moved.reshape(trials_here, 3, 1, boxes, brick_y, cells_z)
        mine = jnp.take(blocks, inverse, axis=3).reshape(trials_here, 3, 1, cells_y, cells_z)
        window = jnp.concatenate(
            [from_behind(mine, "box", -shift) for shift in range(-reach, reach + 1)], axis=2
        )
        ring, planes = 1, 2 * reach + 1
        found = [
            ([window[trial].reshape(-1, cells_z)], [(0, 0, 0, 3 * planes, 0)], []) for trial in range(trials_here)
        ]
        slot = place * lax.axis_size("trial") + lax.axis_index("trial")
        rows = lax.psum(jnp.where((owners == slot)[:, None, None], store, 0.0), ("box", "trial"))
        rows = rows.reshape(STEPS * 3, all_planes, per).transpose(1, 0, 2)
        rows = jnp.pad(rows, ((reach, reach), (0, LINES - STEPS * 3), (0, 0)))
        rows = lax.dynamic_slice_in_dim(rows, place, planes, 0)
        given = jnp.tile(rows, (1, 1, cells_z // per))
        offsets = jnp.pad(offsets, ((reach, reach), (0, 0)), constant_values=-1)
        offsets = lax.dynamic_slice_in_dim(offsets, place, planes, 0)
        slots = list(range(trials_here))
    hots = hot_planes(jnp.tile(offsets, (1, cells_z // per)), cells_y, cells_z)
    shape = (planes, cells_y, cells_z, per)
    before = None
    for trial in range(trials_here):
        geometry = jnp.stack([place, jnp.int32(slots[trial])])
        scalars = (geometry, brick_map, owners)
        results = run_trial(trials_here, shape, ring, scalars, found[trial], hots, given, before)
        before = results[:2]
        if trial == 0:
            given = results[2]
    return tuple(before)


def solution(mesh):
    return jax.shard_map(
        per_device,
        mesh=mesh,
        in_specs=(
            P("trial", None, None, "box", None),
            P(("groups", "box", "trial"), None, None),
            P(),
            P(),
            P(),
        ),
        out_specs=(
            P(("groups", "trial"), None, "box", None, None),
            P(("groups", "trial"), None, "box", None, None),
        ),
        check_vma=False,
    )
```

time: 72.5 us -> 61.2 us (0.84)
  waiting for transfers between devices: 23.9 us -> 9.86 us
  Pallas kernels: 30.4 us -> 24.3 us
  starting transfers between devices: 14.3 us -> 20.2 us
  local copies, waits for them, and re-layouts: 1.98 us -> 3.79 us
    ppermute x14 -> x19, waiting for transfers between devices: 23.9 us -> 9.86 us  [the longest x3 5.8 us: around(): lax.ppermute(forth, 'box', up)]
    pallas_call x2, Pallas kernels: 30.4 us -> 24.3 us  [run_trial(): pl.pallas_call(functools.partial(propagate, (parts, row_parts, ring, plan...]
    ppermute x14 -> x19, starting transfers between devices: 14.2 us -> 20.1 us  [the longest x4 5.26 us: across(): return lax.ppermute(value, 'groups', [(0, 1), (1, 0)])]
    dynamic_slice x0 -> x1, local copies, waits for them, and re-layouts: none -> 1.05 us  [around(): lax.dynamic_index_in_dim(medium, which, 0, False).reshape(-1, lanes)]
    slice x1 -> x12, local copies, waits for them, and re-layouts: 1.05 us -> 1.81 us  [the longest x7 0.94 us: around(): rest = across(jnp.concatenate([forth[third:size], back[third:size]]))]
  transfers between devices with their start and end apart: 15 -> 20, of which waited for: 7 -> 5; matrix products, arithmetic and copies ran while one was open for 2% -> 4% of each run, Pallas kernels for 21% -> 20%
where the time goes in v1:
time: 61.2 us; the launch traced here: 60.3 us
  Pallas kernels  24.3 us (40%)
  starting transfers between devices  20.2 us (33%)
  waiting for transfers between devices  9.86 us (16%)
  local copies, waits for them, and re-layouts  3.79 us (6%)
  other arithmetic  1.26 us (2%)
  between operations  0.85 us (1%)
    pallas_call x2, Pallas kernels, run_trial(): pl.pallas_call(functools.partial(propagate, (parts, row_parts, ring, plan...  24.3 us
    ppermute x3, waiting for transfers between devices, around(): lax.ppermute(forth, 'box', up)  5.8 us
    ppermute x4, starting transfers between devices, across(): return lax.ppermute(value, 'groups', [(0, 1), (1, 0)])  5.26 us
    ppermute x3, starting transfers between devices, around(): back_later = lax.ppermute(back_later, 'box', down)  4.78 us
    ppermute x3, starting transfers between devices, around(): lax.ppermute(back, 'box', down)  4.73 us
    ppermute x1, waiting for transfers between devices, around(): lax.ppermute(forth[:half], 'box', up)  3.24 us
    ppermute x1, starting transfers between devices, around(): lax.ppermute(back[half:], 'box', down)  1.63 us
    ppermute x3, starting transfers between devices, around(): lax.ppermute(forth, 'box', up)  1.4 us
  transfers between devices with their start and end apart: 20, of which 5 were waited for; matrix products, arithmetic and copies ran while one was open for 4% of the time, Pallas kernels for 20%

profile of v1, /device:TPU:10, one launch (start us, length us, event | category | flops | bytes accessed | tf_op | source)
XLA Modules:
  0.0 60.3 jit_solution(8371984005070699811)
XLA Ops:
  0.6 0.7 %reduce = f32[3,256]{1,0:T(4,128)S(1)} reduce(f32[1,3,256]{2,0,1:T(1,128)} %param.6, f32[]{:T(128)} %constant.54), dimensions={0}, to_apply=%param.6.reduce_sub_computation | reduce | bytes 6148 | tf_op args[1]
  1.3 0.1 collective-permute-start.2
  1.4 1.1 %constant_dynamic-slice_fusion.1 = (f32[1,3,8,16,128]{4,3,2,1,0:T(8,128)S(1)}, f32[1,3,8,16,128]{4,3,2,1,0:T(8,128)S(1)}) fusion(f32[2,3,8,16,128]{4,3,2,1,0:T(8,128)} %param.5, s32[]{:T(128)S(6)} %select_n.42, s32[]{:T(128)S(6)} %select_n.41), kind=kLoop, calls=%fused_computation.20 | loop fusion | bytes 786440 | tf_op jit(solution)/shard_map/jit(dynamic_index_in_dim)/dynamic_slice | solution.py:331
  2.5 0.1 pad.13.clone
  2.6 0.0 collective-permute-done.2
  2.6 0.1 maximum_maximum_fusion.refs_3_
  2.7 0.5 collective-permute-start.3
  3.2 1.6 %collective-permute-start.4 = (f32[400,128]{1,0:T(8,128)S(1)}, f32[400,128]{1,0:T(8,128)S(1)}, u32[]{:S(2)}, u32[]{:S(2)}) collective-permute-start(f32[400,128]{1,0:T(8,128)S(1)} %maximum_maximum_fusion.refs_3_), channel_id=1, source_target_pairs={{4,0},{8,4},{12,8},{14,12},{10,14},{6,10},{2,6},{0,2},{5,1},{9,5},... | collective-permute-start | bytes 614408 | tf_op jit(solution)/shard_map/ppermute | solution.py:345
  4.8 0.8 %constant_dynamic-slice_fusion = f32[1,1,8,16,128]{4,3,2,1,0:T(8,128)S(1)} fusion(f32[2,3,8,16,128]{4,3,2,1,0:T(8,128)} %param.5, s32[]{:T(128)S(6)} %select_n.41), kind=kLoop, calls=%fused_computation.19 | loop fusion | bytes 131076 | tf_op jit(solution)/shard_map/slice | solution.py:336
  5.6 0.0 copy-start.4
  5.6 0.4 collective-permute-start
  6.1 1.6 %collective-permute-start.1 = (f32[128,128]{1,0:T(8,128)S(1)}, f32[128,128]{1,0:T(8,128)S(1)}, u32[]{:S(2)}, u32[]{:S(2)}) collective-permute-start(f32[128,128]{1,0:T(8,128)S(1)} %bitcast.9), channel_id=1, source_target_pairs={{4,0},{8,4},{12,8},{14,12},{10,14},{6,10},{2,6},{0,2},{5,1},{9,5},... | collective-permute-start | bytes 196616 | tf_op jit(solution)/shard_map/ppermute | solution.py:347
  7.7 0.0 copy-done.4
  7.7 0.1 tile.9
  7.8 0.1 tile.11
  7.8 2.8 %collective-permute-done.3.refs_4_ = f32[400,128]{1,0:T(8,128)S(1)} collective-permute-done((f32[400,128]{1,0:T(8,128)S(1)}, f32[400,128]{1,0:T(8,128)S(1)}, u32[]{:S(2)}, u32[]{:S(2)}) %collective-permute-start.3) | collective-permute-done | bytes 204832 | tf_op jit(solution)/shard_map/ppermute | solution.py:345
  10.6 0.4 collective-permute-start.8
  11.1 0.0 collective-permute-done.4.refs_5_
  11.1 1.6 %collective-permute-start.9 = (f32[400,128]{1,0:T(8,128)S(1)}, f32[400,128]{1,0:T(8,128)S(1)}, u32[]{:S(2)}, u32[]{:S(2)}) collective-permute-start(f32[400,128]{1,0:T(8,128)S(1)} %collective-permute-done.4.refs_5_), channel_id=1, source_target_pairs={{4,0},{8,4},{12,8},{14,12},{10,14},{6,10},{2,6},{0,2},{5,1},{9,5},... | collective-permute-start | bytes 614408 | tf_op jit(solution)/shard_map/ppermute | solution.py:345
  12.7 0.0 collective-permute-done.refs_4_
  12.7 0.5 collective-permute-start.6
  13.3 1.6 %collective-permute-start.5 = (f32[512,128]{1,0:T(8,128)S(1)}, f32[512,128]{1,0:T(8,128)S(1)}, u32[]{:S(2)}, u32[]{:S(2)}) collective-permute-start(f32[512,128]{1,0:T(8,128)S(1)} %pad_maximum_fusion), channel_id=1, source_target_pairs={{0,16},{16,0},{1,17},{17,1},{2,18},{18,2},{3,19},{19,3},{4,20},{20... | collective-permute-start | bytes 786440 | tf_op jit(solution)/shard_map/ppermute | solution.py:324
  14.9 2.8 %collective-permute-done.8.refs_6_ = f32[400,128]{1,0:T(8,128)S(1)} collective-permute-done((f32[400,128]{1,0:T(8,128)S(1)}, f32[400,128]{1,0:T(8,128)S(1)}, u32[]{:S(2)}, u32[]{:S(2)}) %collective-permute-start.8) | collective-permute-done | bytes 204832 | tf_op jit(solution)/shard_map/ppermute | solution.py:345
  17.6 0.4 collective-permute-start.13
  18.1 0.0 collective-permute-done.9.refs_7_
  18.1 1.6 %collective-permute-start.14 = (f32[400,128]{1,0:T(8,128)S(1)}, f32[400,128]{1,0:T(8,128)S(1)}, u32[]{:S(2)}, u32[]{:S(2)}) collective-permute-start(f32[400,128]{1,0:T(8,128)S(1)} %collective-permute-done.9.refs_7_), channel_id=1, source_target_pairs={{4,0},{8,4},{12,8},{14,12},{10,14},{6,10},{2,6},{0,2},{5,1},{9,5},... | collective-permute-start | bytes 614408 | tf_op jit(solution)/shard_map/ppermute | solution.py:345
  19.7 0.2 fusion
  19.9 0.0 collective-permute-done.1.refs_5_
  19.9 1.6 %collective-permute-start.7 = (f32[128,128]{1,0:T(8,128)S(1)}, f32[128,128]{1,0:T(8,128)S(1)}, u32[]{:S(2)}, u32[]{:S(2)}) collective-permute-start(f32[128,128]{1,0:T(8,128)S(1)} %collective-permute-done.1.refs_5_), channel_id=1, source_target_pairs={{4,0},{8,4},{12,8},{14,12},{10,14},{6,10},{2,6},{0,2},{5,1},{9,5},... | collective-permute-start | bytes 196616 | tf_op jit(solution)/shard_map/ppermute | solution.py:347
  21.5 0.0 collective-permute-done.6.refs_7_
  21.5 0.4 collective-permute-start.11
  22.0 0.0 collective-permute-done.5.refs_6_
  22.0 1.6 %collective-permute-start.10 = (f32[512,128]{1,0:T(8,128)S(1)}, f32[512,128]{1,0:T(8,128)S(1)}, u32[]{:S(2)}, u32[]{:S(2)}) collective-permute-start(f32[512,128]{1,0:T(8,128)S(1)} %pad_maximum_fusion.1), channel_id=1, source_target_pairs={{0,16},{16,0},{1,17},{17,1},{2,18},{18,2},{3,19},{19,3},{4,20},{20... | collective-permute-start | bytes 786440 | tf_op jit(solution)/shard_map/ppermute | solution.py:324
  23.6 0.2 collective-permute-done.13.refs_8_
  23.8 0.0 copy-start
  23.8 0.8 %collective-permute-done.14.refs_9_ = f32[400,128]{1,0:T(8,128)S(1)} collective-permute-done((f32[400,128]{1,0:T(8,128)S(1)}, f32[400,128]{1,0:T(8,128)S(1)}, u32[]{:S(2)}, u32[]{:S(2)}) %collective-permute-start.14) | collective-permute-done | bytes 204832 | tf_op jit(solution)/shard_map/ppermute | solution.py:345
  24.6 1.6 %collective-permute-start.18 = (f32[208,128]{1,0:T(8,128)S(1)}, f32[208,128]{1,0:T(8,128)S(1)}, u32[]{:S(2)}, u32[]{:S(2)}) collective-permute-start(f32[208,128]{1,0:T(8,128)S(1)} %slice.46), channel_id=1, source_target_pairs={{4,0},{8,4},{12,8},{14,12},{10,14},{6,10},{2,6},{0,2},{5,1},{9,5},... | collective-permute-start | bytes 319496 | tf_op jit(solution)/shard_map/ppermute | solution.py:359
  26.3 0.5 collective-permute-start.17
  26.8 0.0 copy-done
  26.8 0.0 slice-start
  26.8 0.9 %slice-done = f32[256,128]{1,0:T(8,128)S(1)} async-done(((f32[400,128]{1,0:T(8,128)}), f32[256,128]{1,0:T(8,128)S(1)}, s32[]{:S(2)}) %slice-start) | async-done | bytes 131096 | tf_op jit(solution)/shard_map/slice | solution.py:348
  27.7 3.2 %collective-permute-done.17.refs_10_ = f32[192,128]{1,0:T(8,128)S(1)} collective-permute-done((f32[192,128]{1,0:T(8,128)S(1)}, f32[192,128]{1,0:T(8,128)S(1)}, u32[]{:S(2)}, u32[]{:S(2)}) %collective-permute-start.17) | collective-permute-done | bytes 98336 | tf_op jit(solution)/shard_map/ppermute | solution.py:359
  30.9 1.5 %collective-permute-start.15 = (f32[512,128]{1,0:T(8,128)S(1)}, f32[512,128]{1,0:T(8,128)S(1)}, u32[]{:S(2)}, u32[]{:S(2)}) collective-permute-start(f32[512,128]{1,0:T(8,128)S(1)} %pad_maximum_fusion.2), channel_id=1, source_target_pairs={{0,16},{16,0},{1,17},{17,1},{2,18},{18,2},{3,19},{19,3},{4,20},{20... | collective-permute-start | bytes 786440 | tf_op jit(solution)/shard_map/ppermute | solution.py:324
  32.5 0.0 copy-start.1
  32.5 0.0 collective-permute-done.18.refs_11_
  32.5 0.6 collective-permute-start.19
  33.1 0.1 pad_add_fusion.1.refs_0_
  33.1 0.0 collective-permute-done.7.refs_8_
  33.1 1.6 %collective-permute-start.12 = (f32[128,128]{1,0:T(8,128)S(1)}, f32[128,128]{1,0:T(8,128)S(1)}, u32[]{:S(2)}, u32[]{:S(2)}) collective-permute-start(f32[128,128]{1,0:T(8,128)S(1)} %collective-permute-done.7.refs_8_), channel_id=1, source_target_pairs={{4,0},{8,4},{12,8},{14,12},{10,14},{6,10},{2,6},{0,2},{5,1},{9,5},... | collective-permute-start | bytes 196616 | tf_op jit(solution)/shard_map/ppermute | solution.py:347
  34.7 0.0 collective-permute-done.11.refs_10_
  34.7 0.4 collective-permute-start.16
  35.2 0.1 pad_add_fusion.refs_0_
  35.3 0.0 collective-permute-done.10.refs_9_
  35.3 0.0 copy-start.2
  35.3 0.0 copy-start.3
  35.3 0.0 copy-done.1
  35.3 0.6 %copy-done.2 = s32[8]{0:T(128)S(1)} copy-done((s32[8]{0:T(128)S(1)}, s32[8]{0:T(128)}, u32[]{:S(2)}) %copy-start.2) | copy-done | bytes 56
  35.9 0.0 copy-done.3
  35.9 12.2 %shard_map.68 = (f32[2,3,1,128,128]{4,3,2,1,0:T(8,128)}, f32[2,6,1,128,128]{4,3,2,1,0:T(8,128)}, f32[8,24,128]{2,1,0:T(8,128)S(1)}) custom-call(s32[2]{0:T(128)S(1)} %pad_add_fusion.1.refs_0_, s32[8]{0:T(128)S(1)} %copy-done.2, s32[6]{0:T(128)S(1)} %copy-done.3, f32[400,128]{1,0:T(8,128)S(1)} %maximum_maximum_fusion.refs_3_, ...), custom_call_target="tpu_custom_call" | custom-call | flops 30000000 | bytes 5000000 | tf_op jit(solution)/shard_map/pallas_call | solution.py:290
  48.2 0.0 collective-permute-done.12.refs_11_
  48.2 0.0 collective-permute-done.16.refs_13_
  48.2 0.0 collective-permute-done.19.refs_14_
  48.2 0.0 collective-permute-done.15.refs_12_
  48.2 12.1 %shard_map.69 = (f32[2,3,1,128,128]{4,3,2,1,0:T(8,128)}, f32[2,6,1,128,128]{4,3,2,1,0:T(8,128)}) custom-call(s32[2]{0:T(128)S(1)} %pad_add_fusion.refs_0_, s32[8]{0:T(128)S(1)} %copy-done.2, s32[6]{0:T(128)S(1)} %copy-done.3, f32[384,128]{1,0:T(8,128)S(1)} %bitcast.6, ...), custom_call_target="tpu_custom_call", output_to_operand_aliasing={{0}: (18, {}), {1}: (19, {})} | custom-call | flops 30000000 | bytes 5000000 | tf_op jit(solution)/shard_map/pallas_call | solution.py:290
  (18 shorter events, 0.2 us)
Async XLA Ops:
  1.3 1.2 %collective-permute-start.2 = (f32[6,128]{1,0:T(8,128)S(1)}, f32[6,128]{1,0:T(8,128)S(1)}, u32[]{:S(2)}, u32[]{:S(2)}) collective-permute-start(f32[6,128]{1,0:T(8,128)S(1)} %reshape_squeeze.3), channel_id=1, source_target_pairs={{0,1},{1,0},{2,3},{3,2},{4,5},{5,4},{6,7},{7,6},{8,9},{9,8},{10,11... | collective-permute-start | bytes 9224 | tf_op jit(solution)/shard_map/ppermute | solution.py:327
  2.7 7.9 %collective-permute-start.3 = (f32[400,128]{1,0:T(8,128)S(1)}, f32[400,128]{1,0:T(8,128)S(1)}, u32[]{:S(2)}, u32[]{:S(2)}) collective-permute-start(f32[400,128]{1,0:T(8,128)S(1)} %maximum_maximum_fusion.refs_3_), channel_id=1, source_target_pairs={{0,4},{4,8},{8,12},{12,14},{14,10},{10,6},{6,2},{2,0},{1,5},{5,9},... | collective-permute-start | bytes 614408 | tf_op jit(solution)/shard_map/ppermute | solution.py:345
  3.2 7.9 %collective-permute-start.4 = (f32[400,128]{1,0:T(8,128)S(1)}, f32[400,128]{1,0:T(8,128)S(1)}, u32[]{:S(2)}, u32[]{:S(2)}) collective-permute-start(f32[400,128]{1,0:T(8,128)S(1)} %maximum_maximum_fusion.refs_3_), channel_id=1, source_target_pairs={{4,0},{8,4},{12,8},{14,12},{10,14},{6,10},{2,6},{0,2},{5,1},{9,5},... | collective-permute-start | bytes 614408 | tf_op jit(solution)/shard_map/ppermute | solution.py:345
  5.6 2.0 %copy-start.4 = (s32[256]{0:T(256)S(1)}, s32[256]{0:T(256)}, u32[]{:S(2)}) copy-start(s32[256]{0:T(256)} %param.7) | copy-start | bytes 3076
  5.6 7.1 %collective-permute-start = (f32[128,128]{1,0:T(8,128)S(1)}, f32[128,128]{1,0:T(8,128)S(1)}, u32[]{:S(2)}, u32[]{:S(2)}) collective-permute-start(f32[128,128]{1,0:T(8,128)S(1)} %bitcast.8), channel_id=1, source_target_pairs={{0,4},{4,8},{8,12},{12,14},{14,10},{10,6},{6,2},{2,0},{1,5},{5,9},... | collective-permute-start | bytes 196616 | tf_op jit(solution)/shard_map/ppermute | solution.py:346
  6.1 13.8 %collective-permute-start.1 = (f32[128,128]{1,0:T(8,128)S(1)}, f32[128,128]{1,0:T(8,128)S(1)}, u32[]{:S(2)}, u32[]{:S(2)}) collective-permute-start(f32[128,128]{1,0:T(8,128)S(1)} %bitcast.9), channel_id=1, source_target_pairs={{4,0},{8,4},{12,8},{14,12},{10,14},{6,10},{2,6},{0,2},{5,1},{9,5},... | collective-permute-start | bytes 196616 | tf_op jit(solution)/shard_map/ppermute | solution.py:347
  10.6 7.0 %collective-permute-start.8 = (f32[400,128]{1,0:T(8,128)S(1)}, f32[400,128]{1,0:T(8,128)S(1)}, u32[]{:S(2)}, u32[]{:S(2)}) collective-permute-start(f32[400,128]{1,0:T(8,128)S(1)} %collective-permute-done.3.refs_4_), channel_id=1, source_target_pairs={{0,4},{4,8},{8,12},{12,14},{14,10},{10,6},{6,2},{2,0},{1,5},{5,9},... | collective-permute-start | bytes 614408 | tf_op jit(solution)/shard_map/ppermute | solution.py:345
  11.1 7.0 %collective-permute-start.9 = (f32[400,128]{1,0:T(8,128)S(1)}, f32[400,128]{1,0:T(8,128)S(1)}, u32[]{:S(2)}, u32[]{:S(2)}) collective-permute-start(f32[400,128]{1,0:T(8,128)S(1)} %collective-permute-done.4.refs_5_), channel_id=1, source_target_pairs={{4,0},{8,4},{12,8},{14,12},{10,14},{6,10},{2,6},{0,2},{5,1},{9,5},... | collective-permute-start | bytes 614408 | tf_op jit(solution)/shard_map/ppermute | solution.py:345
  12.7 8.8 %collective-permute-start.6 = (f32[128,128]{1,0:T(8,128)S(1)}, f32[128,128]{1,0:T(8,128)S(1)}, u32[]{:S(2)}, u32[]{:S(2)}) collective-permute-start(f32[128,128]{1,0:T(8,128)S(1)} %collective-permute-done.refs_4_), channel_id=1, source_target_pairs={{0,4},{4,8},{8,12},{12,14},{14,10},{10,6},{6,2},{2,0},{1,5},{5,9},... | collective-permute-start | bytes 196616 | tf_op jit(solution)/shard_map/ppermute | solution.py:346
  13.3 8.8 %collective-permute-start.5 = (f32[512,128]{1,0:T(8,128)S(1)}, f32[512,128]{1,0:T(8,128)S(1)}, u32[]{:S(2)}, u32[]{:S(2)}) collective-permute-start(f32[512,128]{1,0:T(8,128)S(1)} %pad_maximum_fusion), channel_id=1, source_target_pairs={{0,16},{16,0},{1,17},{17,1},{2,18},{18,2},{3,19},{19,3},{4,20},{20... | collective-permute-start | bytes 786440 | tf_op jit(solution)/shard_map/ppermute | solution.py:324
  17.6 6.2 %collective-permute-start.13 = (f32[400,128]{1,0:T(8,128)S(1)}, f32[400,128]{1,0:T(8,128)S(1)}, u32[]{:S(2)}, u32[]{:S(2)}) collective-permute-start(f32[400,128]{1,0:T(8,128)S(1)} %collective-permute-done.8.refs_6_), channel_id=1, source_target_pairs={{0,4},{4,8},{8,12},{12,14},{14,10},{10,6},{6,2},{2,0},{1,5},{5,9},... | collective-permute-start | bytes 614408 | tf_op jit(solution)/shard_map/ppermute | solution.py:345
  18.1 6.5 %collective-permute-start.14 = (f32[400,128]{1,0:T(8,128)S(1)}, f32[400,128]{1,0:T(8,128)S(1)}, u32[]{:S(2)}, u32[]{:S(2)}) collective-permute-start(f32[400,128]{1,0:T(8,128)S(1)} %collective-permute-done.9.refs_7_), channel_id=1, source_target_pairs={{4,0},{8,4},{12,8},{14,12},{10,14},{6,10},{2,6},{0,2},{5,1},{9,5},... | collective-permute-start | bytes 614408 | tf_op jit(solution)/shard_map/ppermute | solution.py:345
  19.9 13.3 %collective-permute-start.7 = (f32[128,128]{1,0:T(8,128)S(1)}, f32[128,128]{1,0:T(8,128)S(1)}, u32[]{:S(2)}, u32[]{:S(2)}) collective-permute-start(f32[128,128]{1,0:T(8,128)S(1)} %collective-permute-done.1.refs_5_), channel_id=1, source_target_pairs={{4,0},{8,4},{12,8},{14,12},{10,14},{6,10},{2,6},{0,2},{5,1},{9,5},... | collective-permute-start | bytes 196616 | tf_op jit(solution)/shard_map/ppermute | solution.py:347
  21.5 13.2 %collective-permute-start.11 = (f32[128,128]{1,0:T(8,128)S(1)}, f32[128,128]{1,0:T(8,128)S(1)}, u32[]{:S(2)}, u32[]{:S(2)}) collective-permute-start(f32[128,128]{1,0:T(8,128)S(1)} %collective-permute-done.6.refs_7_), channel_id=1, source_target_pairs={{0,4},{4,8},{8,12},{12,14},{14,10},{10,6},{6,2},{2,0},{1,5},{5,9},... | collective-permute-start | bytes 196616 | tf_op jit(solution)/shard_map/ppermute | solution.py:346
  22.0 13.2 %collective-permute-start.10 = (f32[512,128]{1,0:T(8,128)S(1)}, f32[512,128]{1,0:T(8,128)S(1)}, u32[]{:S(2)}, u32[]{:S(2)}) collective-permute-start(f32[512,128]{1,0:T(8,128)S(1)} %pad_maximum_fusion.1), channel_id=1, source_target_pairs={{0,16},{16,0},{1,17},{17,1},{2,18},{18,2},{3,19},{19,3},{4,20},{20... | collective-permute-start | bytes 786440 | tf_op jit(solution)/shard_map/ppermute | solution.py:324
  23.8 2.9 %copy-start = (f32[400,128]{1,0:T(8,128)}, f32[400,128]{1,0:T(8,128)S(1)}, u32[]{:S(2)}) copy-start(f32[400,128]{1,0:T(8,128)S(1)} %collective-permute-done.13.refs_8_) | copy-start | bytes 614404
  24.6 7.8 %collective-permute-start.18 = (f32[208,128]{1,0:T(8,128)S(1)}, f32[208,128]{1,0:T(8,128)S(1)}, u32[]{:S(2)}, u32[]{:S(2)}) collective-permute-start(f32[208,128]{1,0:T(8,128)S(1)} %slice.46), channel_id=1, source_target_pairs={{4,0},{8,4},{12,8},{14,12},{10,14},{6,10},{2,6},{0,2},{5,1},{9,5},... | collective-permute-start | bytes 319496 | tf_op jit(solution)/shard_map/ppermute | solution.py:359
  26.3 4.7 %collective-permute-start.17 = (f32[192,128]{1,0:T(8,128)S(1)}, f32[192,128]{1,0:T(8,128)S(1)}, u32[]{:S(2)}, u32[]{:S(2)}) collective-permute-start(f32[192,128]{1,0:T(8,128)S(1)} %slice.44), channel_id=1, source_target_pairs={{0,4},{4,8},{8,12},{12,14},{14,10},{10,6},{6,2},{2,0},{1,5},{5,9},... | collective-permute-start | bytes 294920 | tf_op jit(solution)/shard_map/ppermute | solution.py:359
  26.8 0.9 %slice-start = ((f32[400,128]{1,0:T(8,128)}), f32[256,128]{1,0:T(8,128)S(1)}, s32[]{:S(2)}) async-start(f32[400,128]{1,0:T(8,128)} %copy-done), calls=%async_computation | async-start | bytes 262144 | tf_op jit(solution)/shard_map/slice | solution.py:348
  30.9 17.3 %collective-permute-start.15 = (f32[512,128]{1,0:T(8,128)S(1)}, f32[512,128]{1,0:T(8,128)S(1)}, u32[]{:S(2)}, u32[]{:S(2)}) collective-permute-start(f32[512,128]{1,0:T(8,128)S(1)} %pad_maximum_fusion.2), channel_id=1, source_target_pairs={{0,16},{16,0},{1,17},{17,1},{2,18},{18,2},{3,19},{19,3},{4,20},{20... | collective-permute-start | bytes 786440 | tf_op jit(solution)/shard_map/ppermute | solution.py:324
  32.5 2.8 %copy-start.1 = (f32[400,128]{1,0:T(8,128)S(1)}, f32[400,128]{1,0:T(8,128)}, u32[]{:S(2)}) copy-start(f32[400,128]{1,0:T(8,128)} %copy-done) | copy-start | bytes 614404
  32.5 15.7 %collective-permute-start.19 = (f32[256,128]{1,0:T(8,128)S(1)}, f32[256,128]{1,0:T(8,128)S(1)}, u32[]{:S(2)}, u32[]{:S(2)}) collective-permute-start(f32[256,128]{1,0:T(8,128)S(1)} %pad_maximum_fusion.3), channel_id=1, source_target_pairs={{0,16},{16,0},{1,17},{17,1},{2,18},{18,2},{3,19},{19,3},{4,20},{20... | collective-permute-start | bytes 393224 | tf_op jit(solution)/shard_map/ppermute | solution.py:324
  33.1 15.0 %collective-permute-start.12 = (f32[128,128]{1,0:T(8,128)S(1)}, f32[128,128]{1,0:T(8,128)S(1)}, u32[]{:S(2)}, u32[]{:S(2)}) collective-permute-start(f32[128,128]{1,0:T(8,128)S(1)} %collective-permute-done.7.refs_8_), channel_id=1, source_target_pairs={{4,0},{8,4},{12,8},{14,12},{10,14},{6,10},{2,6},{0,2},{5,1},{9,5},... | collective-permute-start | bytes 196616 | tf_op jit(solution)/shard_map/ppermute | solution.py:347
  34.7 13.5 %collective-permute-start.16 = (f32[128,128]{1,0:T(8,128)S(1)}, f32[128,128]{1,0:T(8,128)S(1)}, u32[]{:S(2)}, u32[]{:S(2)}) collective-permute-start(f32[128,128]{1,0:T(8,128)S(1)} %collective-permute-done.11.refs_10_), channel_id=1, source_target_pairs={{0,4},{4,8},{8,12},{12,14},{14,10},{10,6},{6,2},{2,0},{1,5},{5,9},... | collective-permute-start | bytes 196616 | tf_op jit(solution)/shard_map/ppermute | solution.py:363
  35.3 0.7 %copy-start.2 = (s32[8]{0:T(128)S(1)}, s32[8]{0:T(128)}, u32[]{:S(2)}) copy-start(s32[8]{0:T(128)} %refs_1_.3) | copy-start | bytes 100
  35.3 0.7 %copy-start.3 = (s32[6]{0:T(128)S(1)}, s32[6]{0:T(128)}, u32[]{:S(2)}) copy-start(s32[6]{0:T(128)} %refs_2_.3) | copy-start | bytes 76

commit v2 on v1

--- a/solution.py
+++ b/solution.py
@@ -12,6 +12,7 @@
 VX, VY, VZ, XX, YY, ZZ, XY, XZ, YZ = range(9)
 ROWS = 8
 LINES = 24
+GROUP = 4
 
 
 def ring_place(box, count):
@@ -41,8 +42,8 @@
 
 
 class Plane:
-    def __init__(self, fields, index, cells_y, cells_z):
-        self.fields, self.index, self.chunks = fields, index, cells_y // ROWS
+    def __init__(self, sources, cells_y, cells_z):
+        self.sources, self.chunks = sources, cells_y // ROWS
         row = lax.broadcasted_iota(jnp.int32, (ROWS, cells_z), 0)
         lane = lax.broadcasted_iota(jnp.int32, (ROWS, cells_z), 1)
         self.first_row, self.last_row = row == 0, row == ROWS - 1
@@ -50,15 +51,17 @@
         self.cells_z = cells_z
         self.loaded, self.rolled = {}, {}
 
-    def at(self, field, chunk, beside=0):
-        if (field, chunk, beside) not in self.loaded:
-            self.loaded[field, chunk, beside] = self.fields[field][
-                self.index + beside, chunk * ROWS : chunk * ROWS + ROWS, :
-            ]
-        return self.loaded[field, chunk, beside]
-
-    def put(self, field, chunk, value):
-        self.fields[field][self.index, chunk * ROWS : chunk * ROWS + ROWS, :] = value
+    def fetch(self, chunk):
+        if chunk < self.chunks:
+            for name, (array, lead) in self.sources.items():
+                self.loaded[name, chunk] = array[lead + (slice(chunk * ROWS, chunk * ROWS + ROWS),)]
+
+    def at(self, name, chunk, beside=0):
+        return self.loaded[(name, beside) if beside else name, chunk]
+
+    def put(self, name, chunk, value):
+        array, lead = self.sources[name]
+        array[lead + (slice(chunk * ROWS, chunk * ROWS + ROWS),)] = value
 
     def roll_rows(self, field, chunk, by):
         if not 0 <= chunk < self.chunks:
@@ -95,10 +98,10 @@
 def propagate(plan, *refs):
     parts, row_parts, ring, planes, cells_y, cells_z, per, first = plan
     refs = list(refs)
-    place_ref, map_ref, owners_ref = refs[:3]
+    scalars = refs[0]
     operands = 1 + max(part[0] for part in parts)
-    piece_refs = refs[3 : 3 + operands]
-    rest = refs[3 + operands :]
+    piece_refs = refs[1 : 1 + operands]
+    rest = refs[1 + operands :]
     hot_y, hot_z = rest[:2]
     rest = rest[2:]
     if ring == 1 or not first:
@@ -118,12 +121,12 @@
     chunks = cells_y // ROWS
 
     if ring > 1:
-        centre = place_ref[0]
+        centre = scalars[0]
         start = ring_place(centre, ring)
         boxes = {
             step: ring_box(lax.rem(start + step + ring, ring), ring) for step in ring_offsets(ring)
         }
-        blocks = {step: map_ref[box] for step, box in boxes.items()}
+        blocks = {step: scalars[2 + box] for step, box in boxes.items()}
     else:
         centre = planes // 2
         blocks = {0: 0}
@@ -147,7 +150,7 @@
         for operand, row, offset in row_parts:
             stored[boxes[offset]] = piece_refs[operand][row : row + 2 * ROWS, :]
         for step in range(STEPS):
-            owner = owners_ref[step]
+            owner = scalars[2 + ring + step]
             for comp in range(3):
                 for half in range(halves):
                     source = (owner % 2) * 3 * halves + comp * halves + half
@@ -167,32 +170,40 @@
         for plane in range(planes):
             values[plane] = split_values(given_ref[plane], per)
 
-    def inject(step, plane):
-        spots = hot_y[plane]
+    def inject(step, plane, begin, size):
+        spots = hot_y[plane, begin : begin + size]
         rows = [values[plane, pl.ds(step * 3 + comp, 1), :] for comp in range(3)]
         weighted = jnp.concatenate([(spots * row).astype(jnp.bfloat16) for row in rows], axis=0)
         found = jnp.dot(weighted, hot_z[plane], preferred_element_type=jnp.float32)
-        return [found[comp * cells_y : comp * cells_y + cells_y] for comp in range(3)]
+        return [found[comp * size : comp * size + size] for comp in range(3)]
 
     def limits(step):
         reach = STEPS - 1 - step
         return jnp.maximum(centre - reach, 0), jnp.minimum(centre + reach, planes - 1)
 
-    def medium_at(component, plane, chunk):
-        return medium[component, plane, chunk * ROWS : chunk * ROWS + ROWS, :]
-
-    def added_at(comp, plane, chunk):
-        return added[comp, plane, chunk * ROWS : chunk * ROWS + ROWS, :]
-
-    def start_velocity(plane, carry):
-        for comp, value in enumerate(inject(0, plane)):
-            fields[comp][plane + 1] = value
-        return carry
+    def beside(field, index, step=0):
+        return fields[field], (index + step,)
 
     def velocity(components, plane, carry):
-        here = Plane(fields, plane + 1, cells_y, cells_z)
+        index = plane + 1
+        sources = {"gain": (medium, (2, plane))}
+        for field in components:
+            sources[field] = beside(field, index)
+            sources["added", field] = (added, (field, plane))
+        if VX in components:
+            sources.update({XX: beside(XX, index), (XX, 1): beside(XX, index, 1)})
+        if VY in components:
+            sources.update({(XY, -1): beside(XY, index, -1), YY: beside(YY, index)})
+        if VZ in components:
+            sources.update({(XZ, -1): beside(XZ, index, -1), ZZ: beside(ZZ, index)})
+        if VY in components or VZ in components:
+            sources[YZ] = beside(YZ, index)
+        sources.update({XY: beside(XY, index), XZ: beside(XZ, index)})
+        here = Plane(sources, cells_y, cells_z)
+        here.fetch(0)
         for chunk in range(chunks):
-            gain = medium_at(2, plane, chunk)
+            here.fetch(chunk + 1)
+            gain = here.at("gain", chunk)
             pulls = []
             if VX in components:
                 pull = here.fore_x(XX, chunk) + here.back_y(XY, chunk) + here.back_z(XZ, chunk)
@@ -203,18 +214,29 @@
             if VZ in components:
                 pull = here.back_x(XZ, chunk) + here.back_y(YZ, chunk) + here.fore_z(ZZ, chunk)
                 pulls.append((VZ, pull))
-            for comp, pull in pulls:
-                new = here.at(comp, chunk) + gain * pull
-                here.put(comp, chunk, new + added_at(comp, plane, chunk))
+            news = [
+                (comp, here.at(comp, chunk) + gain * pull + here.at(("added", comp), chunk))
+                for comp, pull in pulls
+            ]
+            for comp, new in news:
+                here.put(comp, chunk, new)
         return carry
 
     def stress(step, fresh, final, plane, carry):
-        here = Plane(fields, plane + 1, cells_y, cells_z)
-        if not final:
-            for comp, value in enumerate(inject(step + 1, plane)):
-                added[comp, plane] = value
+        index = plane + 1
+        sources = {"lam": (medium, (0, plane)), "mu": (medium, (1, plane))}
+        sources.update({field: beside(field, index) for field in range(3 if fresh else 9)})
+        sources.update({(field, by): beside(field, index, by) for field, by in ((VX, -1), (VY, 1), (VZ, 1))})
+        if fresh:
+            targets = Plane({field: beside(field, index) for field in range(3, 9)}, cells_y, cells_z)
+        here = Plane(sources, cells_y, cells_z)
+        here.fetch(0)
         for chunk in range(chunks):
-            lam, mu = medium_at(0, plane, chunk), medium_at(1, plane, chunk)
+            if not final and chunk % GROUP == 0:
+                begin = chunk * ROWS
+                found = inject(step + 1, plane, begin, GROUP * ROWS)
+            here.fetch(chunk + 1)
+            lam, mu = here.at("lam", chunk), here.at("mu", chunk)
             twice = mu + mu
             grad_x, grad_y, grad_z = here.back_x(VX, chunk), here.back_y(VY, chunk), here.back_z(VZ, chunk)
             spread = lam * (grad_x + grad_y + grad_z)
@@ -226,8 +248,16 @@
                 (XZ, mu * (here.fore_z(VX, chunk) + here.fore_x(VZ, chunk))),
                 (YZ, mu * (here.fore_z(VY, chunk) + here.fore_y(VZ, chunk))),
             )
-            for field, change in changes:
-                here.put(field, chunk, change if fresh else here.at(field, chunk) + change)
+            if fresh:
+                for field, change in changes:
+                    targets.put(field, chunk, change)
+            else:
+                news = [(field, here.at(field, chunk) + change) for field, change in changes]
+                for field, new in news:
+                    here.put(field, chunk, new)
+            if not final and chunk % GROUP == GROUP - 1:
+                for comp, value in enumerate(found):
+                    added[comp, plane, begin : begin + GROUP * ROWS] = value
         return carry
 
     def velocities(step):
@@ -236,8 +266,10 @@
         lax.fori_loop(low, high + 1, functools.partial(velocity, (VX, VY, VZ)), 0)
         lax.fori_loop(high + 1, jnp.minimum(high + 2, planes), functools.partial(velocity, (VY, VZ)), 0)
 
+    for plane in range(planes):
+        for comp, value in enumerate(inject(0, plane, 0, cells_y)):
+            fields[comp][plane + 1] = value
     low, high = limits(0)
-    lax.fori_loop(jnp.maximum(low - 1, 0), jnp.minimum(high + 2, planes), start_velocity, 0)
     lax.fori_loop(low, high + 1, functools.partial(stress, 0, True, False), 0)
 
     def one_step(step, carry):
@@ -247,15 +279,16 @@
         return carry
 
     lax.fori_loop(1, STEPS - 1, one_step, 0)
-    velocities(STEPS - 1)
-    stress(STEPS - 1, False, True, centre, 0)
-
-    trial = place_ref[1]
+    trial = scalars[1]
     copies = []
     for field in range(9):
         target = vel_ref.at[trial, field, 0] if field < 3 else str_ref.at[trial, field - 3, 0]
         copies.append(pltpu.make_async_copy(fields[field].at[centre + 1], target, sems.at[field]))
-    for copy in copies:
+    velocities(STEPS - 1)
+    for copy in copies[:3]:
+        copy.start()
+    stress(STEPS - 1, False, True, centre, 0)
+    for copy in copies[3:]:
         copy.start()
     for copy in copies:
         copy.wait()
@@ -268,8 +301,8 @@
     smem, vmem, anywhere = (
         pl.BlockSpec(memory_space=space) for space in (pltpu.SMEM, pltpu.VMEM, pl.ANY)
     )
-    operands = list(scalars) + list(pieces) + list(hots)
-    specs = [smem] * 3 + [vmem] * (len(operands) - 3)
+    operands = [scalars] + list(pieces) + list(hots)
+    specs = [smem] + [vmem] * (len(operands) - 1)
     if given is not None:
         operands.append(given)
         specs.append(vmem)
@@ -301,8 +334,8 @@
             pltpu.VMEM((2, LINES, cells_z), jnp.float32),
             pltpu.SemaphoreType.DMA((9,)),
         ],
-        compiler_params=pltpu.CompilerParams(vmem_limit_bytes=40 * 1024 * 1024),
-        cost_estimate=pl.CostEstimate(flops=30_000_000, bytes_accessed=5_000_000, transcendentals=0),
+        compiler_params=pltpu.CompilerParams(vmem_limit_bytes=24 * 1024 * 1024),
+        cost_estimate=pl.CostEstimate(flops=1_000_000, bytes_accessed=100_000, transcendentals=0),
     )(*operands)
 
 
@@ -312,7 +345,7 @@
     return lax.ppermute(value, axis, [(source, source + steps) for source in range(leading, last)])
 
 
-def around(medium, store, count):
+def around(medium, store, early, count):
     lanes = medium.shape[-1]
     group = lax.axis_index("groups")
     order = [2 * place for place in range((count + 1) // 2)]
@@ -341,30 +374,35 @@
         pieces[which].append(piece)
 
     forth, back, forth_later, back_later, rests = first, first, later, later, []
+    lates = []
     for distance in range(1, count // 2):
+        if distance == 3:
+            forth, early = lax.optimization_barrier((forth, early))
         forth, back = lax.ppermute(forth, "box", up), lax.ppermute(back, "box", down)
-        forth_later = lax.ppermute(forth_later, "box", up)
-        back_later = lax.ppermute(back_later, "box", down)
-        rest = across(jnp.concatenate([forth[third:size], back[third:size]]))
-        rests.append(rest)
         for piece, offset in ((forth, -distance), (back, distance)):
             row_parts.append((len(pieces[0]), size, offset))
             keep(0, piece, [(0, 0, units, offset)])
-        for piece, offset in ((forth_later, -distance), (back_later, distance)):
-            keep(1, piece, [(0, 0, units // 3, offset)])
-        keep(1, rest, [(0, units // 3, units - units // 3, -distance),
-                       (size - third, units // 3, units - units // 3, distance)])
+        skip = 0
+        if distance < 3:
+            skip = third
+            forth_later = lax.ppermute(forth_later, "box", up)
+            back_later = lax.ppermute(back_later, "box", down)
+            lates.append((forth_later, back_later))
+            for piece, offset in ((forth_later, -distance), (back_later, distance)):
+                keep(1, piece, [(0, 0, units // 3, offset)])
+        left = units - skip * units // size
+        rest = across(jnp.concatenate([forth[skip:size], back[skip:size]]))
+        rests.append(rest)
+        keep(1, rest, [(0, units - left, left, -distance), (size - skip, units - left, left, distance)])
     far = count // 2
-    forth, back, _ = lax.optimization_barrier((forth, back, rests[0]))
+    forth, back, _ = lax.optimization_barrier((forth, back, (rests[:2], lates[0])))
     forth, back = lax.ppermute(forth[:half], "box", up), lax.ppermute(back[half:], "box", down)
     row_parts.append((len(pieces[0]) + 1, size - half, far))
     keep(0, forth, [(0, 0, units // 2, far)])
     keep(0, back, [(0, units // 2, units - units // 2, far)])
-    keep(1, lax.ppermute(forth_later, "box", up), [(0, 0, units // 3, far)])
-    rest = across(jnp.concatenate([forth[third:], back[: size - half]]))
-    pieces[0][-1], _ = lax.optimization_barrier((pieces[0][-1], rests[1]))
-    keep(1, rest, [(0, units // 3, units - units // 3, far)])
-    return (pieces[0], parts[0], row_parts), (pieces[1], parts[1], [])
+    rest = across(jnp.concatenate([forth, back[: size - half]]))
+    keep(1, rest, [(0, 0, units, far)])
+    return ((pieces[0], parts[0], row_parts), (pieces[1], parts[1], [])), early
 
 
 def hot_planes(offsets, cells_y, cells_z):
@@ -386,8 +424,12 @@
     pairs = lax.axis_size("trial") == 2 and lax.axis_size("groups") == 2 and trials_here == 2
     if pairs and boxes == 8 and all_planes == 8:
         ring, planes, given = boxes, all_planes, None
-        found = around(medium, store, boxes)
-        slots = [lax.axis_index("groups"), 1 - lax.axis_index("groups")]
+        group = lax.axis_index("groups")
+        hots = hot_planes(jnp.tile(offsets, (1, cells_z // per)), cells_y, cells_z)
+        scalars = [
+            jnp.concatenate([jnp.stack([place, slot]), brick_map, owners]) for slot in (group, 1 - group)
+        ]
+        found, (hots, scalars) = around(medium, store, (hots, scalars), boxes)
     else:
         inverse = jnp.zeros((boxes,), jnp.int32).at[brick_map].set(jnp.arange(boxes, dtype=jnp.int32))
         moved = lax.all_to_all(medium, "box", split_axis=2, concat_axis=3, tiled=True)
@@ -408,14 +450,12 @@
         given = jnp.tile(rows, (1, 1, cells_z // per))
         offsets = jnp.pad(offsets, ((reach, reach), (0, 0)), constant_values=-1)
         offsets = lax.dynamic_slice_in_dim(offsets, place, planes, 0)
-        slots = list(range(trials_here))
-    hots = hot_planes(jnp.tile(offsets, (1, cells_z // per)), cells_y, cells_z)
+        hots = hot_planes(jnp.tile(offsets, (1, cells_z // per)), cells_y, cells_z)
+        scalars = [jnp.stack([place, jnp.int32(trial)]) for trial in range(trials_here)]
     shape = (planes, cells_y, cells_z, per)
     before = None
     for trial in range(trials_here):
-        geometry = jnp.stack([place, jnp.int32(slots[trial])])
-        scalars = (geometry, brick_map, owners)
-        results = run_trial(trials_here, shape, ring, scalars, found[trial], hots, given, before)
+        results = run_trial(trials_here, shape, ring, scalars[trial], found[trial], hots, given, before)
         before = results[:2]
         if trial == 0:
             given = results[2]

time: 61.2 us -> 61.8 us (level)
  waiting for transfers between devices: 9.86 us -> 15 us
  Pallas kernels: 24.3 us -> 22.5 us
  starting transfers between devices: 20.2 us -> 18.4 us
    ppermute x3, waiting for transfers between devices: 5.8 us -> 8.95 us  [around(): lax.ppermute(forth, 'box', up)]
    ppermute x3 -> x2, waiting for transfers between devices: 0.01 us -> 2.22 us  [around(): back_later = lax.ppermute(back_later, 'box', down)]
    pallas_call x2, Pallas kernels: 24.3 us -> 22.5 us  [run_trial(): pl.pallas_call(functools.partial(propagate, (parts, row_parts, ring, plan...]
    ppermute x3 -> x2, starting transfers between devices: 4.78 us -> 3.15 us  [around(): back_later = lax.ppermute(back_later, 'box', down)]
    ppermute x1, waiting for transfers between devices: 3.24 us -> 2.22 us  [around(): lax.ppermute(forth[:half], 'box', up)]
    slice x9 -> x8, local copies, waits for them, and re-layouts: 0.95 us -> 0.07 us  [the longest x7 0.06 us: around(): rest = across(jnp.concatenate([forth[skip:size], back[skip:size]]))]
    ppermute x1, waiting for transfers between devices: 0.01 us -> 0.83 us  [around(): lax.ppermute(back[half:], 'box', down)]
    ppermute x4, starting transfers between devices: 5.26 us -> 5.98 us  [across(): return lax.ppermute(value, 'groups', [(0, 1), (1, 0)])]
  transfers between devices with their start and end apart: 20 -> 17, of which waited for: 5 -> 8; matrix products, arithmetic and copies ran while one was open for 4% -> 4% of each run, Pallas kernels for 20% -> 19%
where the time goes in v2:
time: 61.8 us; the launch traced here: 61.5 us
  Pallas kernels  22.5 us (36%)
  starting transfers between devices  18.4 us (30%)
  waiting for transfers between devices  15 us (24%)
  local copies, waits for them, and re-layouts  3.59 us (6%)
  other arithmetic  1.2 us (2%)
  between operations  0.84 us (1%)
    pallas_call x2, Pallas kernels, run_trial(): pl.pallas_call(functools.partial(propagate, (parts, row_parts, ring, plan...  22.5 us
    ppermute x3, waiting for transfers between devices, around(): lax.ppermute(forth, 'box', up)  8.95 us
    ppermute x4, starting transfers between devices, across(): return lax.ppermute(value, 'groups', [(0, 1), (1, 0)])  5.98 us
    ppermute x3, starting transfers between devices, around(): lax.ppermute(back, 'box', down)  4.73 us
    ppermute x2, starting transfers between devices, around(): back_later = lax.ppermute(back_later, 'box', down)  3.15 us
    ppermute x1, waiting for transfers between devices, around(): lax.ppermute(forth[:half], 'box', up)  2.22 us
    ppermute x2, waiting for transfers between devices, around(): back_later = lax.ppermute(back_later, 'box', down)  2.22 us
    ppermute x1, starting transfers between devices, around(): lax.ppermute(back[half:], 'box', down)  1.63 us
  transfers between devices with their start and end apart: 17, of which 8 were waited for; matrix products, arithmetic and copies ran while one was open for 4% of the time, Pallas kernels for 19%

profile of v2, /device:TPU:10, one launch (start us, length us, event | category | flops | bytes accessed | tf_op | source)
XLA Modules:
  0.0 61.5 jit_solution(10399141265156286636)
XLA Ops:
  0.6 0.7 %reduce = f32[3,256]{1,0:T(4,128)S(1)} reduce(f32[1,3,256]{2,0,1:T(1,128)} %param.6, f32[]{:T(128)} %constant.54), dimensions={0}, to_apply=%param.6.reduce_sub_computation | reduce | bytes 6148 | tf_op args[1]
  1.3 0.1 collective-permute-start
  1.4 0.0 copy-start.2
  1.4 0.7 %copy-done.2 = s32[256]{0:T(256)S(1)} copy-done((s32[256]{0:T(256)S(1)}, s32[256]{0:T(256)}, u32[]{:S(2)}) %copy-start.2) | copy-done | bytes 1048
  2.1 0.1 tile.9
  2.2 0.1 tile.11
  2.3 1.1 %constant_dynamic-slice_fusion.1 = (f32[1,3,8,16,128]{4,3,2,1,0:T(8,128)S(1)}, f32[1,3,8,16,128]{4,3,2,1,0:T(8,128)S(1)}) fusion(f32[2,3,8,16,128]{4,3,2,1,0:T(8,128)} %param.5, s32[]{:T(128)S(6)} %select_n.47, s32[]{:T(128)S(6)} %select_n.41), kind=kLoop, calls=%fused_computation.20 | loop fusion | bytes 786440 | tf_op jit(solution)/shard_map/jit(dynamic_index_in_dim)/dynamic_slice | solution.py:364
  3.4 0.1 pad.19.clone
  3.4 0.0 collective-permute-done
  3.5 0.1 maximum_maximum_fusion.refs_1_
  3.6 0.5 collective-permute-start.1
  4.1 1.6 %collective-permute-start.5 = (f32[400,128]{1,0:T(8,128)S(1)}, f32[400,128]{1,0:T(8,128)S(1)}, u32[]{:S(2)}, u32[]{:S(2)}) collective-permute-start(f32[400,128]{1,0:T(8,128)S(1)} %maximum_maximum_fusion.refs_1_), channel_id=1, source_target_pairs={{4,0},{8,4},{12,8},{14,12},{10,14},{6,10},{2,6},{0,2},{5,1},{9,5},... | collective-permute-start | bytes 614408 | tf_op jit(solution)/shard_map/ppermute | solution.py:381
  5.7 0.2 fusion
  5.9 5.2 %collective-permute-done.1.refs_2_ = f32[400,128]{1,0:T(8,128)S(1)} collective-permute-done((f32[400,128]{1,0:T(8,128)S(1)}, f32[400,128]{1,0:T(8,128)S(1)}, u32[]{:S(2)}, u32[]{:S(2)}) %collective-permute-start.1) | collective-permute-done | bytes 204832 | tf_op jit(solution)/shard_map/ppermute | solution.py:381
  11.1 0.4 collective-permute-start.2
  11.6 0.0 collective-permute-done.5.refs_3_
  11.6 1.6 %collective-permute-start.9 = (f32[400,128]{1,0:T(8,128)S(1)}, f32[400,128]{1,0:T(8,128)S(1)}, u32[]{:S(2)}, u32[]{:S(2)}) collective-permute-start(f32[400,128]{1,0:T(8,128)S(1)} %collective-permute-done.5.refs_3_), channel_id=1, source_target_pairs={{4,0},{8,4},{12,8},{14,12},{10,14},{6,10},{2,6},{0,2},{5,1},{9,5},... | collective-permute-start | bytes 614408 | tf_op jit(solution)/shard_map/ppermute | solution.py:381
  13.1 0.0 copy-start.3
  13.1 0.0 copy-start.4
  13.1 0.7 %copy-done.3 = s32[6]{0:T(128)S(1)} copy-done((s32[6]{0:T(128)S(1)}, s32[6]{0:T(128)}, u32[]{:S(2)}) %copy-start.3) | copy-done | bytes 48
  13.8 0.0 copy-done.4
  13.8 0.1 add_add_fusion.1
  13.9 1.6 %collective-permute-start.6 = (f32[512,128]{1,0:T(8,128)S(1)}, f32[512,128]{1,0:T(8,128)S(1)}, u32[]{:S(2)}, u32[]{:S(2)}) collective-permute-start(f32[512,128]{1,0:T(8,128)S(1)} %pad_maximum_fusion.1), channel_id=1, source_target_pairs={{0,16},{16,0},{1,17},{17,1},{2,18},{18,2},{3,19},{19,3},{4,20},{20... | collective-permute-start | bytes 786440 | tf_op jit(solution)/shard_map/ppermute | solution.py:357
  15.5 2.3 %collective-permute-done.2.refs_4_ = f32[400,128]{1,0:T(8,128)S(1)} collective-permute-done((f32[400,128]{1,0:T(8,128)S(1)}, f32[400,128]{1,0:T(8,128)S(1)}, u32[]{:S(2)}, u32[]{:S(2)}) %collective-permute-start.2) | collective-permute-done | bytes 204832 | tf_op jit(solution)/shard_map/ppermute | solution.py:381
  17.8 0.4 collective-permute-start.11
  18.2 0.0 collective-permute-done.9.refs_5_
  18.3 1.6 %collective-permute-start.10 = (f32[512,128]{1,0:T(8,128)S(1)}, f32[512,128]{1,0:T(8,128)S(1)}, u32[]{:S(2)}, u32[]{:S(2)}) collective-permute-start(f32[512,128]{1,0:T(8,128)S(1)} %pad_maximum_fusion.2), channel_id=1, source_target_pairs={{0,16},{16,0},{1,17},{17,1},{2,18},{18,2},{3,19},{19,3},{4,20},{20... | collective-permute-start | bytes 786440 | tf_op jit(solution)/shard_map/ppermute | solution.py:357
  19.9 1.6 %collective-permute-start.12 = (f32[400,128]{1,0:T(8,128)S(1)}, f32[400,128]{1,0:T(8,128)S(1)}, u32[]{:S(2)}, u32[]{:S(2)}) collective-permute-start(f32[400,128]{1,0:T(8,128)S(1)} %collective-permute-done.9.refs_5_), channel_id=1, source_target_pairs={{4,0},{8,4},{12,8},{14,12},{10,14},{6,10},{2,6},{0,2},{5,1},{9,5},... | collective-permute-start | bytes 614408 | tf_op jit(solution)/shard_map/ppermute | solution.py:381
  21.5 0.8 %constant_dynamic-slice_fusion = f32[1,1,8,16,128]{4,3,2,1,0:T(8,128)S(1)} fusion(f32[2,3,8,16,128]{4,3,2,1,0:T(8,128)} %param.5, s32[]{:T(128)S(6)} %select_n.47), kind=kLoop, calls=%fused_computation.19 | loop fusion | bytes 131076 | tf_op jit(solution)/shard_map/slice | solution.py:369
  22.3 0.4 collective-permute-start.3
  22.8 1.5 %collective-permute-done.11.refs_6_ = f32[400,128]{1,0:T(8,128)S(1)} collective-permute-done((f32[400,128]{1,0:T(8,128)S(1)}, f32[400,128]{1,0:T(8,128)S(1)}, u32[]{:S(2)}, u32[]{:S(2)}) %collective-permute-start.11) | collective-permute-done | bytes 204832 | tf_op jit(solution)/shard_map/ppermute | solution.py:381
  24.2 1.6 %collective-permute-start.4 = (f32[128,128]{1,0:T(8,128)S(1)}, f32[128,128]{1,0:T(8,128)S(1)}, u32[]{:S(2)}, u32[]{:S(2)}) collective-permute-start(f32[128,128]{1,0:T(8,128)S(1)} %bitcast.9), channel_id=1, source_target_pairs={{4,0},{8,4},{12,8},{14,12},{10,14},{6,10},{2,6},{0,2},{5,1},{9,5},... | collective-permute-start | bytes 196616 | tf_op jit(solution)/shard_map/ppermute | solution.py:389
  25.8 0.5 collective-permute-done.12.refs_7_
  26.4 0.0 copy-start
  26.4 0.2 collective-permute-done.3.refs_2_
  26.6 2.2 %collective-permute-done.4.refs_3_ = f32[128,128]{1,0:T(8,128)S(1)} collective-permute-done((f32[128,128]{1,0:T(8,128)S(1)}, f32[128,128]{1,0:T(8,128)S(1)}, u32[]{:S(2)}, u32[]{:S(2)}) %collective-permute-start.4) | collective-permute-done | bytes 65568 | tf_op jit(solution)/shard_map/ppermute | solution.py:389
  28.8 0.0 collective-permute-done.6.refs_4_
  28.8 0.0 collective-permute-done.10.refs_7_
  28.8 0.0 copy-done
  28.8 0.0 slice-start
  28.8 1.6 %collective-permute-start.15 = (f32[208,128]{1,0:T(8,128)S(1)}, f32[208,128]{1,0:T(8,128)S(1)}, u32[]{:S(2)}, u32[]{:S(2)}) collective-permute-start(f32[208,128]{1,0:T(8,128)S(1)} %slice.42), channel_id=1, source_target_pairs={{4,0},{8,4},{12,8},{14,12},{10,14},{6,10},{2,6},{0,2},{5,1},{9,5},... | collective-permute-start | bytes 319496 | tf_op jit(solution)/shard_map/ppermute | solution.py:399
  30.5 0.5 collective-permute-start.14
  31.0 0.0 slice-done
  31.0 1.8 %collective-permute-start.13 = (f32[768,128]{1,0:T(8,128)S(1)}, f32[768,128]{1,0:T(8,128)S(1)}, u32[]{:S(2)}, u32[]{:S(2)}) collective-permute-start(f32[768,128]{1,0:T(8,128)S(1)} %pad_maximum_fusion), channel_id=1, source_target_pairs={{0,16},{16,0},{1,17},{17,1},{2,18},{18,2},{3,19},{19,3},{4,20},{20... | collective-permute-start | bytes 1179656 | tf_op jit(solution)/shard_map/ppermute | solution.py:357
  32.8 0.8 %collective-permute-done.15.refs_9_ = f32[208,128]{1,0:T(8,128)S(1)} collective-permute-done((f32[208,128]{1,0:T(8,128)S(1)}, f32[208,128]{1,0:T(8,128)S(1)}, u32[]{:S(2)}, u32[]{:S(2)}) %collective-permute-start.15) | collective-permute-done | bytes 106528 | tf_op jit(solution)/shard_map/ppermute | solution.py:399
  33.6 0.0 copy-start.1
  33.6 2.2 %collective-permute-done.14.refs_8_ = f32[192,128]{1,0:T(8,128)S(1)} collective-permute-done((f32[192,128]{1,0:T(8,128)S(1)}, f32[192,128]{1,0:T(8,128)S(1)}, u32[]{:S(2)}, u32[]{:S(2)}) %collective-permute-start.14) | collective-permute-done | bytes 98336 | tf_op jit(solution)/shard_map/ppermute | solution.py:399
  35.9 1.1 %collective-permute-start.16 = (f32[384,128]{1,0:T(8,128)S(1)}, f32[384,128]{1,0:T(8,128)S(1)}, u32[]{:S(2)}, u32[]{:S(2)}) collective-permute-start(f32[384,128]{1,0:T(8,128)S(1)} %pad_maximum_fusion.3), channel_id=1, source_target_pairs={{0,16},{16,0},{1,17},{17,1},{2,18},{18,2},{3,19},{19,3},{4,20},{20... | collective-permute-start | bytes 589832 | tf_op jit(solution)/shard_map/ppermute | solution.py:357
  36.9 0.4 collective-permute-start.7
  37.4 1.6 %collective-permute-start.8 = (f32[128,128]{1,0:T(8,128)S(1)}, f32[128,128]{1,0:T(8,128)S(1)}, u32[]{:S(2)}, u32[]{:S(2)}) collective-permute-start(f32[128,128]{1,0:T(8,128)S(1)} %collective-permute-done.4.refs_3_), channel_id=1, source_target_pairs={{4,0},{8,4},{12,8},{14,12},{10,14},{6,10},{2,6},{0,2},{5,1},{9,5},... | collective-permute-start | bytes 196616 | tf_op jit(solution)/shard_map/ppermute | solution.py:389
  38.9 0.0 copy-done.1
  38.9 11.4 %shard_map.68 = (f32[2,3,1,128,128]{4,3,2,1,0:T(8,128)}, f32[2,6,1,128,128]{4,3,2,1,0:T(8,128)}, f32[8,24,128]{2,1,0:T(8,128)S(1)}) custom-call(s32[16]{0:T(128)S(1)} %get-tuple-element.18.refs_0_, f32[400,128]{1,0:T(8,128)S(1)} %maximum_maximum_fusion.refs_1_, f32[400,128]{1,0:T(8,128)S(1)} %collective-permute-done.1.refs_2_, ...), custom_call_target="tpu_custom_call" | custom-call | flops 1000000 | bytes 100000 | tf_op jit(solution)/shard_map/pallas_call | solution.py:323
  50.4 0.0 collective-permute-done.7.refs_5_
  50.4 0.0 collective-permute-done.8.refs_6_
  50.4 0.0 collective-permute-done.16.refs_9_
  50.4 0.0 collective-permute-done.13.refs_8_
  50.4 11.1 %shard_map.69 = (f32[2,3,1,128,128]{4,3,2,1,0:T(8,128)}, f32[2,6,1,128,128]{4,3,2,1,0:T(8,128)}) custom-call(s32[16]{0:T(128)S(1)} %get-tuple-element.12.refs_0_, f32[384,128]{1,0:T(8,128)S(1)} %bitcast.6, f32[128,128]{1,0:T(8,128)S(1)} %collective-permute-done.3.refs_2_, ...), custom_call_target="tpu_custom_call", output_to_operand_aliasing={{0}: (13, {}), {1}: (14, {})} | custom-call | flops 1000000 | bytes 100000 | tf_op jit(solution)/shard_map/pallas_call | solution.py:323
  (17 shorter events, 0.2 us)
Async XLA Ops:
  1.3 2.1 %collective-permute-start = (f32[6,128]{1,0:T(8,128)S(1)}, f32[6,128]{1,0:T(8,128)S(1)}, u32[]{:S(2)}, u32[]{:S(2)}) collective-permute-start(f32[6,128]{1,0:T(8,128)S(1)} %reshape_squeeze.3), channel_id=1, source_target_pairs={{0,1},{1,0},{2,3},{3,2},{4,5},{5,4},{6,7},{7,6},{8,9},{9,8},{10,11... | collective-permute-start | bytes 9224 | tf_op jit(solution)/shard_map/ppermute | solution.py:360
  1.4 0.7 %copy-start.2 = (s32[256]{0:T(256)S(1)}, s32[256]{0:T(256)}, u32[]{:S(2)}) copy-start(s32[256]{0:T(256)} %param.7) | copy-start | bytes 3076
  3.6 7.5 %collective-permute-start.1 = (f32[400,128]{1,0:T(8,128)S(1)}, f32[400,128]{1,0:T(8,128)S(1)}, u32[]{:S(2)}, u32[]{:S(2)}) collective-permute-start(f32[400,128]{1,0:T(8,128)S(1)} %maximum_maximum_fusion.refs_1_), channel_id=1, source_target_pairs={{0,4},{4,8},{8,12},{12,14},{14,10},{10,6},{6,2},{2,0},{1,5},{5,9},... | collective-permute-start | bytes 614408 | tf_op jit(solution)/shard_map/ppermute | solution.py:381
  4.1 7.5 %collective-permute-start.5 = (f32[400,128]{1,0:T(8,128)S(1)}, f32[400,128]{1,0:T(8,128)S(1)}, u32[]{:S(2)}, u32[]{:S(2)}) collective-permute-start(f32[400,128]{1,0:T(8,128)S(1)} %maximum_maximum_fusion.refs_1_), channel_id=1, source_target_pairs={{4,0},{8,4},{12,8},{14,12},{10,14},{6,10},{2,6},{0,2},{5,1},{9,5},... | collective-permute-start | bytes 614408 | tf_op jit(solution)/shard_map/ppermute | solution.py:381
  11.1 6.7 %collective-permute-start.2 = (f32[400,128]{1,0:T(8,128)S(1)}, f32[400,128]{1,0:T(8,128)S(1)}, u32[]{:S(2)}, u32[]{:S(2)}) collective-permute-start(f32[400,128]{1,0:T(8,128)S(1)} %collective-permute-done.1.refs_2_), channel_id=1, source_target_pairs={{0,4},{4,8},{8,12},{12,14},{14,10},{10,6},{6,2},{2,0},{1,5},{5,9},... | collective-permute-start | bytes 614408 | tf_op jit(solution)/shard_map/ppermute | solution.py:381
  11.6 6.7 %collective-permute-start.9 = (f32[400,128]{1,0:T(8,128)S(1)}, f32[400,128]{1,0:T(8,128)S(1)}, u32[]{:S(2)}, u32[]{:S(2)}) collective-permute-start(f32[400,128]{1,0:T(8,128)S(1)} %collective-permute-done.5.refs_3_), channel_id=1, source_target_pairs={{4,0},{8,4},{12,8},{14,12},{10,14},{6,10},{2,6},{0,2},{5,1},{9,5},... | collective-permute-start | bytes 614408 | tf_op jit(solution)/shard_map/ppermute | solution.py:381
  13.1 0.7 %copy-start.3 = (s32[6]{0:T(128)S(1)}, s32[6]{0:T(128)}, u32[]{:S(2)}) copy-start(s32[6]{0:T(128)} %param.8) | copy-start | bytes 76
  13.1 0.7 %copy-start.4 = (s32[8]{0:T(128)S(1)}, s32[8]{0:T(128)}, u32[]{:S(2)}) copy-start(s32[8]{0:T(128)} %param.9) | copy-start | bytes 100
  13.9 14.9 %collective-permute-start.6 = (f32[512,128]{1,0:T(8,128)S(1)}, f32[512,128]{1,0:T(8,128)S(1)}, u32[]{:S(2)}, u32[]{:S(2)}) collective-permute-start(f32[512,128]{1,0:T(8,128)S(1)} %pad_maximum_fusion.1), channel_id=1, source_target_pairs={{0,16},{16,0},{1,17},{17,1},{2,18},{18,2},{3,19},{19,3},{4,20},{20... | collective-permute-start | bytes 786440 | tf_op jit(solution)/shard_map/ppermute | solution.py:357
  17.8 6.4 %collective-permute-start.11 = (f32[400,128]{1,0:T(8,128)S(1)}, f32[400,128]{1,0:T(8,128)S(1)}, u32[]{:S(2)}, u32[]{:S(2)}) collective-permute-start(f32[400,128]{1,0:T(8,128)S(1)} %collective-permute-done.2.refs_4_), channel_id=1, source_target_pairs={{0,4},{4,8},{8,12},{12,14},{14,10},{10,6},{6,2},{2,0},{1,5},{5,9},... | collective-permute-start | bytes 614408 | tf_op jit(solution)/shard_map/ppermute | solution.py:381
  18.3 10.5 %collective-permute-start.10 = (f32[512,128]{1,0:T(8,128)S(1)}, f32[512,128]{1,0:T(8,128)S(1)}, u32[]{:S(2)}, u32[]{:S(2)}) collective-permute-start(f32[512,128]{1,0:T(8,128)S(1)} %pad_maximum_fusion.2), channel_id=1, source_target_pairs={{0,16},{16,0},{1,17},{17,1},{2,18},{18,2},{3,19},{19,3},{4,20},{20... | collective-permute-start | bytes 786440 | tf_op jit(solution)/shard_map/ppermute | solution.py:357
  19.9 6.5 %collective-permute-start.12 = (f32[400,128]{1,0:T(8,128)S(1)}, f32[400,128]{1,0:T(8,128)S(1)}, u32[]{:S(2)}, u32[]{:S(2)}) collective-permute-start(f32[400,128]{1,0:T(8,128)S(1)} %collective-permute-done.9.refs_5_), channel_id=1, source_target_pairs={{4,0},{8,4},{12,8},{14,12},{10,14},{6,10},{2,6},{0,2},{5,1},{9,5},... | collective-permute-start | bytes 614408 | tf_op jit(solution)/shard_map/ppermute | solution.py:381
  22.3 4.3 %collective-permute-start.3 = (f32[128,128]{1,0:T(8,128)S(1)}, f32[128,128]{1,0:T(8,128)S(1)}, u32[]{:S(2)}, u32[]{:S(2)}) collective-permute-start(f32[128,128]{1,0:T(8,128)S(1)} %bitcast.8), channel_id=1, source_target_pairs={{0,4},{4,8},{8,12},{12,14},{14,10},{10,6},{6,2},{2,0},{1,5},{5,9},... | collective-permute-start | bytes 196616 | tf_op jit(solution)/shard_map/ppermute | solution.py:388
  24.2 4.6 %collective-permute-start.4 = (f32[128,128]{1,0:T(8,128)S(1)}, f32[128,128]{1,0:T(8,128)S(1)}, u32[]{:S(2)}, u32[]{:S(2)}) collective-permute-start(f32[128,128]{1,0:T(8,128)S(1)} %bitcast.9), channel_id=1, source_target_pairs={{4,0},{8,4},{12,8},{14,12},{10,14},{6,10},{2,6},{0,2},{5,1},{9,5},... | collective-permute-start | bytes 196616 | tf_op jit(solution)/shard_map/ppermute | solution.py:389
  26.4 2.5 %copy-start = (f32[400,128]{1,0:T(8,128)}, f32[400,128]{1,0:T(8,128)S(1)}, u32[]{:S(2)}) copy-start(f32[400,128]{1,0:T(8,128)S(1)} %collective-permute-done.12.refs_7_) | copy-start | bytes 614404
  28.8 2.1 %slice-start = ((f32[400,128]{1,0:T(8,128)}), f32[384,128]{1,0:T(8,128)S(1)}, s32[]{:S(2)}) async-start(f32[400,128]{1,0:T(8,128)} %copy-done), calls=%async_computation | async-start | bytes 393216 | tf_op jit(solution)/shard_map/slice | solution.py:394
  28.8 4.8 %collective-permute-start.15 = (f32[208,128]{1,0:T(8,128)S(1)}, f32[208,128]{1,0:T(8,128)S(1)}, u32[]{:S(2)}, u32[]{:S(2)}) collective-permute-start(f32[208,128]{1,0:T(8,128)S(1)} %slice.42), channel_id=1, source_target_pairs={{4,0},{8,4},{12,8},{14,12},{10,14},{6,10},{2,6},{0,2},{5,1},{9,5},... | collective-permute-start | bytes 319496 | tf_op jit(solution)/shard_map/ppermute | solution.py:399
  30.5 5.4 %collective-permute-start.14 = (f32[192,128]{1,0:T(8,128)S(1)}, f32[192,128]{1,0:T(8,128)S(1)}, u32[]{:S(2)}, u32[]{:S(2)}) collective-permute-start(f32[192,128]{1,0:T(8,128)S(1)} %slice.41), channel_id=1, source_target_pairs={{0,4},{4,8},{8,12},{12,14},{14,10},{10,6},{6,2},{2,0},{1,5},{5,9},... | collective-permute-start | bytes 294920 | tf_op jit(solution)/shard_map/ppermute | solution.py:399
  31.0 19.4 %collective-permute-start.13 = (f32[768,128]{1,0:T(8,128)S(1)}, f32[768,128]{1,0:T(8,128)S(1)}, u32[]{:S(2)}, u32[]{:S(2)}) collective-permute-start(f32[768,128]{1,0:T(8,128)S(1)} %pad_maximum_fusion), channel_id=1, source_target_pairs={{0,16},{16,0},{1,17},{17,1},{2,18},{18,2},{3,19},{19,3},{4,20},{20... | collective-permute-start | bytes 1179656 | tf_op jit(solution)/shard_map/ppermute | solution.py:357
  33.6 5.3 %copy-start.1 = (f32[400,128]{1,0:T(8,128)S(1)}, f32[400,128]{1,0:T(8,128)}, u32[]{:S(2)}) copy-start(f32[400,128]{1,0:T(8,128)} %copy-done) | copy-start | bytes 614404
  35.9 14.5 %collective-permute-start.16 = (f32[384,128]{1,0:T(8,128)S(1)}, f32[384,128]{1,0:T(8,128)S(1)}, u32[]{:S(2)}, u32[]{:S(2)}) collective-permute-start(f32[384,128]{1,0:T(8,128)S(1)} %pad_maximum_fusion.3), channel_id=1, source_target_pairs={{0,16},{16,0},{1,17},{17,1},{2,18},{18,2},{3,19},{19,3},{4,20},{20... | collective-permute-start | bytes 589832 | tf_op jit(solution)/shard_map/ppermute | solution.py:357
  36.9 13.5 %collective-permute-start.7 = (f32[128,128]{1,0:T(8,128)S(1)}, f32[128,128]{1,0:T(8,128)S(1)}, u32[]{:S(2)}, u32[]{:S(2)}) collective-permute-start(f32[128,128]{1,0:T(8,128)S(1)} %collective-permute-done.3.refs_2_), channel_id=1, source_target_pairs={{0,4},{4,8},{8,12},{12,14},{14,10},{10,6},{6,2},{2,0},{1,5},{5,9},... | collective-permute-start | bytes 196616 | tf_op jit(solution)/shard_map/ppermute | solution.py:388
  37.4 13.0 %collective-permute-start.8 = (f32[128,128]{1,0:T(8,128)S(1)}, f32[128,128]{1,0:T(8,128)S(1)}, u32[]{:S(2)}, u32[]{:S(2)}) collective-permute-start(f32[128,128]{1,0:T(8,128)S(1)} %collective-permute-done.4.refs_3_), channel_id=1, source_target_pairs={{4,0},{8,4},{12,8},{14,12},{10,14},{6,10},{2,6},{0,2},{5,1},{9,5},... | collective-permute-start | bytes 196616 | tf_op jit(solution)/shard_map/ppermute | solution.py:389

commit v3 on v2

--- a/solution.py
+++ b/solution.py
@@ -49,7 +49,7 @@
         self.first_row, self.last_row = row == 0, row == ROWS - 1
         self.first_lane, self.last_lane = lane == 0, lane == cells_z - 1
         self.cells_z = cells_z
-        self.loaded, self.rolled = {}, {}
+        self.loaded = {}
 
     def fetch(self, chunk):
         if chunk < self.chunks:
@@ -63,22 +63,23 @@
         array, lead = self.sources[name]
         array[lead + (slice(chunk * ROWS, chunk * ROWS + ROWS),)] = value
 
-    def roll_rows(self, field, chunk, by):
-        if not 0 <= chunk < self.chunks:
-            return 0.0
-        if (field, chunk) not in self.rolled:
-            self.rolled[field, chunk] = pltpu.roll(self.at(field, chunk), by, 0)
-        return self.rolled[field, chunk]
+    def edge(self, name, chunk, by):
+        array, lead = self.sources[name]
+        return pltpu.roll(array[lead + (slice(chunk * ROWS, chunk * ROWS + ROWS),)], by, 0)
 
     def back_y(self, field, chunk):
-        here = self.roll_rows(field, chunk, 1)
-        before = self.roll_rows(field, chunk - 1, 1)
-        return self.at(field, chunk) - jnp.where(self.first_row, before, here)
+        if chunk > 0:
+            before = self.at(field, chunk - 1)
+        else:
+            before = jnp.where(self.first_row, 0.0, self.edge(field, self.chunks - 1, 1))
+        return self.at(field, chunk) - before
 
     def fore_y(self, field, chunk):
-        here = self.roll_rows(field, chunk, ROWS - 1)
-        after = self.roll_rows(field, chunk + 1, ROWS - 1)
-        return jnp.where(self.last_row, after, here) - self.at(field, chunk)
+        if chunk < self.chunks - 1:
+            after = self.at(field, chunk + 1)
+        else:
+            after = jnp.where(self.last_row, 0.0, self.edge(field, 0, ROWS - 1))
+        return after - self.at(field, chunk)
 
     def back_x(self, field, chunk):
         return self.at(field, chunk) - self.at(field, chunk, -1)
@@ -116,7 +117,7 @@
         rest = rest[1:]
     else:
         values = given_ref
-    fields, (medium, added, stored, lines, sems) = rest[:9], rest[9:]
+    fields, (medium, added, stored, lines, results, sems) = rest[:9], rest[9:]
     block_y = cells_y // ring
     chunks = cells_y // ROWS
 
@@ -131,13 +132,14 @@
         centre = planes // 2
         blocks = {0: 0}
     for operand, row, first_unit, units, offset in parts:
-        top = pl.multiple_of(blocks[offset] * block_y, 8)
         for unit in range(units):
             component, plane = divmod(first_unit + unit, planes)
-            source = row + unit * block_y
-            medium[component, plane, pl.ds(top, block_y), :] = (
-                TIME_STEP * piece_refs[operand][source : source + block_y, :]
-            )
+            for part in range(block_y // chunks):
+                source = row + unit * block_y + part * chunks
+                line = blocks[offset] * (block_y // chunks) + part
+                medium[component, plane, pl.ds(line, chunks, stride=ROWS), :] = (
+                    TIME_STEP * piece_refs[operand][source : source + chunks, :]
+                )
 
     outside = jnp.zeros((cells_y, cells_z), jnp.float32)
     for field in (XY, XZ, VX):
@@ -281,15 +283,21 @@
     lax.fori_loop(1, STEPS - 1, one_step, 0)
     trial = scalars[1]
     copies = []
-    for field in range(9):
+
+    def give(field):
+        for chunk in range(chunks):
+            found = fields[field][centre + 1, chunk * ROWS : chunk * ROWS + ROWS, :]
+            results[field, pl.ds(chunk, ROWS, stride=chunks), :] = found
         target = vel_ref.at[trial, field, 0] if field < 3 else str_ref.at[trial, field - 3, 0]
-        copies.append(pltpu.make_async_copy(fields[field].at[centre + 1], target, sems.at[field]))
+        copies.append(pltpu.make_async_copy(results.at[field], target, sems.at[field]))
+        copies[-1].start()
+
     velocities(STEPS - 1)
-    for copy in copies[:3]:
-        copy.start()
+    for field in range(3):
+        give(field)
     stress(STEPS - 1, False, True, centre, 0)
-    for copy in copies[3:]:
-        copy.start()
+    for field in range(3, 9):
+        give(field)
     for copy in copies:
         copy.wait()
 
@@ -332,6 +340,7 @@
             pltpu.VMEM((3, planes, cells_y, cells_z), jnp.float32),
             pltpu.VMEM((ring, 2 * ROWS, cells_z), jnp.float32),
             pltpu.VMEM((2, LINES, cells_z), jnp.float32),
+            pltpu.VMEM((9, cells_y, cells_z), jnp.float32),
             pltpu.SemaphoreType.DMA((9,)),
         ],
         compiler_params=pltpu.CompilerParams(vmem_limit_bytes=24 * 1024 * 1024),
@@ -374,8 +383,9 @@
         pieces[which].append(piece)
 
     forth, back, forth_later, back_later, rests = first, first, later, later, []
-    lates = []
     for distance in range(1, count // 2):
+        if distance == 2:
+            forth, _ = lax.optimization_barrier((forth, (forth_later, back_later)))
         if distance == 3:
             forth, early = lax.optimization_barrier((forth, early))
         forth, back = lax.ppermute(forth, "box", up), lax.ppermute(back, "box", down)
@@ -387,15 +397,17 @@
             skip = third
             forth_later = lax.ppermute(forth_later, "box", up)
             back_later = lax.ppermute(back_later, "box", down)
-            lates.append((forth_later, back_later))
             for piece, offset in ((forth_later, -distance), (back_later, distance)):
                 keep(1, piece, [(0, 0, units // 3, offset)])
+        rest = jnp.concatenate([forth[skip:size], back[skip:size]])
+        if distance == 3:
+            rest, _ = lax.optimization_barrier((rest, rests[1]))
+        rest = across(rest)
+        rests.append(rest)
         left = units - skip * units // size
-        rest = across(jnp.concatenate([forth[skip:size], back[skip:size]]))
-        rests.append(rest)
         keep(1, rest, [(0, units - left, left, -distance), (size - skip, units - left, left, distance)])
     far = count // 2
-    forth, back, _ = lax.optimization_barrier((forth, back, (rests[:2], lates[0])))
+    forth, back, _ = lax.optimization_barrier((forth, back, (rests[0], forth_later, back_later)))
     forth, back = lax.ppermute(forth[:half], "box", up), lax.ppermute(back[half:], "box", down)
     row_parts.append((len(pieces[0]) + 1, size - half, far))
     keep(0, forth, [(0, 0, units // 2, far)])
@@ -406,7 +418,7 @@
 
 
 def hot_planes(offsets, cells_y, cells_z):
-    rows = jnp.arange(cells_y, dtype=jnp.int32)[None, :, None]
+    rows = jnp.arange(cells_y, dtype=jnp.int32).reshape(ROWS, cells_y // ROWS).T.reshape(1, cells_y, 1)
     columns = jnp.arange(cells_z, dtype=jnp.int32)[None, None, :]
     hot_y = (offsets[:, None, :] // cells_z == rows).astype(jnp.float32)
     hot_z = (offsets[:, :, None] % cells_z == columns).astype(jnp.bfloat16)

time: 61.8 us -> 62.6 us (1.013)
  waiting for transfers between devices: 15 us -> 17.3 us
  starting transfers between devices: 18.4 us -> 16.6 us
  other arithmetic: 1.2 us -> 0.54 us
    ppermute x2, waiting for transfers between devices: 0.23 us -> 3.82 us  [around(): forth_later = lax.ppermute(forth_later, 'box', up)]
    ppermute x4, starting transfers between devices: 5.98 us -> 4.12 us  [across(): return lax.ppermute(value, 'groups', [(0, 1), (1, 0)])]
    ppermute x3, waiting for transfers between devices: 8.95 us -> 7.41 us  [around(): lax.ppermute(forth, 'box', up)]
    ppermute x2, waiting for transfers between devices: 2.22 us -> 3.37 us  [around(): back_later = lax.ppermute(back_later, 'box', down)]
    slice x7, local copies, waits for them, and re-layouts: 0.06 us -> 0.96 us  [around(): rest = jnp.concatenate([forth[skip:size], back[skip:size]])]
    ppermute x1, waiting for transfers between devices: 2.22 us -> 1.52 us  [around(): lax.ppermute(forth[:half], 'box', up)]
    unnamed x1, other arithmetic: 0.7 us -> 0.02 us
    unnamed x10 -> x12, local copies, waits for them, and re-layouts: 1.35 us -> 0.69 us
  transfers between devices with their start and end apart: 17 -> 17, of which waited for: 8 -> 6; matrix products, arithmetic and copies ran while one was open for 4% -> 3% of each run, Pallas kernels for 19% -> 19%
where the time goes in v3:
time: 62.6 us; the launch traced here: 62.3 us
  Pallas kernels  23 us (37%)
  waiting for transfers between devices  17.3 us (28%)
  starting transfers between devices  16.6 us (27%)
  local copies, waits for them, and re-layouts  3.92 us (6%)
  between operations  0.88 us (1%)
    pallas_call x2, Pallas kernels, run_trial(): pl.pallas_call(functools.partial(propagate, (parts, row_parts, ring, plan...  23 us
    ppermute x3, waiting for transfers between devices, around(): lax.ppermute(forth, 'box', up)  7.41 us
    ppermute x3, starting transfers between devices, around(): lax.ppermute(back, 'box', down)  4.83 us
    ppermute x4, starting transfers between devices, across(): return lax.ppermute(value, 'groups', [(0, 1), (1, 0)])  4.12 us
    ppermute x2, waiting for transfers between devices, around(): forth_later = lax.ppermute(forth_later, 'box', up)  3.82 us
    ppermute x2, waiting for transfers between devices, around(): back_later = lax.ppermute(back_later, 'box', down)  3.37 us
    ppermute x2, starting transfers between devices, around(): back_later = lax.ppermute(back_later, 'box', down)  3.15 us
    ppermute x1, starting transfers between devices, around(): lax.ppermute(back[half:], 'box', down)  1.63 us
  transfers between devices with their start and end apart: 17, of which 6 were waited for; matrix products, arithmetic and copies ran while one was open for 3% of the time, Pallas kernels for 19%

profile of v3, /device:TPU:10, one launch (start us, length us, event | category | flops | bytes accessed | tf_op | source)
XLA Modules:
  0.0 62.3 jit_solution(252831432679697558)
XLA Ops:
  0.6 0.0 copy-start.2
  0.6 0.9 %constant_dynamic-slice_fusion = f32[1,1,8,16,128]{4,3,2,1,0:T(8,128)S(1)} fusion(f32[2,3,8,16,128]{4,3,2,1,0:T(8,128)} %param.5, s32[]{:T(128)S(6)} %select_n.45), kind=kLoop, calls=%fused_computation.19 | loop fusion | bytes 131076 | tf_op jit(solution)/shard_map/slice | solution.py:378
  1.5 0.4 collective-permute-start.2
  1.9 1.6 %collective-permute-start.3 = (f32[128,128]{1,0:T(8,128)S(1)}, f32[128,128]{1,0:T(8,128)S(1)}, u32[]{:S(2)}, u32[]{:S(2)}) collective-permute-start(f32[128,128]{1,0:T(8,128)S(1)} %bitcast.9), channel_id=1, source_target_pairs={{4,0},{8,4},{12,8},{14,12},{10,14},{6,10},{2,6},{0,2},{5,1},{9,5},... | collective-permute-start | bytes 196616 | tf_op jit(solution)/shard_map/ppermute | solution.py:399
  3.5 0.0 copy-done.2
  3.6 0.1 collective-permute-start
  3.6 0.0 copy-start.3
  3.6 1.1 %constant_dynamic-slice_fusion.1 = (f32[1,3,8,16,128]{4,3,2,1,0:T(8,128)S(1)}, f32[1,3,8,16,128]{4,3,2,1,0:T(8,128)S(1)}) fusion(f32[2,3,8,16,128]{4,3,2,1,0:T(8,128)} %param.5, s32[]{:T(128)S(6)} %select_n.45, s32[]{:T(128)S(6)} %select_n.41), kind=kLoop, calls=%fused_computation.20 | loop fusion | bytes 786440 | tf_op jit(solution)/shard_map/jit(dynamic_index_in_dim)/dynamic_slice | solution.py:373
  4.7 0.0 copy-done.3
  4.7 0.1 tile.9
  4.8 0.1 tile.11
  4.9 0.1 reshape.158
  5.0 0.1 pad.19.clone
  5.1 0.0 collective-permute-done
  5.1 0.1 maximum_maximum_fusion.refs_1_
  5.2 0.5 collective-permute-start.1
  5.7 1.6 %collective-permute-start.5 = (f32[400,128]{1,0:T(8,128)S(1)}, f32[400,128]{1,0:T(8,128)S(1)}, u32[]{:S(2)}, u32[]{:S(2)}) collective-permute-start(f32[400,128]{1,0:T(8,128)S(1)} %maximum_maximum_fusion.refs_1_), channel_id=1, source_target_pairs={{4,0},{8,4},{12,8},{14,12},{10,14},{6,10},{2,6},{0,2},{5,1},{9,5},... | collective-permute-start | bytes 614408 | tf_op jit(solution)/shard_map/ppermute | solution.py:391
  7.3 0.2 fusion
  7.5 0.0 collective-permute-done.2.refs_2_
  7.6 0.0 collective-permute-done.3.refs_3_
  7.6 5.2 %collective-permute-done.1.refs_2_ = f32[400,128]{1,0:T(8,128)S(1)} collective-permute-done((f32[400,128]{1,0:T(8,128)S(1)}, f32[400,128]{1,0:T(8,128)S(1)}, u32[]{:S(2)}, u32[]{:S(2)}) %collective-permute-start.1) | collective-permute-done | bytes 204832 | tf_op jit(solution)/shard_map/ppermute | solution.py:391
  12.8 0.4 collective-permute-start.4
  13.2 0.0 collective-permute-done.5.refs_3_
  13.2 1.6 %collective-permute-start.9 = (f32[400,128]{1,0:T(8,128)S(1)}, f32[400,128]{1,0:T(8,128)S(1)}, u32[]{:S(2)}, u32[]{:S(2)}) collective-permute-start(f32[400,128]{1,0:T(8,128)S(1)} %collective-permute-done.5.refs_3_), channel_id=1, source_target_pairs={{4,0},{8,4},{12,8},{14,12},{10,14},{6,10},{2,6},{0,2},{5,1},{9,5},... | collective-permute-start | bytes 614408 | tf_op jit(solution)/shard_map/ppermute | solution.py:391
  14.9 1.6 %collective-permute-start.6 = (f32[512,128]{1,0:T(8,128)S(1)}, f32[512,128]{1,0:T(8,128)S(1)}, u32[]{:S(2)}, u32[]{:S(2)}) collective-permute-start(f32[512,128]{1,0:T(8,128)S(1)} %pad_maximum_fusion.1), channel_id=1, source_target_pairs={{0,16},{16,0},{1,17},{17,1},{2,18},{18,2},{3,19},{19,3},{4,20},{20... | collective-permute-start | bytes 786440 | tf_op jit(solution)/shard_map/ppermute | solution.py:366
  16.5 0.0 copy-start.4
  16.5 0.0 copy-start.5
  16.5 0.7 %copy-done.4 = s32[6]{0:T(128)S(1)} copy-done((s32[6]{0:T(128)S(1)}, s32[6]{0:T(128)}, u32[]{:S(2)}) %copy-start.4) | copy-done | bytes 48
  17.1 0.0 copy-done.5
  17.1 0.1 add_add_fusion.1
  17.2 2.2 %collective-permute-done.4.refs_4_ = f32[400,128]{1,0:T(8,128)S(1)} collective-permute-done((f32[400,128]{1,0:T(8,128)S(1)}, f32[400,128]{1,0:T(8,128)S(1)}, u32[]{:S(2)}, u32[]{:S(2)}) %collective-permute-start.4) | collective-permute-done | bytes 204832 | tf_op jit(solution)/shard_map/ppermute | solution.py:391
  19.4 0.4 collective-permute-start.11
  19.9 0.0 collective-permute-done.9.refs_5_
  19.9 1.6 %collective-permute-start.12 = (f32[400,128]{1,0:T(8,128)S(1)}, f32[400,128]{1,0:T(8,128)S(1)}, u32[]{:S(2)}, u32[]{:S(2)}) collective-permute-start(f32[400,128]{1,0:T(8,128)S(1)} %collective-permute-done.9.refs_5_), channel_id=1, source_target_pairs={{4,0},{8,4},{12,8},{14,12},{10,14},{6,10},{2,6},{0,2},{5,1},{9,5},... | collective-permute-start | bytes 614408 | tf_op jit(solution)/shard_map/ppermute | solution.py:391
  21.6 1.6 %collective-permute-start.10 = (f32[512,128]{1,0:T(8,128)S(1)}, f32[512,128]{1,0:T(8,128)S(1)}, u32[]{:S(2)}, u32[]{:S(2)}) collective-permute-start(f32[512,128]{1,0:T(8,128)S(1)} %pad_maximum_fusion.2), channel_id=1, source_target_pairs={{0,16},{16,0},{1,17},{17,1},{2,18},{18,2},{3,19},{19,3},{4,20},{20... | collective-permute-start | bytes 786440 | tf_op jit(solution)/shard_map/ppermute | solution.py:366
  23.2 0.4 collective-permute-start.7
  23.6 3.8 %collective-permute-done.7.refs_5_ = f32[128,128]{1,0:T(8,128)S(1)} collective-permute-done((f32[128,128]{1,0:T(8,128)S(1)}, f32[128,128]{1,0:T(8,128)S(1)}, u32[]{:S(2)}, u32[]{:S(2)}) %collective-permute-start.7) | collective-permute-done | bytes 65568 | tf_op jit(solution)/shard_map/ppermute | solution.py:398
  27.4 1.6 %collective-permute-start.8 = (f32[128,128]{1,0:T(8,128)S(1)}, f32[128,128]{1,0:T(8,128)S(1)}, u32[]{:S(2)}, u32[]{:S(2)}) collective-permute-start(f32[128,128]{1,0:T(8,128)S(1)} %collective-permute-done.3.refs_3_), channel_id=1, source_target_pairs={{4,0},{8,4},{12,8},{14,12},{10,14},{6,10},{2,6},{0,2},{5,1},{9,5},... | collective-permute-start | bytes 196616 | tf_op jit(solution)/shard_map/ppermute | solution.py:399
  29.0 3.4 %collective-permute-done.8.refs_6_ = f32[128,128]{1,0:T(8,128)S(1)} collective-permute-done((f32[128,128]{1,0:T(8,128)S(1)}, f32[128,128]{1,0:T(8,128)S(1)}, u32[]{:S(2)}, u32[]{:S(2)}) %collective-permute-start.8) | collective-permute-done | bytes 65568 | tf_op jit(solution)/shard_map/ppermute | solution.py:399
  32.4 0.0 collective-permute-done.6.refs_4_
  32.4 0.0 collective-permute-done.11.refs_6_
  32.4 0.0 copy-start
  32.4 0.0 collective-permute-done.12.refs_7_
  32.4 1.6 %collective-permute-start.15 = (f32[208,128]{1,0:T(8,128)S(1)}, f32[208,128]{1,0:T(8,128)S(1)}, u32[]{:S(2)}, u32[]{:S(2)}) collective-permute-start(f32[208,128]{1,0:T(8,128)S(1)} %slice.42), channel_id=1, source_target_pairs={{4,0},{8,4},{12,8},{14,12},{10,14},{6,10},{2,6},{0,2},{5,1},{9,5},... | collective-permute-start | bytes 319496 | tf_op jit(solution)/shard_map/ppermute | solution.py:411
  34.1 0.5 collective-permute-start.14
  34.6 0.0 copy-done
  34.6 0.0 slice-start
  34.6 0.9 %slice-done = f32[384,128]{1,0:T(8,128)S(1)} async-done(((f32[400,128]{1,0:T(8,128)}), f32[384,128]{1,0:T(8,128)S(1)}, s32[]{:S(2)}) %slice-start) | async-done | bytes 196632 | tf_op jit(solution)/shard_map/slice | solution.py:402
  35.5 0.0 collective-permute-done.10.refs_7_
  35.5 0.5 collective-permute-start.13
  36.0 1.2 %collective-permute-done.15.refs_9_ = f32[208,128]{1,0:T(8,128)S(1)} collective-permute-done((f32[208,128]{1,0:T(8,128)S(1)}, f32[208,128]{1,0:T(8,128)S(1)}, u32[]{:S(2)}, u32[]{:S(2)}) %collective-permute-start.15) | collective-permute-done | bytes 106528 | tf_op jit(solution)/shard_map/ppermute | solution.py:411
  37.2 0.0 copy-start.1
  37.2 1.5 %collective-permute-done.14.refs_8_ = f32[192,128]{1,0:T(8,128)S(1)} collective-permute-done((f32[192,128]{1,0:T(8,128)S(1)}, f32[192,128]{1,0:T(8,128)S(1)}, u32[]{:S(2)}, u32[]{:S(2)}) %collective-permute-start.14) | collective-permute-done | bytes 98336 | tf_op jit(solution)/shard_map/ppermute | solution.py:411
  38.7 0.5 collective-permute-start.16
  39.2 0.0 copy-done.1
  39.2 11.7 %shard_map.68 = (f32[2,3,1,128,128]{4,3,2,1,0:T(8,128)}, f32[2,6,1,128,128]{4,3,2,1,0:T(8,128)}, f32[8,24,128]{2,1,0:T(8,128)S(1)}) custom-call(s32[16]{0:T(128)S(1)} %get-tuple-element.22.refs_0_, f32[400,128]{1,0:T(8,128)S(1)} %maximum_maximum_fusion.refs_1_, f32[400,128]{1,0:T(8,128)S(1)} %collective-permute-done.1.refs_2_, ...), custom_call_target="tpu_custom_call" | custom-call | flops 1000000 | bytes 100000 | tf_op jit(solution)/shard_map/pallas_call | solution.py:331
  50.9 0.0 collective-permute-done.16.refs_9_
  50.9 0.0 collective-permute-done.13.refs_8_
  50.9 11.4 %shard_map.69 = (f32[2,3,1,128,128]{4,3,2,1,0:T(8,128)}, f32[2,6,1,128,128]{4,3,2,1,0:T(8,128)}) custom-call(s32[16]{0:T(128)S(1)} %get-tuple-element.15.refs_0_, f32[384,128]{1,0:T(8,128)S(1)} %bitcast.6, f32[128,128]{1,0:T(8,128)S(1)} %collective-permute-done.2.refs_2_, ...), custom_call_target="tpu_custom_call", output_to_operand_aliasing={{0}: (13, {}), {1}: (14, {})} | custom-call | flops 1000000 | bytes 100000 | tf_op jit(solution)/shard_map/pallas_call | solution.py:331
  (19 shorter events, 0.2 us)
Async XLA Ops:
  0.6 2.9 %copy-start.2 = (f32[1,3,256]{2,0,1:T(1,128)S(1)}, f32[1,3,256]{2,0,1:T(1,128)}, u32[]{:S(2)}) copy-start(f32[1,3,256]{2,0,1:T(1,128)} %param.6) | copy-start | bytes 9220
  1.5 6.0 %collective-permute-start.2 = (f32[128,128]{1,0:T(8,128)S(1)}, f32[128,128]{1,0:T(8,128)S(1)}, u32[]{:S(2)}, u32[]{:S(2)}) collective-permute-start(f32[128,128]{1,0:T(8,128)S(1)} %bitcast.8), channel_id=1, source_target_pairs={{0,4},{4,8},{8,12},{12,14},{14,10},{10,6},{6,2},{2,0},{1,5},{5,9},... | collective-permute-start | bytes 196616 | tf_op jit(solution)/shard_map/ppermute | solution.py:398
  1.9 5.6 %collective-permute-start.3 = (f32[128,128]{1,0:T(8,128)S(1)}, f32[128,128]{1,0:T(8,128)S(1)}, u32[]{:S(2)}, u32[]{:S(2)}) collective-permute-start(f32[128,128]{1,0:T(8,128)S(1)} %bitcast.9), channel_id=1, source_target_pairs={{4,0},{8,4},{12,8},{14,12},{10,14},{6,10},{2,6},{0,2},{5,1},{9,5},... | collective-permute-start | bytes 196616 | tf_op jit(solution)/shard_map/ppermute | solution.py:399
  3.6 1.5 %collective-permute-start = (f32[6,128]{1,0:T(8,128)S(1)}, f32[6,128]{1,0:T(8,128)S(1)}, u32[]{:S(2)}, u32[]{:S(2)}) collective-permute-start(f32[6,128]{1,0:T(8,128)S(1)} %reshape_squeeze.3), channel_id=1, source_target_pairs={{0,1},{1,0},{2,3},{3,2},{4,5},{5,4},{6,7},{7,6},{8,9},{9,8},{10,11... | collective-permute-start | bytes 9224 | tf_op jit(solution)/shard_map/ppermute | solution.py:369
  3.6 1.1 %copy-start.3 = (s32[256]{0:T(256)S(1)}, s32[256]{0:T(256)}, u32[]{:S(2)}) copy-start(s32[256]{0:T(256)} %param.7) | copy-start | bytes 3076
  5.2 7.5 %collective-permute-start.1 = (f32[400,128]{1,0:T(8,128)S(1)}, f32[400,128]{1,0:T(8,128)S(1)}, u32[]{:S(2)}, u32[]{:S(2)}) collective-permute-start(f32[400,128]{1,0:T(8,128)S(1)} %maximum_maximum_fusion.refs_1_), channel_id=1, source_target_pairs={{0,4},{4,8},{8,12},{12,14},{14,10},{10,6},{6,2},{2,0},{1,5},{5,9},... | collective-permute-start | bytes 614408 | tf_op jit(solution)/shard_map/ppermute | solution.py:391
  5.7 7.5 %collective-permute-start.5 = (f32[400,128]{1,0:T(8,128)S(1)}, f32[400,128]{1,0:T(8,128)S(1)}, u32[]{:S(2)}, u32[]{:S(2)}) collective-permute-start(f32[400,128]{1,0:T(8,128)S(1)} %maximum_maximum_fusion.refs_1_), channel_id=1, source_target_pairs={{4,0},{8,4},{12,8},{14,12},{10,14},{6,10},{2,6},{0,2},{5,1},{9,5},... | collective-permute-start | bytes 614408 | tf_op jit(solution)/shard_map/ppermute | solution.py:391
  12.8 6.7 %collective-permute-start.4 = (f32[400,128]{1,0:T(8,128)S(1)}, f32[400,128]{1,0:T(8,128)S(1)}, u32[]{:S(2)}, u32[]{:S(2)}) collective-permute-start(f32[400,128]{1,0:T(8,128)S(1)} %collective-permute-done.1.refs_2_), channel_id=1, source_target_pairs={{0,4},{4,8},{8,12},{12,14},{14,10},{10,6},{6,2},{2,0},{1,5},{5,9},... | collective-permute-start | bytes 614408 | tf_op jit(solution)/shard_map/ppermute | solution.py:391
  13.2 6.7 %collective-permute-start.9 = (f32[400,128]{1,0:T(8,128)S(1)}, f32[400,128]{1,0:T(8,128)S(1)}, u32[]{:S(2)}, u32[]{:S(2)}) collective-permute-start(f32[400,128]{1,0:T(8,128)S(1)} %collective-permute-done.5.refs_3_), channel_id=1, source_target_pairs={{4,0},{8,4},{12,8},{14,12},{10,14},{6,10},{2,6},{0,2},{5,1},{9,5},... | collective-permute-start | bytes 614408 | tf_op jit(solution)/shard_map/ppermute | solution.py:391
  14.9 17.5 %collective-permute-start.6 = (f32[512,128]{1,0:T(8,128)S(1)}, f32[512,128]{1,0:T(8,128)S(1)}, u32[]{:S(2)}, u32[]{:S(2)}) collective-permute-start(f32[512,128]{1,0:T(8,128)S(1)} %pad_maximum_fusion.1), channel_id=1, source_target_pairs={{0,16},{16,0},{1,17},{17,1},{2,18},{18,2},{3,19},{19,3},{4,20},{20... | collective-permute-start | bytes 786440 | tf_op jit(solution)/shard_map/ppermute | solution.py:366
  16.5 0.7 %copy-start.4 = (s32[6]{0:T(128)S(1)}, s32[6]{0:T(128)}, u32[]{:S(2)}) copy-start(s32[6]{0:T(128)} %param.8) | copy-start | bytes 76
  16.5 0.7 %copy-start.5 = (s32[8]{0:T(128)S(1)}, s32[8]{0:T(128)}, u32[]{:S(2)}) copy-start(s32[8]{0:T(128)} %param.9) | copy-start | bytes 100
  19.4 12.9 %collective-permute-start.11 = (f32[400,128]{1,0:T(8,128)S(1)}, f32[400,128]{1,0:T(8,128)S(1)}, u32[]{:S(2)}, u32[]{:S(2)}) collective-permute-start(f32[400,128]{1,0:T(8,128)S(1)} %collective-permute-done.4.refs_4_), channel_id=1, source_target_pairs={{0,4},{4,8},{8,12},{12,14},{14,10},{10,6},{6,2},{2,0},{1,5},{5,9},... | collective-permute-start | bytes 614408 | tf_op jit(solution)/shard_map/ppermute | solution.py:391
  19.9 12.5 %collective-permute-start.12 = (f32[400,128]{1,0:T(8,128)S(1)}, f32[400,128]{1,0:T(8,128)S(1)}, u32[]{:S(2)}, u32[]{:S(2)}) collective-permute-start(f32[400,128]{1,0:T(8,128)S(1)} %collective-permute-done.9.refs_5_), channel_id=1, source_target_pairs={{4,0},{8,4},{12,8},{14,12},{10,14},{6,10},{2,6},{0,2},{5,1},{9,5},... | collective-permute-start | bytes 614408 | tf_op jit(solution)/shard_map/ppermute | solution.py:391
  21.6 13.9 %collective-permute-start.10 = (f32[512,128]{1,0:T(8,128)S(1)}, f32[512,128]{1,0:T(8,128)S(1)}, u32[]{:S(2)}, u32[]{:S(2)}) collective-permute-start(f32[512,128]{1,0:T(8,128)S(1)} %pad_maximum_fusion.2), channel_id=1, source_target_pairs={{0,16},{16,0},{1,17},{17,1},{2,18},{18,2},{3,19},{19,3},{4,20},{20... | collective-permute-start | bytes 786440 | tf_op jit(solution)/shard_map/ppermute | solution.py:366
  23.2 4.3 %collective-permute-start.7 = (f32[128,128]{1,0:T(8,128)S(1)}, f32[128,128]{1,0:T(8,128)S(1)}, u32[]{:S(2)}, u32[]{:S(2)}) collective-permute-start(f32[128,128]{1,0:T(8,128)S(1)} %collective-permute-done.2.refs_2_), channel_id=1, source_target_pairs={{0,4},{4,8},{8,12},{12,14},{14,10},{10,6},{6,2},{2,0},{1,5},{5,9},... | collective-permute-start | bytes 196616 | tf_op jit(solution)/shard_map/ppermute | solution.py:398
  27.4 4.9 %collective-permute-start.8 = (f32[128,128]{1,0:T(8,128)S(1)}, f32[128,128]{1,0:T(8,128)S(1)}, u32[]{:S(2)}, u32[]{:S(2)}) collective-permute-start(f32[128,128]{1,0:T(8,128)S(1)} %collective-permute-done.3.refs_3_), channel_id=1, source_target_pairs={{4,0},{8,4},{12,8},{14,12},{10,14},{6,10},{2,6},{0,2},{5,1},{9,5},... | collective-permute-start | bytes 196616 | tf_op jit(solution)/shard_map/ppermute | solution.py:399
  32.4 2.2 %copy-start = (f32[400,128]{1,0:T(8,128)}, f32[400,128]{1,0:T(8,128)S(1)}, u32[]{:S(2)}) copy-start(f32[400,128]{1,0:T(8,128)S(1)} %collective-permute-done.11.refs_6_) | copy-start | bytes 614404
  32.4 4.8 %collective-permute-start.15 = (f32[208,128]{1,0:T(8,128)S(1)}, f32[208,128]{1,0:T(8,128)S(1)}, u32[]{:S(2)}, u32[]{:S(2)}) collective-permute-start(f32[208,128]{1,0:T(8,128)S(1)} %slice.42), channel_id=1, source_target_pairs={{4,0},{8,4},{12,8},{14,12},{10,14},{6,10},{2,6},{0,2},{5,1},{9,5},... | collective-permute-start | bytes 319496 | tf_op jit(solution)/shard_map/ppermute | solution.py:411
  34.1 4.7 %collective-permute-start.14 = (f32[192,128]{1,0:T(8,128)S(1)}, f32[192,128]{1,0:T(8,128)S(1)}, u32[]{:S(2)}, u32[]{:S(2)}) collective-permute-start(f32[192,128]{1,0:T(8,128)S(1)} %slice.41), channel_id=1, source_target_pairs={{0,4},{4,8},{8,12},{12,14},{14,10},{10,6},{6,2},{2,0},{1,5},{5,9},... | collective-permute-start | bytes 294920 | tf_op jit(solution)/shard_map/ppermute | solution.py:411
  34.6 0.9 %slice-start = ((f32[400,128]{1,0:T(8,128)}), f32[384,128]{1,0:T(8,128)S(1)}, s32[]{:S(2)}) async-start(f32[400,128]{1,0:T(8,128)} %copy-done), calls=%async_computation | async-start | bytes 393216 | tf_op jit(solution)/shard_map/slice | solution.py:402
  35.5 15.4 %collective-permute-start.13 = (f32[768,128]{1,0:T(8,128)S(1)}, f32[768,128]{1,0:T(8,128)S(1)}, u32[]{:S(2)}, u32[]{:S(2)}) collective-permute-start(f32[768,128]{1,0:T(8,128)S(1)} %pad_maximum_fusion), channel_id=1, source_target_pairs={{0,16},{16,0},{1,17},{17,1},{2,18},{18,2},{3,19},{19,3},{4,20},{20... | collective-permute-start | bytes 1179656 | tf_op jit(solution)/shard_map/ppermute | solution.py:366
  37.2 2.0 %copy-start.1 = (f32[400,128]{1,0:T(8,128)S(1)}, f32[400,128]{1,0:T(8,128)}, u32[]{:S(2)}) copy-start(f32[400,128]{1,0:T(8,128)} %copy-done) | copy-start | bytes 614404
  38.7 12.2 %collective-permute-start.16 = (f32[384,128]{1,0:T(8,128)S(1)}, f32[384,128]{1,0:T(8,128)S(1)}, u32[]{:S(2)}, u32[]{:S(2)}) collective-permute-start(f32[384,128]{1,0:T(8,128)S(1)} %pad_maximum_fusion.3), channel_id=1, source_target_pairs={{0,16},{16,0},{1,17},{17,1},{2,18},{18,2},{3,19},{19,3},{4,20},{20... | collective-permute-start | bytes 589832 | tf_op jit(solution)/shard_map/ppermute | solution.py:366

commit v4 on v2

--- a/solution.py
+++ b/solution.py
@@ -334,8 +334,8 @@
             pltpu.VMEM((2, LINES, cells_z), jnp.float32),
             pltpu.SemaphoreType.DMA((9,)),
         ],
-        compiler_params=pltpu.CompilerParams(vmem_limit_bytes=24 * 1024 * 1024),
-        cost_estimate=pl.CostEstimate(flops=1_000_000, bytes_accessed=100_000, transcendentals=0),
+        compiler_params=pltpu.CompilerParams(vmem_limit_bytes=40 * 1024 * 1024),
+        cost_estimate=pl.CostEstimate(flops=30_000_000, bytes_accessed=5_000_000, transcendentals=0),
     )(*operands)
 
 
@@ -345,7 +345,7 @@
     return lax.ppermute(value, axis, [(source, source + steps) for source in range(leading, last)])
 
 
-def around(medium, store, early, count):
+def around(medium, store, count):
     lanes = medium.shape[-1]
     group = lax.axis_index("groups")
     order = [2 * place for place in range((count + 1) // 2)]
@@ -374,35 +374,30 @@
         pieces[which].append(piece)
 
     forth, back, forth_later, back_later, rests = first, first, later, later, []
-    lates = []
     for distance in range(1, count // 2):
-        if distance == 3:
-            forth, early = lax.optimization_barrier((forth, early))
         forth, back = lax.ppermute(forth, "box", up), lax.ppermute(back, "box", down)
+        forth_later = lax.ppermute(forth_later, "box", up)
+        back_later = lax.ppermute(back_later, "box", down)
+        rest = across(jnp.concatenate([forth[third:size], back[third:size]]))
+        rests.append(rest)
         for piece, offset in ((forth, -distance), (back, distance)):
             row_parts.append((len(pieces[0]), size, offset))
             keep(0, piece, [(0, 0, units, offset)])
-        skip = 0
-        if distance < 3:
-            skip = third
-            forth_later = lax.ppermute(forth_later, "box", up)
-            back_later = lax.ppermute(back_later, "box", down)
-            lates.append((forth_later, back_later))
-            for piece, offset in ((forth_later, -distance), (back_later, distance)):
-                keep(1, piece, [(0, 0, units // 3, offset)])
-        left = units - skip * units // size
-        rest = across(jnp.concatenate([forth[skip:size], back[skip:size]]))
-        rests.append(rest)
-        keep(1, rest, [(0, units - left, left, -distance), (size - skip, units - left, left, distance)])
+        for piece, offset in ((forth_later, -distance), (back_later, distance)):
+            keep(1, piece, [(0, 0, units // 3, offset)])
+        left = units - units // 3
+        keep(1, rest, [(0, units - left, left, -distance), (size - third, units - left, left, distance)])
     far = count // 2
-    forth, back, _ = lax.optimization_barrier((forth, back, (rests[:2], lates[0])))
+    forth, back, _ = lax.optimization_barrier((forth, back, rests[0]))
     forth, back = lax.ppermute(forth[:half], "box", up), lax.ppermute(back[half:], "box", down)
     row_parts.append((len(pieces[0]) + 1, size - half, far))
     keep(0, forth, [(0, 0, units // 2, far)])
     keep(0, back, [(0, units // 2, units - units // 2, far)])
-    rest = across(jnp.concatenate([forth, back[: size - half]]))
-    keep(1, rest, [(0, 0, units, far)])
-    return ((pieces[0], parts[0], row_parts), (pieces[1], parts[1], [])), early
+    keep(1, lax.ppermute(forth_later, "box", up), [(0, 0, units // 3, far)])
+    rest = across(jnp.concatenate([forth[third:], back[: size - half]]))
+    pieces[0][-1], _ = lax.optimization_barrier((pieces[0][-1], rests[1]))
+    keep(1, rest, [(0, units // 3, units - units // 3, far)])
+    return ((pieces[0], parts[0], row_parts), (pieces[1], parts[1], []))
 
 
 def hot_planes(offsets, cells_y, cells_z):
@@ -429,7 +424,7 @@
         scalars = [
             jnp.concatenate([jnp.stack([place, slot]), brick_map, owners]) for slot in (group, 1 - group)
         ]
-        found, (hots, scalars) = around(medium, store, (hots, scalars), boxes)
+        found = around(medium, store, boxes)
     else:
         inverse = jnp.zeros((boxes,), jnp.int32).at[brick_map].set(jnp.arange(boxes, dtype=jnp.int32))
         moved = lax.all_to_all(medium, "box", split_axis=2, concat_axis=3, tiled=True)

time: 61.8 us -> 63.2 us (1.023)
  waiting for transfers between devices: 15 us -> 11.7 us
  other arithmetic: 1.2 us -> 3.24 us
  starting transfers between devices: 18.4 us -> 20.1 us
    ppermute x3, waiting for transfers between devices: 8.95 us -> 5.44 us  [around(): lax.ppermute(forth, 'box', up)]
    ppermute x2 -> x3, waiting for transfers between devices: 0.23 us -> 3.02 us  [around(): forth_later = lax.ppermute(forth_later, 'box', up)]
    ppermute x2 -> x3, waiting for transfers between devices: 2.22 us -> 0.01 us  [around(): back_later = lax.ppermute(back_later, 'box', down)]
    concatenate x4, other arithmetic: 0.08 us -> 2.13 us  [the longest x3 1.45 us: around(): rest = across(jnp.concatenate([forth[third:size], back[third:size]]))]
    ppermute x2 -> x3, starting transfers between devices: 3.15 us -> 4.84 us  [around(): back_later = lax.ppermute(back_later, 'box', down)]
    slice x8 -> x9, local copies, waits for them, and re-layouts: 0.07 us -> 0.95 us  [the longest x7 0.94 us: around(): rest = across(jnp.concatenate([forth[third:size], back[third:size]]))]
    ppermute x4, starting transfers between devices: 5.98 us -> 5.13 us  [across(): return lax.ppermute(value, 'groups', [(0, 1), (1, 0)])]
    ppermute x1, waiting for transfers between devices: 0.83 us -> 0.01 us  [around(): lax.ppermute(back[half:], 'box', down)]
  transfers between devices with their start and end apart: 17 -> 20, of which waited for: 8 -> 4; matrix products, arithmetic and copies ran while one was open for 4% -> 7% of each run, Pallas kernels for 19% -> 18%
where the time goes in v4:
time: 63.2 us; the launch traced here: 62.6 us
  Pallas kernels  22.8 us (36%)
  starting transfers between devices  20.1 us (32%)
  waiting for transfers between devices  11.7 us (19%)
  local copies, waits for them, and re-layouts  3.96 us (6%)
  other arithmetic  3.24 us (5%)
  between operations  0.84 us (1%)
    pallas_call x2, Pallas kernels, run_trial(): pl.pallas_call(functools.partial(propagate, (parts, row_parts, ring, plan...  22.8 us
    ppermute x3, waiting for transfers between devices, around(): lax.ppermute(forth, 'box', up)  5.44 us
    ppermute x4, starting transfers between devices, across(): return lax.ppermute(value, 'groups', [(0, 1), (1, 0)])  5.13 us
    ppermute x3, starting transfers between devices, around(): back_later = lax.ppermute(back_later, 'box', down)  4.84 us
    ppermute x3, starting transfers between devices, around(): lax.ppermute(back, 'box', down)  4.73 us
    ppermute x3, waiting for transfers between devices, around(): forth_later = lax.ppermute(forth_later, 'box', up)  3.02 us
    ppermute x1, waiting for transfers between devices, around(): lax.ppermute(forth[:half], 'box', up)  2.55 us
    ppermute x1, starting transfers between devices, around(): lax.ppermute(back[half:], 'box', down)  1.63 us
  transfers between devices with their start and end apart: 20, of which 4 were waited for; matrix products, arithmetic and copies ran while one was open for 7% of the time, Pallas kernels for 18%

profile of v4, /device:TPU:10, one launch (start us, length us, event | category | flops | bytes accessed | tf_op | source)
XLA Modules:
  0.0 62.6 jit_solution(8731497503801054833)
XLA Ops:
  0.6 0.7 %reduce = f32[3,256]{1,0:T(4,128)S(1)} reduce(f32[1,3,256]{2,0,1:T(1,128)} %param.6, f32[]{:T(128)} %constant.54), dimensions={0}, to_apply=%param.6.reduce_sub_computation | reduce | bytes 6148 | tf_op args[1]
  1.3 0.1 collective-permute-start.2
  1.4 1.1 %constant_dynamic-slice_fusion.1 = (f32[1,3,8,16,128]{4,3,2,1,0:T(8,128)S(1)}, f32[1,3,8,16,128]{4,3,2,1,0:T(8,128)S(1)}) fusion(f32[2,3,8,16,128]{4,3,2,1,0:T(8,128)} %param.5, s32[]{:T(128)S(6)} %select_n.42, s32[]{:T(128)S(6)} %select_n.41), kind=kLoop, calls=%fused_computation.20 | loop fusion | bytes 786440 | tf_op jit(solution)/shard_map/jit(dynamic_index_in_dim)/dynamic_slice | solution.py:364
  2.5 0.1 pad.15.clone
  2.6 0.0 collective-permute-done.2
  2.6 0.1 maximum_maximum_fusion.refs_1_
  2.7 0.5 collective-permute-start.3
  3.2 1.6 %collective-permute-start.4 = (f32[400,128]{1,0:T(8,128)S(1)}, f32[400,128]{1,0:T(8,128)S(1)}, u32[]{:S(2)}, u32[]{:S(2)}) collective-permute-start(f32[400,128]{1,0:T(8,128)S(1)} %maximum_maximum_fusion.refs_1_), channel_id=1, source_target_pairs={{4,0},{8,4},{12,8},{14,12},{10,14},{6,10},{2,6},{0,2},{5,1},{9,5},... | collective-permute-start | bytes 614408 | tf_op jit(solution)/shard_map/ppermute | solution.py:378
  4.8 5.4 %collective-permute-done.3.refs_2_ = f32[400,128]{1,0:T(8,128)S(1)} collective-permute-done((f32[400,128]{1,0:T(8,128)S(1)}, f32[400,128]{1,0:T(8,128)S(1)}, u32[]{:S(2)}, u32[]{:S(2)}) %collective-permute-start.3) | collective-permute-done | bytes 204832 | tf_op jit(solution)/shard_map/ppermute | solution.py:378
  10.2 0.4 collective-permute-start.8
  10.7 0.0 collective-permute-done.4.refs_3_
  10.7 1.6 %collective-permute-start.9 = (f32[400,128]{1,0:T(8,128)S(1)}, f32[400,128]{1,0:T(8,128)S(1)}, u32[]{:S(2)}, u32[]{:S(2)}) collective-permute-start(f32[400,128]{1,0:T(8,128)S(1)} %collective-permute-done.4.refs_3_), channel_id=1, source_target_pairs={{4,0},{8,4},{12,8},{14,12},{10,14},{6,10},{2,6},{0,2},{5,1},{9,5},... | collective-permute-start | bytes 614408 | tf_op jit(solution)/shard_map/ppermute | solution.py:378
  12.3 0.8 %constant_dynamic-slice_fusion = f32[1,1,8,16,128]{4,3,2,1,0:T(8,128)S(1)} fusion(f32[2,3,8,16,128]{4,3,2,1,0:T(8,128)} %param.5, s32[]{:T(128)S(6)} %select_n.41), kind=kLoop, calls=%fused_computation.19 | loop fusion | bytes 131076 | tf_op jit(solution)/shard_map/slice | solution.py:369
  13.1 0.0 copy-start.4
  13.1 0.4 collective-permute-start
  13.6 1.6 %collective-permute-start.1 = (f32[128,128]{1,0:T(8,128)S(1)}, f32[128,128]{1,0:T(8,128)}, u32[]{:S(2)}, u32[]{:S(2)}) collective-permute-start(f32[128,128]{1,0:T(8,128)S(1)} %bitcast.9), channel_id=1, source_target_pairs={{4,0},{8,4},{12,8},{14,12},{10,14},{6,10},{2,6},{0,2},{5,1},{9,5},... | collective-permute-start | bytes 196616 | tf_op jit(solution)/shard_map/ppermute | solution.py:380
  15.1 0.0 copy-done.4
  15.1 0.1 tile.9
  15.2 0.1 tile.11
  15.3 3.0 %collective-permute-done.refs_2_ = f32[128,128]{1,0:T(8,128)S(1)} collective-permute-done((f32[128,128]{1,0:T(8,128)S(1)}, f32[128,128]{1,0:T(8,128)S(1)}, u32[]{:S(2)}, u32[]{:S(2)}) %collective-permute-start) | collective-permute-done | bytes 65568 | tf_op jit(solution)/shard_map/ppermute | solution.py:379
  18.3 0.4 collective-permute-start.6
  18.8 0.2 copy-done.2
  19.0 1.6 %collective-permute-start.5 = (f32[512,128]{1,0:T(8,128)S(1)}, f32[512,128]{1,0:T(8,128)S(1)}, u32[]{:S(2)}, u32[]{:S(2)}) collective-permute-start(f32[512,128]{1,0:T(8,128)S(1)} %pad_maximum_fusion), channel_id=1, source_target_pairs={{0,16},{16,0},{1,17},{17,1},{2,18},{18,2},{3,19},{19,3},{4,20},{20... | collective-permute-start | bytes 786440 | tf_op jit(solution)/shard_map/ppermute | solution.py:357
  20.6 0.0 collective-permute-done.8.refs_4_
  20.6 0.5 collective-permute-start.13
  21.0 0.0 collective-permute-done.9.refs_5_
  21.0 1.6 %collective-permute-start.14 = (f32[400,128]{1,0:T(8,128)S(1)}, f32[400,128]{1,0:T(8,128)S(1)}, u32[]{:S(2)}, u32[]{:S(2)}) collective-permute-start(f32[400,128]{1,0:T(8,128)S(1)} %collective-permute-done.9.refs_5_), channel_id=1, source_target_pairs={{4,0},{8,4},{12,8},{14,12},{10,14},{6,10},{2,6},{0,2},{5,1},{9,5},... | collective-permute-start | bytes 614408 | tf_op jit(solution)/shard_map/ppermute | solution.py:378
  22.6 0.0 collective-permute-done.1.refs_3_
  22.6 1.6 %collective-permute-start.7 = (f32[128,128]{1,0:T(8,128)}, f32[128,128]{1,0:T(8,128)}, u32[]{:S(2)}, u32[]{:S(2)}) collective-permute-start(f32[128,128]{1,0:T(8,128)} %collective-permute-done.1.refs_3_), channel_id=1, source_target_pairs={{4,0},{8,4},{12,8},{14,12},{10,14},{6,10},{2,6},{0,2},{5,1},{9,5},... | collective-permute-start | bytes 196616 | tf_op jit(solution)/shard_map/ppermute | solution.py:380
  24.3 0.0 collective-permute-done.6.refs_5_
  24.3 0.4 collective-permute-start.11
  24.7 0.7 %pad_maximum_fusion.1 = f32[512,128]{1,0:T(8,128)} fusion(f32[256,128]{1,0:T(8,128)S(1)} %slice.51, f32[256,128]{1,0:T(8,128)S(1)} %slice.50), kind=kLoop, calls=%fused_computation.5 | loop fusion | flops 65536 | bytes 524288 | tf_op jit(solution)/shard_map/concatenate | solution.py:381
  25.5 0.6 collective-permute-done.5.refs_4_
  26.1 1.5 %collective-permute-start.10 = (f32[512,128]{1,0:T(8,128)}, f32[512,128]{1,0:T(8,128)S(1)}, u32[]{:S(2)}, u32[]{:S(2)}) collective-permute-start(f32[512,128]{1,0:T(8,128)} %pad_maximum_fusion.1), channel_id=1, source_target_pairs={{0,16},{16,0},{1,17},{17,1},{2,18},{18,2},{3,19},{19,3},{4,20},{20... | collective-permute-start | bytes 786440 | tf_op jit(solution)/shard_map/ppermute | solution.py:357
  27.6 0.0 collective-permute-done.13.refs_6_
  27.6 0.0 collective-permute-done.14.refs_7_
  27.6 1.6 %collective-permute-start.18 = (f32[208,128]{1,0:T(8,128)S(1)}, f32[208,128]{1,0:T(8,128)S(1)}, u32[]{:S(2)}, u32[]{:S(2)}) collective-permute-start(f32[208,128]{1,0:T(8,128)S(1)} %slice.46), channel_id=1, source_target_pairs={{4,0},{8,4},{12,8},{14,12},{10,14},{6,10},{2,6},{0,2},{5,1},{9,5},... | collective-permute-start | bytes 319496 | tf_op jit(solution)/shard_map/ppermute | solution.py:392
  29.3 0.5 collective-permute-start.17
  29.8 0.0 copy-done
  29.8 0.9 %slice-done = f32[256,128]{1,0:T(8,128)S(1)} async-done(((f32[400,128]{1,0:T(8,128)}), f32[256,128]{1,0:T(8,128)S(1)}, s32[]{:S(2)}) %slice-start) | async-done | bytes 131096 | tf_op jit(solution)/shard_map/slice | solution.py:381
  30.7 0.7 %pad_maximum_fusion.2 = f32[512,128]{1,0:T(8,128)} fusion(f32[256,128]{1,0:T(8,128)S(1)} %slice.53, f32[256,128]{1,0:T(8,128)S(1)} %slice-done), kind=kLoop, calls=%fused_computation.6 | loop fusion | flops 65536 | bytes 524288 | tf_op jit(solution)/shard_map/concatenate | solution.py:381
  31.4 2.5 %collective-permute-done.17.refs_8_ = f32[192,128]{1,0:T(8,128)S(1)} collective-permute-done((f32[192,128]{1,0:T(8,128)S(1)}, f32[192,128]{1,0:T(8,128)S(1)}, u32[]{:S(2)}, u32[]{:S(2)}) %collective-permute-start.17) | collective-permute-done | bytes 98336 | tf_op jit(solution)/shard_map/ppermute | solution.py:392
  33.9 0.5 collective-permute-start.15
  34.4 0.0 collective-permute-done.18.refs_9_
  34.5 0.7 %pad_maximum_fusion.3 = f32[256,128]{1,0:T(8,128)} fusion(f32[192,128]{1,0:T(8,128)S(1)} %slice.55, f32[64,128]{1,0:T(8,128)S(1)} %slice.54), kind=kLoop, calls=%fused_computation.8 | loop fusion | flops 32768 | bytes 262144 | tf_op jit(solution)/shard_map/concatenate | solution.py:397
  35.1 1.5 %collective-permute-start.19 = (f32[256,128]{1,0:T(8,128)}, f32[256,128]{1,0:T(8,128)S(1)}, u32[]{:S(2)}, u32[]{:S(2)}) collective-permute-start(f32[256,128]{1,0:T(8,128)} %pad_maximum_fusion.3), channel_id=1, source_target_pairs={{0,16},{16,0},{1,17},{17,1},{2,18},{18,2},{3,19},{19,3},{4,20},{20... | collective-permute-start | bytes 393224 | tf_op jit(solution)/shard_map/ppermute | solution.py:357
  36.7 0.2 fusion
  36.9 0.0 collective-permute-done.7.refs_6_
  36.9 1.6 %collective-permute-start.12 = (f32[128,128]{1,0:T(8,128)}, f32[128,128]{1,0:T(8,128)S(1)}, u32[]{:S(2)}, u32[]{:S(2)}) collective-permute-start(f32[128,128]{1,0:T(8,128)} %collective-permute-done.7.refs_6_), channel_id=1, source_target_pairs={{4,0},{8,4},{12,8},{14,12},{10,14},{6,10},{2,6},{0,2},{5,1},{9,5},... | collective-permute-start | bytes 196616 | tf_op jit(solution)/shard_map/ppermute | solution.py:380
  38.5 0.0 collective-permute-done.11.refs_8_
  38.5 0.4 collective-permute-start.16
  39.0 0.7 %copy-done.5 = s32[6]{0:T(128)S(1)} copy-done((s32[6]{0:T(128)S(1)}, s32[6]{0:T(128)}, u32[]{:S(2)}) %copy-start.5) | copy-done | bytes 48
  39.6 0.0 copy-done.6
  39.6 0.1 add_add_fusion.1
  39.7 0.0 collective-permute-done.10.refs_7_
  39.7 0.0 copy-done.1
  39.7 0.0 copy-start.3
  39.7 11.4 %shard_map.68 = (f32[2,3,1,128,128]{4,3,2,1,0:T(8,128)}, f32[2,6,1,128,128]{4,3,2,1,0:T(8,128)}, f32[8,24,128]{2,1,0:T(8,128)S(1)}) custom-call(s32[16]{0:T(128)S(1)} %get-tuple-element.20.refs_0_, f32[400,128]{1,0:T(8,128)S(1)} %maximum_maximum_fusion.refs_1_, f32[400,128]{1,0:T(8,128)S(1)} %collective-permute-done.3.refs_2_, ...), custom_call_target="tpu_custom_call" | custom-call | flops 30000000 | bytes 5000000 | tf_op jit(solution)/shard_map/pallas_call | solution.py:323
  51.1 0.0 collective-permute-done.12.refs_9_
  51.1 0.0 collective-permute-done.16.refs_11_
  51.1 0.0 collective-permute-done.19.refs_12_
  51.2 0.0 collective-permute-done.15.refs_10_
  51.2 0.0 copy-done.3
  51.2 11.4 %shard_map.69 = (f32[2,3,1,128,128]{4,3,2,1,0:T(8,128)}, f32[2,6,1,128,128]{4,3,2,1,0:T(8,128)}) custom-call(s32[16]{0:T(128)S(1)} %get-tuple-element.21.refs_0_, f32[384,128]{1,0:T(8,128)S(1)} %bitcast.6, f32[128,128]{1,0:T(8,128)S(1)} %copy-done.3, f32[128,128]{1,0:T(8,128)} %collective-permute-done.1.refs_3_, ...), custom_call_target="tpu_custom_call", output_to_operand_aliasing={{0}: (16, {}), {1}: (17, {})} | custom-call | flops 30000000 | bytes 5000000 | tf_op jit(solution)/shard_map/pallas_call | solution.py:323
  (21 shorter events, 0.1 us)
Async XLA Ops:
  1.3 1.2 %collective-permute-start.2 = (f32[6,128]{1,0:T(8,128)S(1)}, f32[6,128]{1,0:T(8,128)S(1)}, u32[]{:S(2)}, u32[]{:S(2)}) collective-permute-start(f32[6,128]{1,0:T(8,128)S(1)} %reshape_squeeze.3), channel_id=1, source_target_pairs={{0,1},{1,0},{2,3},{3,2},{4,5},{5,4},{6,7},{7,6},{8,9},{9,8},{10,11... | collective-permute-start | bytes 9224 | tf_op jit(solution)/shard_map/ppermute | solution.py:360
  2.7 7.5 %collective-permute-start.3 = (f32[400,128]{1,0:T(8,128)S(1)}, f32[400,128]{1,0:T(8,128)S(1)}, u32[]{:S(2)}, u32[]{:S(2)}) collective-permute-start(f32[400,128]{1,0:T(8,128)S(1)} %maximum_maximum_fusion.refs_1_), channel_id=1, source_target_pairs={{0,4},{4,8},{8,12},{12,14},{14,10},{10,6},{6,2},{2,0},{1,5},{5,9},... | collective-permute-start | bytes 614408 | tf_op jit(solution)/shard_map/ppermute | solution.py:378
  3.2 7.5 %collective-permute-start.4 = (f32[400,128]{1,0:T(8,128)S(1)}, f32[400,128]{1,0:T(8,128)S(1)}, u32[]{:S(2)}, u32[]{:S(2)}) collective-permute-start(f32[400,128]{1,0:T(8,128)S(1)} %maximum_maximum_fusion.refs_1_), channel_id=1, source_target_pairs={{4,0},{8,4},{12,8},{14,12},{10,14},{6,10},{2,6},{0,2},{5,1},{9,5},... | collective-permute-start | bytes 614408 | tf_op jit(solution)/shard_map/ppermute | solution.py:378
  10.2 10.3 %collective-permute-start.8 = (f32[400,128]{1,0:T(8,128)S(1)}, f32[400,128]{1,0:T(8,128)S(1)}, u32[]{:S(2)}, u32[]{:S(2)}) collective-permute-start(f32[400,128]{1,0:T(8,128)S(1)} %collective-permute-done.3.refs_2_), channel_id=1, source_target_pairs={{0,4},{4,8},{8,12},{12,14},{14,10},{10,6},{6,2},{2,0},{1,5},{5,9},... | collective-permute-start | bytes 614408 | tf_op jit(solution)/shard_map/ppermute | solution.py:378
  10.7 10.3 %collective-permute-start.9 = (f32[400,128]{1,0:T(8,128)S(1)}, f32[400,128]{1,0:T(8,128)S(1)}, u32[]{:S(2)}, u32[]{:S(2)}) collective-permute-start(f32[400,128]{1,0:T(8,128)S(1)} %collective-permute-done.4.refs_3_), channel_id=1, source_target_pairs={{4,0},{8,4},{12,8},{14,12},{10,14},{6,10},{2,6},{0,2},{5,1},{9,5},... | collective-permute-start | bytes 614408 | tf_op jit(solution)/shard_map/ppermute | solution.py:378
  13.1 2.0 %copy-start.4 = (s32[256]{0:T(256)S(1)}, s32[256]{0:T(256)}, u32[]{:S(2)}) copy-start(s32[256]{0:T(256)} %param.7) | copy-start | bytes 3076
  13.1 5.2 %collective-permute-start = (f32[128,128]{1,0:T(8,128)S(1)}, f32[128,128]{1,0:T(8,128)S(1)}, u32[]{:S(2)}, u32[]{:S(2)}) collective-permute-start(f32[128,128]{1,0:T(8,128)S(1)} %bitcast.8), channel_id=1, source_target_pairs={{0,4},{4,8},{8,12},{12,14},{14,10},{10,6},{6,2},{2,0},{1,5},{5,9},... | collective-permute-start | bytes 196616 | tf_op jit(solution)/shard_map/ppermute | solution.py:379
  13.6 9.1 %collective-permute-start.1 = (f32[128,128]{1,0:T(8,128)S(1)}, f32[128,128]{1,0:T(8,128)}, u32[]{:S(2)}, u32[]{:S(2)}) collective-permute-start(f32[128,128]{1,0:T(8,128)S(1)} %bitcast.9), channel_id=1, source_target_pairs={{4,0},{8,4},{12,8},{14,12},{10,14},{6,10},{2,6},{0,2},{5,1},{9,5},... | collective-permute-start | bytes 196616 | tf_op jit(solution)/shard_map/ppermute | solution.py:380
  18.3 0.6 copy-start.2
  18.3 5.9 %collective-permute-start.6 = (f32[128,128]{1,0:T(8,128)S(1)}, f32[128,128]{1,0:T(8,128)}, u32[]{:S(2)}, u32[]{:S(2)}) collective-permute-start(f32[128,128]{1,0:T(8,128)S(1)} %collective-permute-done.refs_2_), channel_id=1, source_target_pairs={{0,4},{4,8},{8,12},{12,14},{14,10},{10,6},{6,2},{2,0},{1,5},{5,9},... | collective-permute-start | bytes 196616 | tf_op jit(solution)/shard_map/ppermute | solution.py:379
  19.0 7.1 %collective-permute-start.5 = (f32[512,128]{1,0:T(8,128)S(1)}, f32[512,128]{1,0:T(8,128)S(1)}, u32[]{:S(2)}, u32[]{:S(2)}) collective-permute-start(f32[512,128]{1,0:T(8,128)S(1)} %pad_maximum_fusion), channel_id=1, source_target_pairs={{0,16},{16,0},{1,17},{17,1},{2,18},{18,2},{3,19},{19,3},{4,20},{20... | collective-permute-start | bytes 786440 | tf_op jit(solution)/shard_map/ppermute | solution.py:357
  20.6 7.0 %collective-permute-start.13 = (f32[400,128]{1,0:T(8,128)S(1)}, f32[400,128]{1,0:T(8,128)S(1)}, u32[]{:S(2)}, u32[]{:S(2)}) collective-permute-start(f32[400,128]{1,0:T(8,128)S(1)} %collective-permute-done.8.refs_4_), channel_id=1, source_target_pairs={{0,4},{4,8},{8,12},{12,14},{14,10},{10,6},{6,2},{2,0},{1,5},{5,9},... | collective-permute-start | bytes 614408 | tf_op jit(solution)/shard_map/ppermute | solution.py:378
  21.0 6.6 %collective-permute-start.14 = (f32[400,128]{1,0:T(8,128)S(1)}, f32[400,128]{1,0:T(8,128)S(1)}, u32[]{:S(2)}, u32[]{:S(2)}) collective-permute-start(f32[400,128]{1,0:T(8,128)S(1)} %collective-permute-done.9.refs_5_), channel_id=1, source_target_pairs={{4,0},{8,4},{12,8},{14,12},{10,14},{6,10},{2,6},{0,2},{5,1},{9,5},... | collective-permute-start | bytes 614408 | tf_op jit(solution)/shard_map/ppermute | solution.py:378
  22.6 14.2 %collective-permute-start.7 = (f32[128,128]{1,0:T(8,128)}, f32[128,128]{1,0:T(8,128)}, u32[]{:S(2)}, u32[]{:S(2)}) collective-permute-start(f32[128,128]{1,0:T(8,128)} %collective-permute-done.1.refs_3_), channel_id=1, source_target_pairs={{4,0},{8,4},{12,8},{14,12},{10,14},{6,10},{2,6},{0,2},{5,1},{9,5},... | collective-permute-start | bytes 196616 | tf_op jit(solution)/shard_map/ppermute | solution.py:380
  24.3 14.2 %collective-permute-start.11 = (f32[128,128]{1,0:T(8,128)}, f32[128,128]{1,0:T(8,128)}, u32[]{:S(2)}, u32[]{:S(2)}) collective-permute-start(f32[128,128]{1,0:T(8,128)} %collective-permute-done.6.refs_5_), channel_id=1, source_target_pairs={{0,4},{4,8},{8,12},{12,14},{14,10},{10,6},{6,2},{2,0},{1,5},{5,9},... | collective-permute-start | bytes 196616 | tf_op jit(solution)/shard_map/ppermute | solution.py:379
  26.1 13.6 %collective-permute-start.10 = (f32[512,128]{1,0:T(8,128)}, f32[512,128]{1,0:T(8,128)S(1)}, u32[]{:S(2)}, u32[]{:S(2)}) collective-permute-start(f32[512,128]{1,0:T(8,128)} %pad_maximum_fusion.1), channel_id=1, source_target_pairs={{0,16},{16,0},{1,17},{17,1},{2,18},{18,2},{3,19},{19,3},{4,20},{20... | collective-permute-start | bytes 786440 | tf_op jit(solution)/shard_map/ppermute | solution.py:357
  27.6 2.2 %copy-start = (f32[400,128]{1,0:T(8,128)}, f32[400,128]{1,0:T(8,128)S(1)}, u32[]{:S(2)}) copy-start(f32[400,128]{1,0:T(8,128)S(1)} %collective-permute-done.13.refs_6_) | copy-start | bytes 614404
  27.6 6.8 %collective-permute-start.18 = (f32[208,128]{1,0:T(8,128)S(1)}, f32[208,128]{1,0:T(8,128)S(1)}, u32[]{:S(2)}, u32[]{:S(2)}) collective-permute-start(f32[208,128]{1,0:T(8,128)S(1)} %slice.46), channel_id=1, source_target_pairs={{4,0},{8,4},{12,8},{14,12},{10,14},{6,10},{2,6},{0,2},{5,1},{9,5},... | collective-permute-start | bytes 319496 | tf_op jit(solution)/shard_map/ppermute | solution.py:392
  29.3 4.7 %collective-permute-start.17 = (f32[192,128]{1,0:T(8,128)S(1)}, f32[192,128]{1,0:T(8,128)S(1)}, u32[]{:S(2)}, u32[]{:S(2)}) collective-permute-start(f32[192,128]{1,0:T(8,128)S(1)} %slice.44), channel_id=1, source_target_pairs={{0,4},{4,8},{8,12},{12,14},{14,10},{10,6},{6,2},{2,0},{1,5},{5,9},... | collective-permute-start | bytes 294920 | tf_op jit(solution)/shard_map/ppermute | solution.py:392
  29.8 0.9 %slice-start = ((f32[400,128]{1,0:T(8,128)}), f32[256,128]{1,0:T(8,128)S(1)}, s32[]{:S(2)}) async-start(f32[400,128]{1,0:T(8,128)} %copy-done), calls=%async_computation | async-start | bytes 262144 | tf_op jit(solution)/shard_map/slice | solution.py:381
  33.9 17.2 %collective-permute-start.15 = (f32[512,128]{1,0:T(8,128)}, f32[512,128]{1,0:T(8,128)S(1)}, u32[]{:S(2)}, u32[]{:S(2)}) collective-permute-start(f32[512,128]{1,0:T(8,128)} %pad_maximum_fusion.2), channel_id=1, source_target_pairs={{0,16},{16,0},{1,17},{17,1},{2,18},{18,2},{3,19},{19,3},{4,20},{20... | collective-permute-start | bytes 786440 | tf_op jit(solution)/shard_map/ppermute | solution.py:357
  35.1 16.0 %collective-permute-start.19 = (f32[256,128]{1,0:T(8,128)}, f32[256,128]{1,0:T(8,128)S(1)}, u32[]{:S(2)}, u32[]{:S(2)}) collective-permute-start(f32[256,128]{1,0:T(8,128)} %pad_maximum_fusion.3), channel_id=1, source_target_pairs={{0,16},{16,0},{1,17},{17,1},{2,18},{18,2},{3,19},{19,3},{4,20},{20... | collective-permute-start | bytes 393224 | tf_op jit(solution)/shard_map/ppermute | solution.py:357
  36.7 3.1 %copy-start.1 = (f32[400,128]{1,0:T(8,128)S(1)}, f32[400,128]{1,0:T(8,128)}, u32[]{:S(2)}) copy-start(f32[400,128]{1,0:T(8,128)} %copy-done) | copy-start | bytes 614404
  36.9 14.2 %collective-permute-start.12 = (f32[128,128]{1,0:T(8,128)}, f32[128,128]{1,0:T(8,128)S(1)}, u32[]{:S(2)}, u32[]{:S(2)}) collective-permute-start(f32[128,128]{1,0:T(8,128)} %collective-permute-done.7.refs_6_), channel_id=1, source_target_pairs={{4,0},{8,4},{12,8},{14,12},{10,14},{6,10},{2,6},{0,2},{5,1},{9,5},... | collective-permute-start | bytes 196616 | tf_op jit(solution)/shard_map/ppermute | solution.py:380
  38.5 12.6 %collective-permute-start.16 = (f32[128,128]{1,0:T(8,128)}, f32[128,128]{1,0:T(8,128)S(1)}, u32[]{:S(2)}, u32[]{:S(2)}) collective-permute-start(f32[128,128]{1,0:T(8,128)} %collective-permute-done.11.refs_8_), channel_id=1, source_target_pairs={{0,4},{4,8},{8,12},{12,14},{14,10},{10,6},{6,2},{2,0},{1,5},{5,9},... | collective-permute-start | bytes 196616 | tf_op jit(solution)/shard_map/ppermute | solution.py:396
  39.0 0.7 %copy-start.5 = (s32[6]{0:T(128)S(1)}, s32[6]{0:T(128)}, u32[]{:S(2)}) copy-start(s32[6]{0:T(128)} %param.8) | copy-start | bytes 76
  39.0 0.7 %copy-start.6 = (s32[8]{0:T(128)S(1)}, s32[8]{0:T(128)}, u32[]{:S(2)}) copy-start(s32[8]{0:T(128)} %param.9) | copy-start | bytes 100
  39.7 11.5 %copy-start.3 = (f32[128,128]{1,0:T(8,128)S(1)}, f32[128,128]{1,0:T(8,128)}, u32[]{:S(2)}) copy-start(f32[128,128]{1,0:T(8,128)} %copy-done.2) | copy-start | bytes 196612
